TPU v7x, 128 devices: a whole 4x4x4 slice. The times are simulated.
128 devices in a mesh: ctx: 32 (over z, x_hi, y), head: 4 (over x_lo, core).
Axes of the slice: x: 4 (x_hi: 2, x_lo: 2; x = x_hi * 2 + x_lo), y: 4, z: 4, core: 2. Of those that a mesh axis runs over, the one named last changes fastest.
Arguments:
- queries: bfloat16 [512, 16384], P('ctx', 'head'), may hold values from -18 to 18
- new_keys: bfloat16 [512, 1024], P('ctx', 'head'), may hold values from -7 to 7
- new_values: bfloat16 [512, 1024], P('ctx', 'head'), may hold values from -6 to 6
- cache_keys: bfloat16 [32768, 1024], P('ctx', 'head'), may hold values from -6 to 6
- cache_values: bfloat16 [32768, 1024], P('ctx', 'head'), may hold values from -6 to 6
- span_ids: int32 [256], P('ctx'), may hold values from 0 to 255, each once
- valid_len: int32 [256], P('ctx'), may hold values from 1 to 128, 20480 in all
- pos_ids: int32 [512], replicated, may hold values from 0 to 511, each once
- offset: int32 [1], replicated, may hold values from 16384 to 32768
- out_weight: bfloat16 [16384, 16384], P('head', 'ctx'), may hold values from -0.046875 to 0.046875
Outputs:
- layer_out: bfloat16 [512, 16384], P('head', 'ctx')
Inputs may be any that keep to these rules, and one draw needn't show every extreme that they name: `span_ids`: each span number appears once. `pos_ids`: each position of the turn appears once.
All inputs are finite; a program needn't handle non-finite values. No bound on the sum of `valid_len` on one device may be relied on, other than what follows from the above.
Results may differ from a plain program's by a relative error of at most 0.014.
Values may be sent and summed in bfloat16 or wider, within the bound.
No kernel may reach another device: no remote copies, remote signals or barrier semaphores. Data moves between devices by JAX's collectives and lax.ppermute only.
A program may use at most 128 MiB of HBM per device.

v0:
```python
import math

import jax
import jax.numpy as jnp
from jax import lax
from jax.sharding import PartitionSpec as P

HD = 128


masked_fill = -1e30


def passed_along(block, axis, distance):
    devices = range(lax.axis_size(axis))
    route = [((i - distance) % len(devices), i) for i in devices]
    return lax.ppermute(block, axis, route)


def attend(blocks, block_pos, res_keys, res_values, cache_live, local_pos):
    row_count = blocks.shape[0]
    kv_dev = res_keys.shape[1]
    head_count = blocks.shape[1] // HD
    group_size = head_count // kv_dev
    grouped = blocks.reshape(row_count, kv_dev, group_size, HD)
    scores = jnp.einsum("qagd,nad->aqgn", grouped, res_keys, preferred_element_type=jnp.float32) * (
        1.0 / math.sqrt(HD)
    )
    turn_live = local_pos[None, :] <= block_pos[:, None]
    visible = jnp.concatenate(
        [jnp.broadcast_to(cache_live[None, :], (row_count, cache_live.shape[0])), turn_live], axis=1
    )
    visible = visible[None, :, None, :]
    scores = jnp.where(visible, scores, masked_fill)
    maxima = jnp.max(scores, axis=3)
    weights = jnp.where(visible, jnp.exp(scores - maxima[..., None]), 0.0)
    totals = jnp.sum(weights, axis=3)
    numerator = jnp.einsum(
        "aqgn,nad->qagd",
        weights.astype(jnp.bfloat16),
        res_values,
        preferred_element_type=jnp.float32,
    )
    maxima = jnp.transpose(maxima, (1, 0, 2)).reshape(row_count, head_count)
    totals = jnp.transpose(totals, (1, 0, 2)).reshape(row_count, head_count)
    return (maxima, totals, numerator.reshape(row_count, head_count, HD))


def settle(parts):
    maxima, totals, numerator = parts
    highest = jnp.max(maxima, axis=0)
    scaling = jnp.exp(maxima - highest[None])
    total_sum = jnp.sum(scaling * totals, axis=0)
    merged = jnp.sum(scaling[..., None] * numerator, axis=0) / total_sum[..., None]
    return merged.reshape(merged.shape[0], -1).astype(jnp.bfloat16)


def record(outbox, partial_value, owner, first_row):
    placed = []
    for buffer, new_piece in zip(outbox, partial_value):
        corner = (owner, first_row) + (0,) * (buffer.ndim - 2)
        placed.append(lax.dynamic_update_slice(buffer, new_piece[None], corner))
    return tuple(placed)


def pass_queries(blocks, step_by):
    return passed_along(blocks, "ctx", step_by)


def shards(
    queries,
    new_keys,
    new_values,
    cache_keys,
    cache_values,
    span_ids,
    valid_len,
    pos_ids,
    offset,
    out_weight,
):
    axis_count = lax.axis_size("ctx")
    my_index = lax.axis_index("ctx")
    token_count = queries.shape[0]
    head_count = queries.shape[1] // HD
    kv_dev = new_keys.shape[1] // HD
    slot_count = span_ids.shape[0]
    span_size = cache_keys.shape[0] // slot_count
    local_pos = lax.dynamic_slice_in_dim(pos_ids, my_index * token_count, token_count)
    within = lax.broadcasted_iota(jnp.int32, (slot_count, span_size), 1)
    cache_position = span_ids[:, None] * span_size + within
    cache_live = ((within < valid_len[:, None]) & (cache_position < offset[0])).reshape(-1)
    res_keys = jnp.concatenate([cache_keys, new_keys], axis=0).reshape(-1, kv_dev, HD)
    res_values = jnp.concatenate([cache_values, new_values], axis=0).reshape(-1, kv_dev, HD)

    def visit(blocks, owner, first_row):
        block_pos = lax.dynamic_slice_in_dim(
            pos_ids, owner * token_count + first_row, blocks.shape[0]
        )
        return attend(blocks, block_pos, res_keys, res_values, cache_live, local_pos)

    route_plan = ((0, token_count, 1),)
    starting = tuple((queries for first_row, row_count, step_by in route_plan))
    outbox = (
        jnp.zeros((axis_count, token_count, head_count), jnp.float32),
        jnp.zeros((axis_count, token_count, head_count), jnp.float32),
        jnp.zeros((axis_count, token_count, head_count, HD), jnp.float32),
    )
    for blocks, plan_entry in zip(starting, route_plan):
        outbox = record(outbox, visit(blocks, my_index, plan_entry[0]), my_index, plan_entry[0])

    def advance_listed(turn_index, carry):
        moving, outbox = carry
        next_moving = []
        for blocks, plan_entry in zip(moving, route_plan):
            first_row, row_count, step_by = plan_entry
            blocks = pass_queries(blocks, step_by)
            owner = (my_index - step_by * turn_index) % axis_count
            outbox = record(outbox, visit(blocks, owner, first_row), owner, first_row)
            next_moving.append(blocks)
        return (tuple(next_moving), outbox)

    moving, outbox = lax.fori_loop(1, axis_count, advance_listed, (starting, outbox))
    attended = settle(
        (
            lax.all_to_all(outbox[0], "ctx", split_axis=0, concat_axis=0, tiled=True),
            lax.all_to_all(outbox[1], "ctx", split_axis=0, concat_axis=0, tiled=True),
            lax.all_to_all(outbox[2], "ctx", split_axis=0, concat_axis=0, tiled=True),
        )
    )
    terms = jnp.dot(
        lax.all_gather(attended, "ctx", axis=0, tiled=True),
        out_weight,
        preferred_element_type=jnp.float32,
    )
    return lax.psum_scatter(terms, "head", scatter_dimension=0, tiled=True).astype(jnp.bfloat16)


def solution(mesh):
    in_specs = (
        P("ctx", "head"),
        P("ctx", "head"),
        P("ctx", "head"),
        P("ctx", "head"),
        P("ctx", "head"),
        P("ctx"),
        P("ctx"),
        P(),
        P(),
        P("head", "ctx"),
    )
    out_specs = P("head", "ctx")
    return jax.shard_map(shards, mesh=mesh, in_specs=in_specs, out_specs=out_specs, check_vma=False)
```

profile of v0, /device:TPU:1, one launch (start us, length us, event | category | flops | bytes accessed | tf_op | source)
XLA Modules:
  0.0 764.8 jit_solution(9413780745766560159)
XLA Ops:
  16.4 2.0 fusion.37
  26.8 2.2 copy-done
  29.0 449.6 %while.22 = (s32[]{:T(128)}, bf16[16,4096]{1,0:T(8,128)(2,1)S(1)}, f32[32,16,32]{2,1,0:T(8,128)}, f32[32,16,32]{2,1,0:T(8,128)}, f32[32,16,32,128]{3,2,1,0:T(8,1...) while((s32[]{:T(128)}, bf16[16,4096]{1,0:T(8,128)(2,1)S(1)}, ...), condition=%wide.region_5.6_spmd.clone, body=%wide.region_2.5_spmd.clone.sunk | while | flops 277442048 | bytes 10062103 | solution.py:123
  29.0 2.2 collective-permute-start
  32.8 9.0 %collective-permute-done = bf16[16,4096]{1,0:T(8,128)(2,1)S(1)} collective-permute-done((bf16[16,4096]{1,0:T(8,128)(2,1)S(1)}, bf16[16,4096]{1,0:T(8,128)(2,1)S(1)}, u32[]{:S(2)}, u32[]{:S(2)}) %collective-permute-start) | collective-permute-done | bytes 131104 | tf_op jit(solution)/shard_map/while/body/eval_jaxpr/ppermute | solution.py:17
  48.1 7.9 %collective-permute-done = bf16[16,4096]{1,0:T(8,128)(2,1)S(1)} collective-permute-done((bf16[16,4096]{1,0:T(8,128)(2,1)S(1)}, bf16[16,4096]{1,0:T(8,128)(2,1)S(1)}, u32[]{:S(2)}, u32[]{:S(2)}) %collective-permute-start) | collective-permute-done | bytes 131104 | tf_op jit(solution)/shard_map/while/body/eval_jaxpr/ppermute | solution.py:17
  62.4 7.9 %collective-permute-done = bf16[16,4096]{1,0:T(8,128)(2,1)S(1)} collective-permute-done((bf16[16,4096]{1,0:T(8,128)(2,1)S(1)}, bf16[16,4096]{1,0:T(8,128)(2,1)S(1)}, u32[]{:S(2)}, u32[]{:S(2)}) %collective-permute-start) | collective-permute-done | bytes 131104 | tf_op jit(solution)/shard_map/while/body/eval_jaxpr/ppermute | solution.py:17
  76.6 7.9 %collective-permute-done = bf16[16,4096]{1,0:T(8,128)(2,1)S(1)} collective-permute-done((bf16[16,4096]{1,0:T(8,128)(2,1)S(1)}, bf16[16,4096]{1,0:T(8,128)(2,1)S(1)}, u32[]{:S(2)}, u32[]{:S(2)}) %collective-permute-start) | collective-permute-done | bytes 131104 | tf_op jit(solution)/shard_map/while/body/eval_jaxpr/ppermute | solution.py:17
  90.8 7.9 %collective-permute-done = bf16[16,4096]{1,0:T(8,128)(2,1)S(1)} collective-permute-done((bf16[16,4096]{1,0:T(8,128)(2,1)S(1)}, bf16[16,4096]{1,0:T(8,128)(2,1)S(1)}, u32[]{:S(2)}, u32[]{:S(2)}) %collective-permute-start) | collective-permute-done | bytes 131104 | tf_op jit(solution)/shard_map/while/body/eval_jaxpr/ppermute | solution.py:17
  100.2 1.7 fusion.55
  105.1 7.9 %collective-permute-done = bf16[16,4096]{1,0:T(8,128)(2,1)S(1)} collective-permute-done((bf16[16,4096]{1,0:T(8,128)(2,1)S(1)}, bf16[16,4096]{1,0:T(8,128)(2,1)S(1)}, u32[]{:S(2)}, u32[]{:S(2)}) %collective-permute-start) | collective-permute-done | bytes 131104 | tf_op jit(solution)/shard_map/while/body/eval_jaxpr/ppermute | solution.py:17
  119.3 7.9 %collective-permute-done = bf16[16,4096]{1,0:T(8,128)(2,1)S(1)} collective-permute-done((bf16[16,4096]{1,0:T(8,128)(2,1)S(1)}, bf16[16,4096]{1,0:T(8,128)(2,1)S(1)}, u32[]{:S(2)}, u32[]{:S(2)}) %collective-permute-start) | collective-permute-done | bytes 131104 | tf_op jit(solution)/shard_map/while/body/eval_jaxpr/ppermute | solution.py:17
  133.5 7.9 %collective-permute-done = bf16[16,4096]{1,0:T(8,128)(2,1)S(1)} collective-permute-done((bf16[16,4096]{1,0:T(8,128)(2,1)S(1)}, bf16[16,4096]{1,0:T(8,128)(2,1)S(1)}, u32[]{:S(2)}, u32[]{:S(2)}) %collective-permute-start) | collective-permute-done | bytes 131104 | tf_op jit(solution)/shard_map/while/body/eval_jaxpr/ppermute | solution.py:17
  147.8 7.9 %collective-permute-done = bf16[16,4096]{1,0:T(8,128)(2,1)S(1)} collective-permute-done((bf16[16,4096]{1,0:T(8,128)(2,1)S(1)}, bf16[16,4096]{1,0:T(8,128)(2,1)S(1)}, u32[]{:S(2)}, u32[]{:S(2)}) %collective-permute-start) | collective-permute-done | bytes 131104 | tf_op jit(solution)/shard_map/while/body/eval_jaxpr/ppermute | solution.py:17
  162.0 7.9 %collective-permute-done = bf16[16,4096]{1,0:T(8,128)(2,1)S(1)} collective-permute-done((bf16[16,4096]{1,0:T(8,128)(2,1)S(1)}, bf16[16,4096]{1,0:T(8,128)(2,1)S(1)}, u32[]{:S(2)}, u32[]{:S(2)}) %collective-permute-start) | collective-permute-done | bytes 131104 | tf_op jit(solution)/shard_map/while/body/eval_jaxpr/ppermute | solution.py:17
  176.3 7.9 %collective-permute-done = bf16[16,4096]{1,0:T(8,128)(2,1)S(1)} collective-permute-done((bf16[16,4096]{1,0:T(8,128)(2,1)S(1)}, bf16[16,4096]{1,0:T(8,128)(2,1)S(1)}, u32[]{:S(2)}, u32[]{:S(2)}) %collective-permute-start) | collective-permute-done | bytes 131104 | tf_op jit(solution)/shard_map/while/body/eval_jaxpr/ppermute | solution.py:17
  190.5 7.9 %collective-permute-done = bf16[16,4096]{1,0:T(8,128)(2,1)S(1)} collective-permute-done((bf16[16,4096]{1,0:T(8,128)(2,1)S(1)}, bf16[16,4096]{1,0:T(8,128)(2,1)S(1)}, u32[]{:S(2)}, u32[]{:S(2)}) %collective-permute-start) | collective-permute-done | bytes 131104 | tf_op jit(solution)/shard_map/while/body/eval_jaxpr/ppermute | solution.py:17
  204.8 8.3 %collective-permute-done = bf16[16,4096]{1,0:T(8,128)(2,1)S(1)} collective-permute-done((bf16[16,4096]{1,0:T(8,128)(2,1)S(1)}, bf16[16,4096]{1,0:T(8,128)(2,1)S(1)}, u32[]{:S(2)}, u32[]{:S(2)}) %collective-permute-start) | collective-permute-done | bytes 131104 | tf_op jit(solution)/shard_map/while/body/eval_jaxpr/ppermute | solution.py:17
  219.4 9.5 %collective-permute-done = bf16[16,4096]{1,0:T(8,128)(2,1)S(1)} collective-permute-done((bf16[16,4096]{1,0:T(8,128)(2,1)S(1)}, bf16[16,4096]{1,0:T(8,128)(2,1)S(1)}, u32[]{:S(2)}, u32[]{:S(2)}) %collective-permute-start) | collective-permute-done | bytes 131104 | tf_op jit(solution)/shard_map/while/body/eval_jaxpr/ppermute | solution.py:17
  235.1 8.6 %collective-permute-done = bf16[16,4096]{1,0:T(8,128)(2,1)S(1)} collective-permute-done((bf16[16,4096]{1,0:T(8,128)(2,1)S(1)}, bf16[16,4096]{1,0:T(8,128)(2,1)S(1)}, u32[]{:S(2)}, u32[]{:S(2)}) %collective-permute-start) | collective-permute-done | bytes 131104 | tf_op jit(solution)/shard_map/while/body/eval_jaxpr/ppermute | solution.py:17
  245.3 1.7 fusion.55
  250.1 7.9 %collective-permute-done = bf16[16,4096]{1,0:T(8,128)(2,1)S(1)} collective-permute-done((bf16[16,4096]{1,0:T(8,128)(2,1)S(1)}, bf16[16,4096]{1,0:T(8,128)(2,1)S(1)}, u32[]{:S(2)}, u32[]{:S(2)}) %collective-permute-start) | collective-permute-done | bytes 131104 | tf_op jit(solution)/shard_map/while/body/eval_jaxpr/ppermute | solution.py:17
  264.3 7.9 %collective-permute-done = bf16[16,4096]{1,0:T(8,128)(2,1)S(1)} collective-permute-done((bf16[16,4096]{1,0:T(8,128)(2,1)S(1)}, bf16[16,4096]{1,0:T(8,128)(2,1)S(1)}, u32[]{:S(2)}, u32[]{:S(2)}) %collective-permute-start) | collective-permute-done | bytes 131104 | tf_op jit(solution)/shard_map/while/body/eval_jaxpr/ppermute | solution.py:17
  278.6 7.9 %collective-permute-done = bf16[16,4096]{1,0:T(8,128)(2,1)S(1)} collective-permute-done((bf16[16,4096]{1,0:T(8,128)(2,1)S(1)}, bf16[16,4096]{1,0:T(8,128)(2,1)S(1)}, u32[]{:S(2)}, u32[]{:S(2)}) %collective-permute-start) | collective-permute-done | bytes 131104 | tf_op jit(solution)/shard_map/while/body/eval_jaxpr/ppermute | solution.py:17
  292.8 7.9 %collective-permute-done = bf16[16,4096]{1,0:T(8,128)(2,1)S(1)} collective-permute-done((bf16[16,4096]{1,0:T(8,128)(2,1)S(1)}, bf16[16,4096]{1,0:T(8,128)(2,1)S(1)}, u32[]{:S(2)}, u32[]{:S(2)}) %collective-permute-start) | collective-permute-done | bytes 131104 | tf_op jit(solution)/shard_map/while/body/eval_jaxpr/ppermute | solution.py:17
  307.0 7.9 %collective-permute-done = bf16[16,4096]{1,0:T(8,128)(2,1)S(1)} collective-permute-done((bf16[16,4096]{1,0:T(8,128)(2,1)S(1)}, bf16[16,4096]{1,0:T(8,128)(2,1)S(1)}, u32[]{:S(2)}, u32[]{:S(2)}) %collective-permute-start) | collective-permute-done | bytes 131104 | tf_op jit(solution)/shard_map/while/body/eval_jaxpr/ppermute | solution.py:17
  321.2 7.9 %collective-permute-done = bf16[16,4096]{1,0:T(8,128)(2,1)S(1)} collective-permute-done((bf16[16,4096]{1,0:T(8,128)(2,1)S(1)}, bf16[16,4096]{1,0:T(8,128)(2,1)S(1)}, u32[]{:S(2)}, u32[]{:S(2)}) %collective-permute-start) | collective-permute-done | bytes 131104 | tf_op jit(solution)/shard_map/while/body/eval_jaxpr/ppermute | solution.py:17
  335.5 7.9 %collective-permute-done = bf16[16,4096]{1,0:T(8,128)(2,1)S(1)} collective-permute-done((bf16[16,4096]{1,0:T(8,128)(2,1)S(1)}, bf16[16,4096]{1,0:T(8,128)(2,1)S(1)}, u32[]{:S(2)}, u32[]{:S(2)}) %collective-permute-start) | collective-permute-done | bytes 131104 | tf_op jit(solution)/shard_map/while/body/eval_jaxpr/ppermute | solution.py:17
  349.7 7.9 %collective-permute-done = bf16[16,4096]{1,0:T(8,128)(2,1)S(1)} collective-permute-done((bf16[16,4096]{1,0:T(8,128)(2,1)S(1)}, bf16[16,4096]{1,0:T(8,128)(2,1)S(1)}, u32[]{:S(2)}, u32[]{:S(2)}) %collective-permute-start) | collective-permute-done | bytes 131104 | tf_op jit(solution)/shard_map/while/body/eval_jaxpr/ppermute | solution.py:17
  363.9 7.9 %collective-permute-done = bf16[16,4096]{1,0:T(8,128)(2,1)S(1)} collective-permute-done((bf16[16,4096]{1,0:T(8,128)(2,1)S(1)}, bf16[16,4096]{1,0:T(8,128)(2,1)S(1)}, u32[]{:S(2)}, u32[]{:S(2)}) %collective-permute-start) | collective-permute-done | bytes 131104 | tf_op jit(solution)/shard_map/while/body/eval_jaxpr/ppermute | solution.py:17
  378.2 7.9 %collective-permute-done = bf16[16,4096]{1,0:T(8,128)(2,1)S(1)} collective-permute-done((bf16[16,4096]{1,0:T(8,128)(2,1)S(1)}, bf16[16,4096]{1,0:T(8,128)(2,1)S(1)}, u32[]{:S(2)}, u32[]{:S(2)}) %collective-permute-start) | collective-permute-done | bytes 131104 | tf_op jit(solution)/shard_map/while/body/eval_jaxpr/ppermute | solution.py:17
  392.4 7.9 %collective-permute-done = bf16[16,4096]{1,0:T(8,128)(2,1)S(1)} collective-permute-done((bf16[16,4096]{1,0:T(8,128)(2,1)S(1)}, bf16[16,4096]{1,0:T(8,128)(2,1)S(1)}, u32[]{:S(2)}, u32[]{:S(2)}) %collective-permute-start) | collective-permute-done | bytes 131104 | tf_op jit(solution)/shard_map/while/body/eval_jaxpr/ppermute | solution.py:17
  406.7 8.5 %collective-permute-done = bf16[16,4096]{1,0:T(8,128)(2,1)S(1)} collective-permute-done((bf16[16,4096]{1,0:T(8,128)(2,1)S(1)}, bf16[16,4096]{1,0:T(8,128)(2,1)S(1)}, u32[]{:S(2)}, u32[]{:S(2)}) %collective-permute-start) | collective-permute-done | bytes 131104 | tf_op jit(solution)/shard_map/while/body/eval_jaxpr/ppermute | solution.py:17
  421.5 9.3 %collective-permute-done = bf16[16,4096]{1,0:T(8,128)(2,1)S(1)} collective-permute-done((bf16[16,4096]{1,0:T(8,128)(2,1)S(1)}, bf16[16,4096]{1,0:T(8,128)(2,1)S(1)}, u32[]{:S(2)}, u32[]{:S(2)}) %collective-permute-start) | collective-permute-done | bytes 131104 | tf_op jit(solution)/shard_map/while/body/eval_jaxpr/ppermute | solution.py:17
  437.1 8.5 %collective-permute-done = bf16[16,4096]{1,0:T(8,128)(2,1)S(1)} collective-permute-done((bf16[16,4096]{1,0:T(8,128)(2,1)S(1)}, bf16[16,4096]{1,0:T(8,128)(2,1)S(1)}, u32[]{:S(2)}, u32[]{:S(2)}) %collective-permute-start) | collective-permute-done | bytes 131104 | tf_op jit(solution)/shard_map/while/body/eval_jaxpr/ppermute | solution.py:17
  447.1 1.7 fusion.55
  451.9 7.9 %collective-permute-done = bf16[16,4096]{1,0:T(8,128)(2,1)S(1)} collective-permute-done((bf16[16,4096]{1,0:T(8,128)(2,1)S(1)}, bf16[16,4096]{1,0:T(8,128)(2,1)S(1)}, u32[]{:S(2)}, u32[]{:S(2)}) %collective-permute-start) | collective-permute-done | bytes 131104 | tf_op jit(solution)/shard_map/while/body/eval_jaxpr/ppermute | solution.py:17
  466.1 7.9 %collective-permute-done = bf16[16,4096]{1,0:T(8,128)(2,1)S(1)} collective-permute-done((bf16[16,4096]{1,0:T(8,128)(2,1)S(1)}, bf16[16,4096]{1,0:T(8,128)(2,1)S(1)}, u32[]{:S(2)}, u32[]{:S(2)}) %collective-permute-start) | collective-permute-done | bytes 131104 | tf_op jit(solution)/shard_map/while/body/eval_jaxpr/ppermute | solution.py:17
  478.6 1.7 reshape.117
  480.4 3.9 all-to-all-start.2
  485.3 7.7 %all-to-all-done.2 = f32[32,1,512]{2,1,0:T(1,128)S(1)} async-done(((f32[32,1,512]{2,1,0:T(1,128)}), f32[32,1,512]{2,1,0:T(1,128)S(1)}, u32[]{:S(2)}, u32[]{:S(2)}) %all-to-all-start.2) | async-done | bytes 65568 | tf_op jit(solution)/shard_map/all_to_all | solution.py:127
  493.1 12.0 %all_to_all.15 = f32[32,1,512]{2,1,0:T(1,128)S(1)} all-to-all(f32[32,1,512]{2,1,0:T(1,128)S(1)} %reshape.115), channel_id=1, replica_groups=mesh['ctx'=32,'head'=4] {'ctx'}, dimensions={0} | all-to-all | bytes 131072 | tf_op jit(solution)/shard_map/all_to_all | solution.py:126
  505.0 5.0 all-to-all-start.1
  512.6 55.2 %all-to-all-done.1 = f32[32,16,32,128]{3,2,1,0:T(8,128)} async-done(((f32[32,16,32,128]{3,2,1,0:T(8,128)}), f32[32,16,32,128]{3,2,1,0:T(8,128)}, u32[]{:S(2)}, u32[]{:S(2)}) %all-to-all-start.1) | async-done | bytes 8388640 | tf_op jit(solution)/shard_map/all_to_all | solution.py:128
  567.8 5.3 multiply_reduce_fusion
  574.0 155.5 %all-gather.2.cloned.1.call-done = bf16[512,4096]{1,0:T(8,128)(2,1)} async-done(((bf16[16,4096]{1,0:T(8,128)(2,1)}), bf16[512,4096]{1,0:T(8,128)(2,1)}) %all-gather.2.cloned.1.call-update) | async-done | bytes 4194320 | tf_op jit(solution)/shard_map/all_gather | solution.py:132
  729.4 6.8 fusion.41
  736.2 20.1 %reduce-scatter.2.cloned.1.call-done = f32[128,512]{1,0:T(8,128)} async-done(((f32[512,512]{1,0:T(8,128)}), f32[128,512]{1,0:T(8,128)}) %reduce-scatter.2.cloned.1.call-update) | async-done | bytes 262160 | tf_op jit(solution)/shard_map/reduce_scatter | solution.py:136
  (618 shorter events, 211.0 us)
Async XLA Ops:
  6.5 4.4 copy-start.11
  6.5 4.5 copy-start.7
  10.2 0.9 copy-start.5
  11.0 0.5 copy-start.9
  11.1 2.0 copy-start.2
  13.1 0.6 copy-start.3
  19.4 2.5 copy-start.4
  24.5 1.1 copy-start.1
  25.6 3.4 copy-start.6
  25.6 3.4 copy-start.8
  25.6 3.4 copy-start.10
  25.6 3.4 copy-start
  29.0 12.8 %collective-permute-start = (bf16[16,4096]{1,0:T(8,128)(2,1)S(1)}, bf16[16,4096]{1,0:T(8,128)(2,1)S(1)}, u32[]{:S(2)}, u32[]{:S(2)}) collective-permute-start(bf16[16,4096]{1,0:T(8,128)(2,1)S(1)} %get-tuple-element.493), channel_id=1, source_target_pairs={{124,0},{0,4},{4,8},{8,12},{12,16},{16,20},{20,24},{24,28},{28,32}... | collective-permute-start | bytes 393224 | tf_op jit(solution)/shard_map/while/body/eval_jaxpr/ppermute | solution.py:17
  46.4 9.6 %collective-permute-start = (bf16[16,4096]{1,0:T(8,128)(2,1)S(1)}, bf16[16,4096]{1,0:T(8,128)(2,1)S(1)}, u32[]{:S(2)}, u32[]{:S(2)}) collective-permute-start(bf16[16,4096]{1,0:T(8,128)(2,1)S(1)} %get-tuple-element.493), channel_id=1, source_target_pairs={{124,0},{0,4},{4,8},{8,12},{12,16},{16,20},{20,24},{24,28},{28,32}... | collective-permute-start | bytes 393224 | tf_op jit(solution)/shard_map/while/body/eval_jaxpr/ppermute | solution.py:17
  60.7 9.6 %collective-permute-start = (bf16[16,4096]{1,0:T(8,128)(2,1)S(1)}, bf16[16,4096]{1,0:T(8,128)(2,1)S(1)}, u32[]{:S(2)}, u32[]{:S(2)}) collective-permute-start(bf16[16,4096]{1,0:T(8,128)(2,1)S(1)} %get-tuple-element.493), channel_id=1, source_target_pairs={{124,0},{0,4},{4,8},{8,12},{12,16},{16,20},{20,24},{24,28},{28,32}... | collective-permute-start | bytes 393224 | tf_op jit(solution)/shard_map/while/body/eval_jaxpr/ppermute | solution.py:17
  74.9 9.6 %collective-permute-start = (bf16[16,4096]{1,0:T(8,128)(2,1)S(1)}, bf16[16,4096]{1,0:T(8,128)(2,1)S(1)}, u32[]{:S(2)}, u32[]{:S(2)}) collective-permute-start(bf16[16,4096]{1,0:T(8,128)(2,1)S(1)} %get-tuple-element.493), channel_id=1, source_target_pairs={{124,0},{0,4},{4,8},{8,12},{12,16},{16,20},{20,24},{24,28},{28,32}... | collective-permute-start | bytes 393224 | tf_op jit(solution)/shard_map/while/body/eval_jaxpr/ppermute | solution.py:17
  89.1 9.6 %collective-permute-start = (bf16[16,4096]{1,0:T(8,128)(2,1)S(1)}, bf16[16,4096]{1,0:T(8,128)(2,1)S(1)}, u32[]{:S(2)}, u32[]{:S(2)}) collective-permute-start(bf16[16,4096]{1,0:T(8,128)(2,1)S(1)} %get-tuple-element.493), channel_id=1, source_target_pairs={{124,0},{0,4},{4,8},{8,12},{12,16},{16,20},{20,24},{24,28},{28,32}... | collective-permute-start | bytes 393224 | tf_op jit(solution)/shard_map/while/body/eval_jaxpr/ppermute | solution.py:17
  103.4 9.6 %collective-permute-start = (bf16[16,4096]{1,0:T(8,128)(2,1)S(1)}, bf16[16,4096]{1,0:T(8,128)(2,1)S(1)}, u32[]{:S(2)}, u32[]{:S(2)}) collective-permute-start(bf16[16,4096]{1,0:T(8,128)(2,1)S(1)} %get-tuple-element.493), channel_id=1, source_target_pairs={{124,0},{0,4},{4,8},{8,12},{12,16},{16,20},{20,24},{24,28},{28,32}... | collective-permute-start | bytes 393224 | tf_op jit(solution)/shard_map/while/body/eval_jaxpr/ppermute | solution.py:17
  117.6 9.6 %collective-permute-start = (bf16[16,4096]{1,0:T(8,128)(2,1)S(1)}, bf16[16,4096]{1,0:T(8,128)(2,1)S(1)}, u32[]{:S(2)}, u32[]{:S(2)}) collective-permute-start(bf16[16,4096]{1,0:T(8,128)(2,1)S(1)} %get-tuple-element.493), channel_id=1, source_target_pairs={{124,0},{0,4},{4,8},{8,12},{12,16},{16,20},{20,24},{24,28},{28,32}... | collective-permute-start | bytes 393224 | tf_op jit(solution)/shard_map/while/body/eval_jaxpr/ppermute | solution.py:17
  131.8 9.6 %collective-permute-start = (bf16[16,4096]{1,0:T(8,128)(2,1)S(1)}, bf16[16,4096]{1,0:T(8,128)(2,1)S(1)}, u32[]{:S(2)}, u32[]{:S(2)}) collective-permute-start(bf16[16,4096]{1,0:T(8,128)(2,1)S(1)} %get-tuple-element.493), channel_id=1, source_target_pairs={{124,0},{0,4},{4,8},{8,12},{12,16},{16,20},{20,24},{24,28},{28,32}... | collective-permute-start | bytes 393224 | tf_op jit(solution)/shard_map/while/body/eval_jaxpr/ppermute | solution.py:17
  146.1 9.6 %collective-permute-start = (bf16[16,4096]{1,0:T(8,128)(2,1)S(1)}, bf16[16,4096]{1,0:T(8,128)(2,1)S(1)}, u32[]{:S(2)}, u32[]{:S(2)}) collective-permute-start(bf16[16,4096]{1,0:T(8,128)(2,1)S(1)} %get-tuple-element.493), channel_id=1, source_target_pairs={{124,0},{0,4},{4,8},{8,12},{12,16},{16,20},{20,24},{24,28},{28,32}... | collective-permute-start | bytes 393224 | tf_op jit(solution)/shard_map/while/body/eval_jaxpr/ppermute | solution.py:17
  160.3 9.6 %collective-permute-start = (bf16[16,4096]{1,0:T(8,128)(2,1)S(1)}, bf16[16,4096]{1,0:T(8,128)(2,1)S(1)}, u32[]{:S(2)}, u32[]{:S(2)}) collective-permute-start(bf16[16,4096]{1,0:T(8,128)(2,1)S(1)} %get-tuple-element.493), channel_id=1, source_target_pairs={{124,0},{0,4},{4,8},{8,12},{12,16},{16,20},{20,24},{24,28},{28,32}... | collective-permute-start | bytes 393224 | tf_op jit(solution)/shard_map/while/body/eval_jaxpr/ppermute | solution.py:17
  174.6 9.6 %collective-permute-start = (bf16[16,4096]{1,0:T(8,128)(2,1)S(1)}, bf16[16,4096]{1,0:T(8,128)(2,1)S(1)}, u32[]{:S(2)}, u32[]{:S(2)}) collective-permute-start(bf16[16,4096]{1,0:T(8,128)(2,1)S(1)} %get-tuple-element.493), channel_id=1, source_target_pairs={{124,0},{0,4},{4,8},{8,12},{12,16},{16,20},{20,24},{24,28},{28,32}... | collective-permute-start | bytes 393224 | tf_op jit(solution)/shard_map/while/body/eval_jaxpr/ppermute | solution.py:17
  188.8 9.6 %collective-permute-start = (bf16[16,4096]{1,0:T(8,128)(2,1)S(1)}, bf16[16,4096]{1,0:T(8,128)(2,1)S(1)}, u32[]{:S(2)}, u32[]{:S(2)}) collective-permute-start(bf16[16,4096]{1,0:T(8,128)(2,1)S(1)} %get-tuple-element.493), channel_id=1, source_target_pairs={{124,0},{0,4},{4,8},{8,12},{12,16},{16,20},{20,24},{24,28},{28,32}... | collective-permute-start | bytes 393224 | tf_op jit(solution)/shard_map/while/body/eval_jaxpr/ppermute | solution.py:17
  203.1 10.0 %collective-permute-start = (bf16[16,4096]{1,0:T(8,128)(2,1)S(1)}, bf16[16,4096]{1,0:T(8,128)(2,1)S(1)}, u32[]{:S(2)}, u32[]{:S(2)}) collective-permute-start(bf16[16,4096]{1,0:T(8,128)(2,1)S(1)} %get-tuple-element.493), channel_id=1, source_target_pairs={{124,0},{0,4},{4,8},{8,12},{12,16},{16,20},{20,24},{24,28},{28,32}... | collective-permute-start | bytes 393224 | tf_op jit(solution)/shard_map/while/body/eval_jaxpr/ppermute | solution.py:17
  217.7 11.2 %collective-permute-start = (bf16[16,4096]{1,0:T(8,128)(2,1)S(1)}, bf16[16,4096]{1,0:T(8,128)(2,1)S(1)}, u32[]{:S(2)}, u32[]{:S(2)}) collective-permute-start(bf16[16,4096]{1,0:T(8,128)(2,1)S(1)} %get-tuple-element.493), channel_id=1, source_target_pairs={{124,0},{0,4},{4,8},{8,12},{12,16},{16,20},{20,24},{24,28},{28,32}... | collective-permute-start | bytes 393224 | tf_op jit(solution)/shard_map/while/body/eval_jaxpr/ppermute | solution.py:17
  233.5 10.3 %collective-permute-start = (bf16[16,4096]{1,0:T(8,128)(2,1)S(1)}, bf16[16,4096]{1,0:T(8,128)(2,1)S(1)}, u32[]{:S(2)}, u32[]{:S(2)}) collective-permute-start(bf16[16,4096]{1,0:T(8,128)(2,1)S(1)} %get-tuple-element.493), channel_id=1, source_target_pairs={{124,0},{0,4},{4,8},{8,12},{12,16},{16,20},{20,24},{24,28},{28,32}... | collective-permute-start | bytes 393224 | tf_op jit(solution)/shard_map/while/body/eval_jaxpr/ppermute | solution.py:17
  248.4 9.6 %collective-permute-start = (bf16[16,4096]{1,0:T(8,128)(2,1)S(1)}, bf16[16,4096]{1,0:T(8,128)(2,1)S(1)}, u32[]{:S(2)}, u32[]{:S(2)}) collective-permute-start(bf16[16,4096]{1,0:T(8,128)(2,1)S(1)} %get-tuple-element.493), channel_id=1, source_target_pairs={{124,0},{0,4},{4,8},{8,12},{12,16},{16,20},{20,24},{24,28},{28,32}... | collective-permute-start | bytes 393224 | tf_op jit(solution)/shard_map/while/body/eval_jaxpr/ppermute | solution.py:17
  262.6 9.6 %collective-permute-start = (bf16[16,4096]{1,0:T(8,128)(2,1)S(1)}, bf16[16,4096]{1,0:T(8,128)(2,1)S(1)}, u32[]{:S(2)}, u32[]{:S(2)}) collective-permute-start(bf16[16,4096]{1,0:T(8,128)(2,1)S(1)} %get-tuple-element.493), channel_id=1, source_target_pairs={{124,0},{0,4},{4,8},{8,12},{12,16},{16,20},{20,24},{24,28},{28,32}... | collective-permute-start | bytes 393224 | tf_op jit(solution)/shard_map/while/body/eval_jaxpr/ppermute | solution.py:17
  276.9 9.6 %collective-permute-start = (bf16[16,4096]{1,0:T(8,128)(2,1)S(1)}, bf16[16,4096]{1,0:T(8,128)(2,1)S(1)}, u32[]{:S(2)}, u32[]{:S(2)}) collective-permute-start(bf16[16,4096]{1,0:T(8,128)(2,1)S(1)} %get-tuple-element.493), channel_id=1, source_target_pairs={{124,0},{0,4},{4,8},{8,12},{12,16},{16,20},{20,24},{24,28},{28,32}... | collective-permute-start | bytes 393224 | tf_op jit(solution)/shard_map/while/body/eval_jaxpr/ppermute | solution.py:17
  291.1 9.6 %collective-permute-start = (bf16[16,4096]{1,0:T(8,128)(2,1)S(1)}, bf16[16,4096]{1,0:T(8,128)(2,1)S(1)}, u32[]{:S(2)}, u32[]{:S(2)}) collective-permute-start(bf16[16,4096]{1,0:T(8,128)(2,1)S(1)} %get-tuple-element.493), channel_id=1, source_target_pairs={{124,0},{0,4},{4,8},{8,12},{12,16},{16,20},{20,24},{24,28},{28,32}... | collective-permute-start | bytes 393224 | tf_op jit(solution)/shard_map/while/body/eval_jaxpr/ppermute | solution.py:17
  305.3 9.6 %collective-permute-start = (bf16[16,4096]{1,0:T(8,128)(2,1)S(1)}, bf16[16,4096]{1,0:T(8,128)(2,1)S(1)}, u32[]{:S(2)}, u32[]{:S(2)}) collective-permute-start(bf16[16,4096]{1,0:T(8,128)(2,1)S(1)} %get-tuple-element.493), channel_id=1, source_target_pairs={{124,0},{0,4},{4,8},{8,12},{12,16},{16,20},{20,24},{24,28},{28,32}... | collective-permute-start | bytes 393224 | tf_op jit(solution)/shard_map/while/body/eval_jaxpr/ppermute | solution.py:17
  319.5 9.6 %collective-permute-start = (bf16[16,4096]{1,0:T(8,128)(2,1)S(1)}, bf16[16,4096]{1,0:T(8,128)(2,1)S(1)}, u32[]{:S(2)}, u32[]{:S(2)}) collective-permute-start(bf16[16,4096]{1,0:T(8,128)(2,1)S(1)} %get-tuple-element.493), channel_id=1, source_target_pairs={{124,0},{0,4},{4,8},{8,12},{12,16},{16,20},{20,24},{24,28},{28,32}... | collective-permute-start | bytes 393224 | tf_op jit(solution)/shard_map/while/body/eval_jaxpr/ppermute | solution.py:17
  333.8 9.6 %collective-permute-start = (bf16[16,4096]{1,0:T(8,128)(2,1)S(1)}, bf16[16,4096]{1,0:T(8,128)(2,1)S(1)}, u32[]{:S(2)}, u32[]{:S(2)}) collective-permute-start(bf16[16,4096]{1,0:T(8,128)(2,1)S(1)} %get-tuple-element.493), channel_id=1, source_target_pairs={{124,0},{0,4},{4,8},{8,12},{12,16},{16,20},{20,24},{24,28},{28,32}... | collective-permute-start | bytes 393224 | tf_op jit(solution)/shard_map/while/body/eval_jaxpr/ppermute | solution.py:17
  348.0 9.6 %collective-permute-start = (bf16[16,4096]{1,0:T(8,128)(2,1)S(1)}, bf16[16,4096]{1,0:T(8,128)(2,1)S(1)}, u32[]{:S(2)}, u32[]{:S(2)}) collective-permute-start(bf16[16,4096]{1,0:T(8,128)(2,1)S(1)} %get-tuple-element.493), channel_id=1, source_target_pairs={{124,0},{0,4},{4,8},{8,12},{12,16},{16,20},{20,24},{24,28},{28,32}... | collective-permute-start | bytes 393224 | tf_op jit(solution)/shard_map/while/body/eval_jaxpr/ppermute | solution.py:17
  362.3 9.6 %collective-permute-start = (bf16[16,4096]{1,0:T(8,128)(2,1)S(1)}, bf16[16,4096]{1,0:T(8,128)(2,1)S(1)}, u32[]{:S(2)}, u32[]{:S(2)}) collective-permute-start(bf16[16,4096]{1,0:T(8,128)(2,1)S(1)} %get-tuple-element.493), channel_id=1, source_target_pairs={{124,0},{0,4},{4,8},{8,12},{12,16},{16,20},{20,24},{24,28},{28,32}... | collective-permute-start | bytes 393224 | tf_op jit(solution)/shard_map/while/body/eval_jaxpr/ppermute | solution.py:17
  376.5 9.6 %collective-permute-start = (bf16[16,4096]{1,0:T(8,128)(2,1)S(1)}, bf16[16,4096]{1,0:T(8,128)(2,1)S(1)}, u32[]{:S(2)}, u32[]{:S(2)}) collective-permute-start(bf16[16,4096]{1,0:T(8,128)(2,1)S(1)} %get-tuple-element.493), channel_id=1, source_target_pairs={{124,0},{0,4},{4,8},{8,12},{12,16},{16,20},{20,24},{24,28},{28,32}... | collective-permute-start | bytes 393224 | tf_op jit(solution)/shard_map/while/body/eval_jaxpr/ppermute | solution.py:17
  390.7 9.6 %collective-permute-start = (bf16[16,4096]{1,0:T(8,128)(2,1)S(1)}, bf16[16,4096]{1,0:T(8,128)(2,1)S(1)}, u32[]{:S(2)}, u32[]{:S(2)}) collective-permute-start(bf16[16,4096]{1,0:T(8,128)(2,1)S(1)} %get-tuple-element.493), channel_id=1, source_target_pairs={{124,0},{0,4},{4,8},{8,12},{12,16},{16,20},{20,24},{24,28},{28,32}... | collective-permute-start | bytes 393224 | tf_op jit(solution)/shard_map/while/body/eval_jaxpr/ppermute | solution.py:17
  405.0 10.2 %collective-permute-start = (bf16[16,4096]{1,0:T(8,128)(2,1)S(1)}, bf16[16,4096]{1,0:T(8,128)(2,1)S(1)}, u32[]{:S(2)}, u32[]{:S(2)}) collective-permute-start(bf16[16,4096]{1,0:T(8,128)(2,1)S(1)} %get-tuple-element.493), channel_id=1, source_target_pairs={{124,0},{0,4},{4,8},{8,12},{12,16},{16,20},{20,24},{24,28},{28,32}... | collective-permute-start | bytes 393224 | tf_op jit(solution)/shard_map/while/body/eval_jaxpr/ppermute | solution.py:17
  419.8 11.0 %collective-permute-start = (bf16[16,4096]{1,0:T(8,128)(2,1)S(1)}, bf16[16,4096]{1,0:T(8,128)(2,1)S(1)}, u32[]{:S(2)}, u32[]{:S(2)}) collective-permute-start(bf16[16,4096]{1,0:T(8,128)(2,1)S(1)} %get-tuple-element.493), channel_id=1, source_target_pairs={{124,0},{0,4},{4,8},{8,12},{12,16},{16,20},{20,24},{24,28},{28,32}... | collective-permute-start | bytes 393224 | tf_op jit(solution)/shard_map/while/body/eval_jaxpr/ppermute | solution.py:17
  435.4 10.2 %collective-permute-start = (bf16[16,4096]{1,0:T(8,128)(2,1)S(1)}, bf16[16,4096]{1,0:T(8,128)(2,1)S(1)}, u32[]{:S(2)}, u32[]{:S(2)}) collective-permute-start(bf16[16,4096]{1,0:T(8,128)(2,1)S(1)} %get-tuple-element.493), channel_id=1, source_target_pairs={{124,0},{0,4},{4,8},{8,12},{12,16},{16,20},{20,24},{24,28},{28,32}... | collective-permute-start | bytes 393224 | tf_op jit(solution)/shard_map/while/body/eval_jaxpr/ppermute | solution.py:17
  450.2 9.6 %collective-permute-start = (bf16[16,4096]{1,0:T(8,128)(2,1)S(1)}, bf16[16,4096]{1,0:T(8,128)(2,1)S(1)}, u32[]{:S(2)}, u32[]{:S(2)}) collective-permute-start(bf16[16,4096]{1,0:T(8,128)(2,1)S(1)} %get-tuple-element.493), channel_id=1, source_target_pairs={{124,0},{0,4},{4,8},{8,12},{12,16},{16,20},{20,24},{24,28},{28,32}... | collective-permute-start | bytes 393224 | tf_op jit(solution)/shard_map/while/body/eval_jaxpr/ppermute | solution.py:17
  464.4 9.6 %collective-permute-start = (bf16[16,4096]{1,0:T(8,128)(2,1)S(1)}, bf16[16,4096]{1,0:T(8,128)(2,1)S(1)}, u32[]{:S(2)}, u32[]{:S(2)}) collective-permute-start(bf16[16,4096]{1,0:T(8,128)(2,1)S(1)} %get-tuple-element.493), channel_id=1, source_target_pairs={{124,0},{0,4},{4,8},{8,12},{12,16},{16,20},{20,24},{24,28},{28,32}... | collective-permute-start | bytes 393224 | tf_op jit(solution)/shard_map/while/body/eval_jaxpr/ppermute | solution.py:17
  480.4 12.7 %all-to-all-start.2 = ((f32[32,1,512]{2,1,0:T(1,128)}), f32[32,1,512]{2,1,0:T(1,128)S(1)}, u32[]{:S(2)}, u32[]{:S(2)}) async-start(f32[32,1,512]{2,1,0:T(1,128)} %reshape.117), calls=%async_computation.2 | async-start | bytes 131072 | tf_op jit(solution)/shard_map/all_to_all | solution.py:127
  505.0 62.8 %all-to-all-start.1 = ((f32[32,16,32,128]{3,2,1,0:T(8,128)}), f32[32,16,32,128]{3,2,1,0:T(8,128)}, u32[]{:S(2)}, u32[]{:S(2)}) async-start(f32[32,16,32,128]{3,2,1,0:T(8,128)} %get-tuple-element.273), calls=%async_computation.1 | async-start | bytes 16777216 | tf_op jit(solution)/shard_map/all_to_all | solution.py:128
  510.0 219.4 %all-gather.2.cloned.1.call-start = ((), (), s32[]{:S(2)}) async-start(), calls=%async_computation.4 | async-start | bytes 4325376 | tf_op jit(solution)/shard_map/all_gather | solution.py:132
  573.9 182.4 %reduce-scatter.2.cloned.1.call-start = ((), (), s32[]{:S(2)}) async-start(), calls=%async_computation.5 | async-start | bytes 1310720 | tf_op jit(solution)/shard_map/reduce_scatter | solution.py:136
Sparse Core Ops, SparseCore 0:
  574.0 155.3 all-gather.1
  736.3 19.9 reduce-scatter.1
where the time goes:
time: 769 us; the launch traced here: 765 us
  waiting for transfers between devices  490 us (64%)
  local copies, waits for them, and re-layouts  90.5 us (12%)
  matrix products  83.3 us (11%)
  other arithmetic  58 us (8%)
  between operations  14.3 us (2%)
  starting transfers between devices  13.4 us (2%)
  blocking collectives  12 us (2%)
    ppermute x31, waiting for transfers between devices, passed_along(): return lax.ppermute(block, axis, route)  252 us
    all_gather x1, waiting for transfers between devices, shards(): lax.all_gather(attended, 'ctx', axis=0, tiled=True)  155 us
    all_to_all x1, waiting for transfers between devices, shards(): lax.all_to_all(outbox[2], 'ctx', split_axis=0, concat_axis=0, tiled=True)  55.2 us
    dot_general x32, matrix products, attend(): jnp.einsum('aqgn,nad->qagd', weights.astype(jnp.bfloat16), res_values, pr...  54.7 us
    dynamic_update_slice x65, local copies, waits for them, and re-layouts, record(): placed.append(lax.dynamic_update_slice(buffer, new_piece[None], corner))  43.2 us
    dynamic_slice x31, local copies, waits for them, and re-layouts, visit(): lax.dynamic_slice_in_dim(pos_ids, owner * token_count + first_row, blocks...  23.5 us
    broadcast_in_dim x31, other arithmetic, attend(): jnp.broadcast_to(cache_live[None, :], (row_count, cache_live.shape[0]))  22.3 us
    dot_general x32, matrix products, attend(): jnp.einsum('qagd,nad->aqgn', grouped, res_keys, preferred_element_type=jn...  21.8 us
  transfers between devices with their start and end apart: 35, of which 35 were waited for; matrix products, arithmetic and copies ran while one was open for 7% of the time, Pallas kernels for 0%

commit v1 on v0

v1 whole, which is shorter than its diff:
```python
import math

import jax
import jax.numpy as jnp
import numpy as np
from jax import lax
from jax.experimental import pallas as pl
from jax.experimental.pallas import tpu as pltpu
from jax.sharding import Mesh
from jax.sharding import PartitionSpec as P

HD = 128
SPAN = 128
KEY_BLOCK = 512
FILL = -1e30
LOG2_SCALE = math.log2(math.e) / math.sqrt(HD)
F32 = jnp.float32
BF16 = jnp.bfloat16
VMEM = pl.BlockSpec(memory_space=pltpu.VMEM)
SMEM = pl.BlockSpec(memory_space=pltpu.SMEM)


def dot_nt(a, b):
    return lax.dot_general(a, b, (((1,), (1,)), ((), ())), preferred_element_type=F32)


def grant(mib):
    return pltpu.CompilerParams(vmem_limit_bytes=mib << 20)


def pack_kernel(place, live, keys, values, new_keys, new_values, *outs):
    slots = live.shape[0]
    rows = slots * SPAN
    fresh = new_keys.shape[0]
    row_id = lax.broadcasted_iota(jnp.int32, (SPAN, HD), 0)
    lane_id = lax.broadcasted_iota(jnp.int32, (16, HD), 1)
    counts = jnp.zeros((16, HD), F32)
    for s in range(slots):
        counts = jnp.where(lane_id == s, live[s].astype(F32), counts)
    for k, out in enumerate(outs):
        head = lax.rem(place[0] + k, 4) // 2
        cols = pl.ds(pl.multiple_of(head * HD, HD), HD)
        for s in range(slots):
            part = pl.ds(s * SPAN, SPAN)
            visible = row_id < live[s]
            key = keys[part, cols].astype(F32)
            key = jnp.where(visible, key, jnp.broadcast_to(key[:1], key.shape))
            out[0, part, :] = key.astype(BF16)
            out[1, part, :] = jnp.where(visible, values[part, cols].astype(F32), 0.0).astype(BF16)
        out[0, rows : rows + fresh, :] = new_keys[:, cols]
        out[1, rows : rows + fresh, :] = new_values[:, cols]
        out[0, rows + fresh :, :] = counts.astype(BF16)
        out[1, rows + fresh :, :] = counts.astype(BF16)


def attend_kernel(live, queries, kv0, kv1, kv2, kv3, pos_q, pos_n, out, kc, vc, kn, vn, scores, fresh_scores, peak, top, acc):
    sources = (kv0, kv1, kv2, kv3)
    slots = live.shape[0] // len(sources)
    rows = slots * SPAN
    fresh = pos_n.shape[1] // len(sources) // 2
    heads = queries.shape[1] // HD
    tokens = queries.shape[0]
    row_id = lax.broadcasted_iota(jnp.int32, (SPAN, HD), 0)

    kn[...] = jnp.zeros_like(kn)
    vn[:, :HD] = jnp.zeros((vn.shape[0], HD), BF16)
    vn[:, HD:] = jnp.ones((vn.shape[0], HD), BF16)
    place = jnp.int32(0)
    for i, kv in enumerate(sources):
        kn[i * fresh : (i + 1) * fresh, :] = kv[0, rows : rows + fresh, :]
        vn[i * fresh : (i + 1) * fresh, :HD] = kv[1, rows : rows + fresh, :]

        def gather_slot(s, at, kv=kv, i=i):
            count = live[i * slots + s]
            source = pl.ds(pl.multiple_of(s * SPAN, SPAN), SPAN)
            target = pl.ds(pl.multiple_of(at, 16), SPAN)
            kc[target, :] = kv[0, source, :]
            vc[target, :HD] = kv[1, source, :]
            vc[target, HD:] = jnp.where(row_id < count, 1.0, 0.0).astype(BF16)
            return at + ((count + 15) // 16) * 16

        place = lax.fori_loop(0, slots, gather_slot, place)
    tail = pl.ds(pl.multiple_of(place, 16), KEY_BLOCK)
    spare = kc[:16, :].astype(F32)[:1]
    kc[tail, :] = jnp.broadcast_to(spare, (KEY_BLOCK, HD)).astype(BF16)
    vc[tail, :] = jnp.zeros((KEY_BLOCK, 2 * HD), BF16)
    blocks = (place + KEY_BLOCK - 1) // KEY_BLOCK

    seen = pos_n[...] <= pos_q[...]
    lane_id = lax.broadcasted_iota(jnp.int32, (tokens, HD), 1)

    def head_cols(h):
        if isinstance(h, int):
            return pl.ds(h * HD, HD)
        return pl.ds(pl.multiple_of(h * HD, HD), HD)

    def block_rows(b):
        return pl.ds(pl.multiple_of(b * KEY_BLOCK, KEY_BLOCK), KEY_BLOCK)

    def score_fresh(h, slot):
        s = jnp.where(seen, dot_nt(queries[:, head_cols(h)], kn[...]), FILL)
        fresh_scores[slot] = s
        peak[...] = s

    def score_block(h, slot, b):
        s = dot_nt(queries[:, head_cols(h)], kc[block_rows(b), :])
        scores[slot, b] = s
        high = peak[...]
        for j in range(KEY_BLOCK // HD):
            high = jnp.maximum(high, s[:, j * HD : (j + 1) * HD])
        peak[...] = high

    def score_end(slot):
        m = jnp.max(peak[...], axis=1, keepdims=True) * LOG2_SCALE
        top[slot] = jnp.broadcast_to(m.astype(BF16).astype(F32), (tokens, HD))

    def weigh_fresh(slot):
        p = jnp.where(seen, jnp.exp2(fresh_scores[slot] * LOG2_SCALE - top[slot]), 0.0)
        acc[...] = jnp.dot(p.astype(BF16), vn[...], preferred_element_type=F32)

    def weigh_block(slot, b):
        m = top[slot]
        p = [
            jnp.exp2(scores[slot, b, :, j * HD : (j + 1) * HD] * LOG2_SCALE - m).astype(BF16)
            for j in range(KEY_BLOCK // HD)
        ]
        p = jnp.concatenate(p, axis=1)
        acc[...] += jnp.dot(p, vc[block_rows(b), :], preferred_element_type=F32)

    def weigh_end(h, slot):
        total = acc[:, HD:]
        high = total.astype(BF16).astype(F32)
        out[:, head_cols(h)] = acc[:, :HD].astype(BF16)
        notes = out[:, heads * HD :].astype(F32)
        notes = jnp.where(lane_id == h, top[slot], notes)
        notes = jnp.where(lane_id == heads + h, high, notes)
        notes = jnp.where(lane_id == 2 * heads + h, total - high, notes)
        out[:, heads * HD :] = notes.astype(BF16)

    out[:, heads * HD :] = jnp.zeros((tokens, HD), BF16)
    score_fresh(0, 0)

    def first(b, _):
        score_block(0, 0, b)
        return _

    lax.fori_loop(0, blocks, first, 0)
    score_end(0)

    def step(h, _):
        slot = lax.rem(h, 2)
        weigh_fresh(1 - slot)
        score_fresh(h, slot)

        def both(b, _):
            weigh_block(1 - slot, b)
            score_block(h, slot, b)
            return _

        lax.fori_loop(0, blocks, both, 0)
        score_end(slot)
        weigh_end(h - 1, 1 - slot)
        return _

    lax.fori_loop(1, heads, step, 0)
    last = (heads - 1) % 2
    weigh_fresh(last)

    def final(b, _):
        weigh_block(last, b)
        return _

    lax.fori_loop(0, blocks, final, 0)
    weigh_end(heads - 1, last)


def settle_kernel(parts, out):
    groups, tokens, width = parts.shape
    heads = width // HD - 1
    notes = [parts[g, :, heads * HD :].astype(F32) for g in range(groups)]
    highest = notes[0]
    for g in range(1, groups):
        highest = jnp.maximum(highest, notes[g])
    factors = [jnp.exp2(notes[g] - highest) for g in range(groups)]
    for h in range(heads):
        cols = slice(h * HD, (h + 1) * HD)
        numerator = jnp.zeros((tokens, HD), F32)
        total = jnp.zeros((tokens, 1), F32)
        for g in range(groups):
            factor = factors[g][:, h : h + 1]
            numerator += factor * parts[g, :, cols].astype(F32)
            total += factor * (
                notes[g][:, heads + h : heads + h + 1] + notes[g][:, 2 * heads + h : 2 * heads + h + 1]
            )
        attended = (numerator / total).astype(BF16)
        for g in range(groups):
            out[g, :, cols] = attended


def project_kernel(place, attended, w0, w1, w2, w3, out):
    for k, w in enumerate((w0, w1, w2, w3)):
        target = lax.rem(place[0] + 4 - k, 4)
        for r in range(out.shape[1]):
            rows = slice(r * out.shape[2], (r + 1) * out.shape[2])
            out[target, r] = jnp.dot(attended[rows, :], w[...], preferred_element_type=F32).astype(BF16)


def swap(x, axes):
    return lax.all_to_all(x, axes, split_axis=0, concat_axis=0, tiled=False)


def along_y(x, distance):
    return lax.ppermute(x, "y", [(i, (i + distance) % 4) for i in range(4)])


def shards(
    queries,
    new_keys,
    new_values,
    cache_keys,
    cache_values,
    span_ids,
    valid_len,
    pos_ids,
    offset,
    out_weight,
):
    y = lax.axis_index("y")
    group = lax.axis_index("z") * 2 + lax.axis_index("x_hi")
    place = y[None].astype(jnp.int32)
    groups = 8
    fresh, width = queries.shape
    slots = span_ids.shape[0]
    rows = slots * SPAN
    quarter = width // 4
    tokens = pos_ids.shape[0]

    live = jnp.clip(jnp.minimum(valid_len, offset[0] - span_ids * SPAN), 0, SPAN)
    packet = jax.ShapeDtypeStruct((2, rows + fresh + 16, HD), BF16)
    with jax.named_scope("pack"):
        packets = pl.pallas_call(
            pack_kernel,
            out_shape=[packet] * 4,
            in_specs=[SMEM, SMEM] + [VMEM] * 4,
            out_specs=[VMEM] * 4,
            compiler_params=grant(24),
            cost_estimate=pl.CostEstimate(flops=0, bytes_accessed=4 << 20, transcendentals=0),
        )(place, live, cache_keys, cache_values, new_keys, new_values)
    with jax.named_scope("move_kv"):
        kv = [packets[0]] + [along_y(packets[k], k) for k in range(1, 4)]

    with jax.named_scope("move_queries"):
        mine = swap(queries.reshape(fresh, 4, quarter).transpose(1, 0, 2), "y")
        mine = mine.reshape(4 * fresh, quarter)
        mine = swap(jnp.broadcast_to(mine[None], (groups,) + mine.shape), ("z", "x_hi"))
        mine = mine.reshape(tokens, quarter)

    lives = [live] + [kv[k][0, rows + fresh, :slots].astype(jnp.int32) for k in range(1, 4)]
    pos_n = [
        lax.dynamic_slice_in_dim(pos_ids, (group * 4 + lax.rem(y + 4 - k, 4)) * fresh, fresh) for k in range(4)
    ]
    pos_n = jnp.concatenate(pos_n + [jnp.full((4 * fresh,), 1 << 30, jnp.int32)])[None]
    pos_q = pos_ids[:, None]
    all_live = jnp.concatenate(lives)

    with jax.named_scope("move_weight"):
        late = jnp.minimum(sum(l[0] for l in lives), 0)
        weights = [lax.dynamic_slice_in_dim(out_weight, y * quarter, quarter)]
        for k in range(1, 4):
            first = lax.rem(y + k, 4) * quarter + late
            weights.append(along_y(lax.dynamic_slice_in_dim(out_weight, first, quarter), k))

    capacity = 4 * rows + KEY_BLOCK
    most_blocks = -(-4 * rows // KEY_BLOCK)
    heads = quarter // HD
    with jax.named_scope("attend"):
        partial = pl.pallas_call(
            attend_kernel,
            out_shape=jax.ShapeDtypeStruct((tokens, quarter + HD), BF16),
            in_specs=[SMEM] + [VMEM] * 7,
            out_specs=VMEM,
            scratch_shapes=[
                pltpu.VMEM((capacity, HD), BF16),
                pltpu.VMEM((capacity, 2 * HD), BF16),
                pltpu.VMEM((8 * fresh, HD), BF16),
                pltpu.VMEM((8 * fresh, 2 * HD), BF16),
                pltpu.VMEM((2, most_blocks, tokens, KEY_BLOCK), F32),
                pltpu.VMEM((2, tokens, HD), F32),
                pltpu.VMEM((tokens, HD), F32),
                pltpu.VMEM((2, tokens, HD), F32),
                pltpu.VMEM((tokens, 2 * HD), F32),
            ],
            compiler_params=grant(40),
            cost_estimate=pl.CostEstimate(
                flops=8 * tokens * quarter * rows, bytes_accessed=5 << 20, transcendentals=tokens * heads * rows * 2
            ),
        )(all_live, mine, *kv, pos_q, pos_n)

    with jax.named_scope("move_partials"):
        partial = swap(partial.reshape(groups, tokens // groups, quarter + HD), ("z", "x_hi"))
    with jax.named_scope("settle"):
        attended = pl.pallas_call(
            settle_kernel,
            out_shape=jax.ShapeDtypeStruct((groups, tokens // groups, quarter), BF16),
            in_specs=[VMEM],
            out_specs=VMEM,
            compiler_params=grant(24),
            cost_estimate=pl.CostEstimate(flops=1 << 22, bytes_accessed=2 << 20, transcendentals=0),
        )(partial)
    with jax.named_scope("move_attended"):
        attended = swap(attended, ("z", "x_hi")).reshape(tokens, quarter)

    with jax.named_scope("project"):
        columns = out_weight.shape[1]
        terms = pl.pallas_call(
            project_kernel,
            out_shape=jax.ShapeDtypeStruct((4, 4, tokens // 4, columns), BF16),
            in_specs=[SMEM] + [VMEM] * 5,
            out_specs=VMEM,
            compiler_params=grant(32),
            cost_estimate=pl.CostEstimate(
                flops=8 * tokens * quarter * columns, bytes_accessed=7 << 20, transcendentals=0
            ),
        )(place, attended, *weights)
    with jax.named_scope("move_terms"):
        terms = swap(terms.reshape(16, tokens // 4, columns), ("y", "x_lo", "core"))
    return jnp.sum(terms.astype(F32), axis=0).astype(BF16)


def solution(mesh):
    fine = Mesh(mesh.devices.reshape(4, 2, 4, 2, 2), ("z", "x_hi", "y", "x_lo", "core"))
    ctx, head = ("z", "x_hi", "y"), ("x_lo", "core")
    in_specs = (
        P(ctx, head),
        P(ctx, head),
        P(ctx, head),
        P(ctx, head),
        P(ctx, head),
        P(ctx),
        P(ctx),
        P(),
        P(),
        P(head, ctx),
    )
    return jax.shard_map(shards, mesh=fine, in_specs=in_specs, out_specs=P(head, ctx), check_vma=False)
```

time: 769 us -> 180 us (0.23)
  waiting for transfers between devices: 490 us -> 50.5 us
  matrix products: 83.3 us -> 0 us
  local copies, waits for them, and re-layouts: 90.5 us -> 10.2 us
  other arithmetic: 58 us -> 2.41 us
  blocking collectives: 12 us -> 58.6 us
  Pallas kernels: 0 us -> 33.6 us
  between operations: 14.3 us -> 0.91 us
  starting transfers between devices: 13.4 us -> 22.4 us
    ppermute x31 -> x6, waiting for transfers between devices: 252 us -> 38.9 us  [along_y(): return lax.ppermute(x, 'y', [(i, (i + distance) % 4) for i in range(4)])]
    all_gather x1 -> x0, waiting for transfers between devices: 155 us -> none  [shards(): lax.all_gather(attended, 'ctx', axis=0, tiled=True)]
    dot_general x65 -> x0, matrix products: 83.3 us -> none  [the longest x32 54.7 us: attend(): jnp.einsum('aqgn,nad->qagd', weights.astype(jnp.bfloat16), res_values, pr...]
    all_to_all x2 -> x3, waiting for transfers between devices: 62.9 us -> 11.6 us  [swap(): return lax.all_to_all(x, axes, split_axis=0, concat_axis=0, tiled=False)]
    all_to_all x1 -> x2, blocking collectives: 12 us -> 58.6 us  [swap(): return lax.all_to_all(x, axes, split_axis=0, concat_axis=0, tiled=False)]
    dynamic_update_slice x65 -> x0, local copies, waits for them, and re-layouts: 43.2 us -> none  [record(): placed.append(lax.dynamic_update_slice(buffer, new_piece[None], corner))]
    pallas_call x0 -> x4, Pallas kernels: none -> 33.6 us  [the longest x1 25.5 us: shards(): pl.pallas_call(attend_kernel, out_shape=jax.ShapeDtypeStruct((tokens, qua...]
    reduce_sum x34 -> x1, other arithmetic: 26.1 us -> 0.96 us  [shards(): return jnp.sum(terms.astype(F32), axis=0).astype(BF16)]
  transfers between devices with their start and end apart: 35 -> 9, of which waited for: 35 -> 6; matrix products, arithmetic and copies ran while one was open for 7% -> 4% of each run, Pallas kernels for 0% -> 1%
where the time goes in v1:
time: 180 us; the launch traced here: 179 us
  blocking collectives  58.6 us (33%)
  waiting for transfers between devices  50.5 us (28%)
  Pallas kernels  33.6 us (19%)
  starting transfers between devices  22.4 us (12%)
  local copies, waits for them, and re-layouts  10.2 us (6%)
  other arithmetic  2.41 us (1%)
    all_to_all x2, blocking collectives, swap(): return lax.all_to_all(x, axes, split_axis=0, concat_axis=0, tiled=False)  58.6 us
    ppermute x6, waiting for transfers between devices, along_y(): return lax.ppermute(x, 'y', [(i, (i + distance) % 4) for i in range(4)])  38.9 us
    pallas_call x1, Pallas kernels, shards(): pl.pallas_call(attend_kernel, out_shape=jax.ShapeDtypeStruct((tokens, qua...  25.5 us
    all_to_all x3, starting transfers between devices, swap(): return lax.all_to_all(x, axes, split_axis=0, concat_axis=0, tiled=False)  15.5 us
    all_to_all x3, waiting for transfers between devices, swap(): return lax.all_to_all(x, axes, split_axis=0, concat_axis=0, tiled=False)  11.6 us
    ppermute x6, starting transfers between devices, along_y(): return lax.ppermute(x, 'y', [(i, (i + distance) % 4) for i in range(4)])  6.84 us
    dynamic_slice x1, local copies, waits for them, and re-layouts, shards(): lax.dynamic_slice_in_dim(out_weight, first, quarter)  4.26 us
    pallas_call x1, Pallas kernels, shards(): pl.pallas_call(project_kernel, out_shape=jax.ShapeDtypeStruct((4, 4, toke...  3.9 us
  transfers between devices with their start and end apart: 9, of which 6 were waited for; matrix products, arithmetic and copies ran while one was open for 4% of the time, Pallas kernels for 1%

profile of v1, /device:TPU:1, one launch (start us, length us, event | category | flops | bytes accessed | tf_op | source)
XLA Modules:
  0.0 178.6 jit_solution(12887534798453652467)
XLA Ops:
  0.7 0.7 minimum_clamp_fusion.live
  1.3 0.0 copy-start
  1.3 1.0 copy-done
  2.4 0.0 copy-start.1
  2.4 1.0 copy-done.1
  3.4 0.0 copy-start.2
  3.4 0.7 copy-done.2
  4.1 0.0 copy-start.3
  4.1 0.7 copy-done.3
  4.8 1.9 %pack.1 = (bf16[2,1056,128]{2,1,0:T(8,128)(2,1)S(1)}, bf16[2,1056,128]{2,1,0:T(8,128)(2,1)}, bf16[2,1056,128]{2,1,0:T(8,128)(2,1)}, bf16[2,1056,128]{2,1,0:T(8,128)(2,1)S(1)}) custom-call(s32[1]{0:T(128)} %bitcast.place, s32[8]{0:T(128)S(1)} %minimum_clamp_fusion.live, bf16[1024,256]{1,0:T(8,128)(2,1)S(1)} %copy-done, bf16[1024,256]{1,0:T(8,128)(2,1)S(1)} %copy-done.1, ...), custom_call_target="tpu_custom_call" | custom-call | bytes 4194304 | tf_op jit(solution)/shard_map/pack/pallas_call | solution.py:241
  6.7 0.0 copy-start.4
  6.7 2.1 %collective-permute-start = (bf16[2,1056,128]{2,1,0:T(8,128)(2,1)}, bf16[2,1056,128]{2,1,0:T(8,128)(2,1)S(1)}, u32[]{:S(2)}, u32[]{:S(2)}) collective-permute-start(bf16[2,1056,128]{2,1,0:T(8,128)(2,1)} %get-tuple-element.9), channel_id=1, source_target_pairs={{0,4},{4,8},{8,12},{12,0},{1,5},{5,9},{9,13},{13,1},{2,6},{6,10},{... | collective-permute-start | bytes 1622024 | tf_op jit(solution)/shard_map/move_kv/ppermute | solution.py:213
  8.8 2.6 %collective-permute-start.1 = (bf16[2,1056,128]{2,1,0:T(8,128)(2,1)}, bf16[2,1056,128]{2,1,0:T(8,128)(2,1)S(1)}, u32[]{:S(2)}, u32[]{:S(2)}) collective-permute-start(bf16[2,1056,128]{2,1,0:T(8,128)(2,1)} %get-tuple-element.10), channel_id=1, source_target_pairs={{0,8},{4,12},{8,0},{12,4},{1,9},{5,13},{9,1},{13,5},{2,10},{6,14},... | collective-permute-start | bytes 1622024 | tf_op jit(solution)/shard_map/move_kv/ppermute | solution.py:213
  11.4 1.0 reshape.26
  12.5 23.8 %all_to_all.25 = bf16[4,16,1024]{2,1,0:T(8,128)(2,1)S(1)} all-to-all(bf16[4,16,1024]{2,1,0:T(8,128)(2,1)S(1)} %copy.14), channel_id=1, replica_groups=mesh['z'=4,'x_hi'=2,'y'=4,'x_lo'=2,'core'=2] {'y'}, dimensions={0} | all-to-all | bytes 262144 | tf_op jit(solution)/shard_map/move_queries/all_to_all | solution.py:209
  36.3 1.1 broadcast_in_dim.21
  37.4 7.5 %all-to-all-start.1 = ((bf16[8,64,1024]{2,1,0:T(8,128)(2,1)}), bf16[8,64,1024]{2,1,0:T(8,128)(2,1)S(1)}, u32[]{:S(2)}, u32[]{:S(2)}) async-start(bf16[8,64,1024]{2,1,0:T(8,128)(2,1)} %broadcast_in_dim.21), calls=%async_computation.1 | async-start | bytes 2097152 | tf_op jit(solution)/shard_map/move_queries/all_to_all | solution.py:209
  44.9 0.0 collective-permute-start.2
  45.0 0.0 copy-done.4
  45.0 0.1 copy.15.pos_q
  45.2 0.1 fusion.3
  45.3 0.1 concatenate.7
  45.3 0.0 collective-permute-done.kv1
  45.3 0.0 collective-permute-done.1.kv2
  45.4 11.6 %collective-permute-done.2.kv3 = bf16[2,1056,128]{2,1,0:T(8,128)(2,1)} collective-permute-done((bf16[2,1056,128]{2,1,0:T(8,128)(2,1)S(1)}, bf16[2,1056,128]{2,1,0:T(8,128)(2,1)}, u32[]{:S(2)}, u32[]{:S(2)}) %collective-permute-start.2) | collective-permute-done | bytes 540704 | tf_op jit(solution)/shard_map/move_kv/ppermute | solution.py:213
  57.0 0.7 slice_convert_fusion
  57.7 0.1 pad_add_fusion.live
  57.7 2.3 %all-to-all-done.1 = bf16[8,64,1024]{2,1,0:T(8,128)(2,1)S(1)} async-done(((bf16[8,64,1024]{2,1,0:T(8,128)(2,1)}), bf16[8,64,1024]{2,1,0:T(8,128)(2,1)S(1)}, u32[]{:S(2)}, u32[]{:S(2)}) %all-to-all-start.1) | async-done | bytes 1048608 | tf_op jit(solution)/shard_map/move_queries/all_to_all | solution.py:209
  60.1 25.5 %attend.1 = bf16[512,1152]{1,0:T(8,128)(2,1)} custom-call(s32[32]{0:T(128)S(1)} %pad_add_fusion.live, bf16[512,1024]{1,0:T(8,128)(2,1)S(1)} %bitcast.26, bf16[2,1056,128]{2,1,0:T(8,128)(2,1)S(1)} %get-tuple-element.12.kv0, bf16[2,1056,128]{2,1,0:T(8,128)(2,1)S(1)} %collective-permute-done.kv1, bf16[2,1056,128]{2,1,0:T(8,128)(2,1)S(1)} %collective-permute-done.1.kv2, ...), custom_call_target="tpu_custom_call" | custom-call | flops 4294967296 | bytes 5242880 | tf_op jit(solution)/shard_map/attend/pallas_call | solution.py:277
  85.5 4.1 %all-to-all-start.2 = ((bf16[8,64,1152]{2,1,0:T(8,128)(2,1)}), bf16[8,64,1152]{2,1,0:T(8,128)(2,1)S(1)}, u32[]{:S(2)}, u32[]{:S(2)}) async-start(bf16[8,64,1152]{2,1,0:T(8,128)(2,1)} %bitcast.10), calls=%async_computation.2 | async-start | bytes 2359296 | tf_op jit(solution)/shard_map/move_partials/all_to_all | solution.py:209
  89.8 4.3 %constant_dynamic-slice_fusion = (bf16[1024,512]{1,0:T(8,128)(2,1)}, bf16[1024,512]{1,0:T(8,128)(2,1)}, bf16[1024,512]{1,0:T(8,128)(2,1)S(1)}, bf16[1024,512]{1,0:T(8,128)(2,1)}) fusion(bf16[4096,512]{1,0:T(8,128)(2,1)} %param.19, s32[]{:T(128)S(6)} %select_n.31, s32[]{:T(128)S(6)} %select_n.29, s32[]{:T(128)S(6)} %select_n.28, s32[]{:T(128)S(6)} %select_n.30), kind=kLoop, calls=%fused_computation | loop fusion | bytes 8388624 | tf_op jit(solution)/shard_map/move_weight/dynamic_slice | solution.py:271
  94.1 0.9 collective-permute-start.5
  95.0 0.6 collective-permute-start.3
  95.5 0.6 collective-permute-start.4
  96.2 9.2 %all-to-all-done.2.parts = bf16[8,64,1152]{2,1,0:T(8,128)(2,1)S(1)} async-done(((bf16[8,64,1152]{2,1,0:T(8,128)(2,1)}), bf16[8,64,1152]{2,1,0:T(8,128)(2,1)S(1)}, u32[]{:S(2)}, u32[]{:S(2)}) %all-to-all-start.2) | async-done | bytes 1179680 | tf_op jit(solution)/shard_map/move_partials/all_to_all | solution.py:209
  105.4 2.4 %settle.1 = bf16[8,64,1024]{2,1,0:T(8,128)(2,1)} custom-call(bf16[8,64,1152]{2,1,0:T(8,128)(2,1)S(1)} %all-to-all-done.2.parts), custom_call_target="tpu_custom_call" | custom-call | flops 4194304 | bytes 2097152 | tf_op jit(solution)/shard_map/settle/pallas_call | solution.py:302
  107.8 3.9 %all-to-all-start.3 = ((bf16[8,64,1024]{2,1,0:T(8,128)(2,1)}), bf16[8,64,1024]{2,1,0:T(8,128)(2,1)S(1)}, u32[]{:S(2)}, u32[]{:S(2)}) async-start(bf16[8,64,1024]{2,1,0:T(8,128)(2,1)} %settle.1), calls=%async_computation.3 | async-start | bytes 2097152 | tf_op jit(solution)/shard_map/move_attended/all_to_all | solution.py:209
  111.7 4.4 %collective-permute-done.5.w3 = bf16[1024,512]{1,0:T(8,128)(2,1)S(1)} collective-permute-done((bf16[1024,512]{1,0:T(8,128)(2,1)}, bf16[1024,512]{1,0:T(8,128)(2,1)S(1)}, u32[]{:S(2)}, u32[]{:S(2)}) %collective-permute-start.5) | collective-permute-done | bytes 1048608 | tf_op jit(solution)/shard_map/move_weight/ppermute | solution.py:213
  116.1 2.7 %collective-permute-done.3.w1 = bf16[1024,512]{1,0:T(8,128)(2,1)} collective-permute-done((bf16[1024,512]{1,0:T(8,128)(2,1)}, bf16[1024,512]{1,0:T(8,128)(2,1)}, u32[]{:S(2)}, u32[]{:S(2)}) %collective-permute-start.3) | collective-permute-done | bytes 1048608 | tf_op jit(solution)/shard_map/move_weight/ppermute | solution.py:213
  118.8 20.1 %collective-permute-done.4.w2 = bf16[1024,512]{1,0:T(8,128)(2,1)} collective-permute-done((bf16[1024,512]{1,0:T(8,128)(2,1)}, bf16[1024,512]{1,0:T(8,128)(2,1)}, u32[]{:S(2)}, u32[]{:S(2)}) %collective-permute-start.4) | collective-permute-done | bytes 1048608 | tf_op jit(solution)/shard_map/move_weight/ppermute | solution.py:213
  138.9 0.0 all-to-all-done.3
  138.9 3.9 %project.1 = bf16[4,4,128,512]{3,2,1,0:T(8,128)(2,1)S(1)} custom-call(s32[1]{0:T(128)} %bitcast.place, bf16[512,1024]{1,0:T(8,128)(2,1)S(1)} %bitcast.27, bf16[1024,512]{1,0:T(8,128)(2,1)S(1)} %get-tuple-element.15.w0, bf16[1024,512]{1,0:T(8,128)(2,1)} %collective-permute-done.3.w1, bf16[1024,512]{1,0:T(8,128)(2,1)} %collective-permute-done.4.w2, ...), custom_call_target="tpu_custom_call" | custom-call | flops 2147483648 | bytes 7340032 | tf_op jit(solution)/shard_map/project/pallas_call | solution.py:315
  142.9 34.8 %all_to_all.26 = bf16[16,128,512]{2,1,0:T(8,128)(2,1)S(1)} all-to-all(bf16[16,128,512]{2,1,0:T(8,128)(2,1)S(1)} %bitcast.25), channel_id=1, replica_groups=mesh['z'=4,'x_hi'=2,'y'=4,'x_lo'=2,'core'=2] {'y','x_lo','core'}, dimensions={0} | all-to-all | bytes 4194304 | tf_op jit(solution)/shard_map/move_terms/all_to_all | solution.py:209
  177.6 1.0 reduce_sum.12
  (4 shorter events, 0.1 us)
Async XLA Ops:
  1.3 1.0 copy-start
  2.4 1.0 copy-start.1
  3.4 0.7 copy-start.2
  4.1 0.7 copy-start.3
  6.7 38.3 %copy-start.4 = (s32[512]{0:T(512)S(1)}, s32[512]{0:T(512)}, u32[]{:S(2)}) copy-start(s32[512]{0:T(512)} %param.17) | copy-start | bytes 6148
  6.7 38.6 %collective-permute-start = (bf16[2,1056,128]{2,1,0:T(8,128)(2,1)}, bf16[2,1056,128]{2,1,0:T(8,128)(2,1)S(1)}, u32[]{:S(2)}, u32[]{:S(2)}) collective-permute-start(bf16[2,1056,128]{2,1,0:T(8,128)(2,1)} %get-tuple-element.9), channel_id=1, source_target_pairs={{0,4},{4,8},{8,12},{12,0},{1,5},{5,9},{9,13},{13,1},{2,6},{6,10},{... | collective-permute-start | bytes 1622024 | tf_op jit(solution)/shard_map/move_kv/ppermute | solution.py:213
  8.8 36.5 %collective-permute-start.1 = (bf16[2,1056,128]{2,1,0:T(8,128)(2,1)}, bf16[2,1056,128]{2,1,0:T(8,128)(2,1)S(1)}, u32[]{:S(2)}, u32[]{:S(2)}) collective-permute-start(bf16[2,1056,128]{2,1,0:T(8,128)(2,1)} %get-tuple-element.10), channel_id=1, source_target_pairs={{0,8},{4,12},{8,0},{12,4},{1,9},{5,13},{9,1},{13,5},{2,10},{6,14},... | collective-permute-start | bytes 1622024 | tf_op jit(solution)/shard_map/move_kv/ppermute | solution.py:213
  37.4 22.6 %all-to-all-start.1 = ((bf16[8,64,1024]{2,1,0:T(8,128)(2,1)}), bf16[8,64,1024]{2,1,0:T(8,128)(2,1)S(1)}, u32[]{:S(2)}, u32[]{:S(2)}) async-start(bf16[8,64,1024]{2,1,0:T(8,128)(2,1)} %broadcast_in_dim.21), calls=%async_computation.1 | async-start | bytes 2097152 | tf_op jit(solution)/shard_map/move_queries/all_to_all | solution.py:209
  44.9 12.0 %collective-permute-start.2 = (bf16[2,1056,128]{2,1,0:T(8,128)(2,1)S(1)}, bf16[2,1056,128]{2,1,0:T(8,128)(2,1)}, u32[]{:S(2)}, u32[]{:S(2)}) collective-permute-start(bf16[2,1056,128]{2,1,0:T(8,128)(2,1)S(1)} %get-tuple-element.11), channel_id=1, source_target_pairs={{0,12},{4,0},{8,4},{12,8},{1,13},{5,1},{9,5},{13,9},{2,14},{6,2},{... | collective-permute-start | bytes 1622024 | tf_op jit(solution)/shard_map/move_kv/ppermute | solution.py:213
  85.5 19.9 %all-to-all-start.2 = ((bf16[8,64,1152]{2,1,0:T(8,128)(2,1)}), bf16[8,64,1152]{2,1,0:T(8,128)(2,1)S(1)}, u32[]{:S(2)}, u32[]{:S(2)}) async-start(bf16[8,64,1152]{2,1,0:T(8,128)(2,1)} %bitcast.10), calls=%async_computation.2 | async-start | bytes 2359296 | tf_op jit(solution)/shard_map/move_partials/all_to_all | solution.py:209
  94.1 22.0 %collective-permute-start.5 = (bf16[1024,512]{1,0:T(8,128)(2,1)}, bf16[1024,512]{1,0:T(8,128)(2,1)S(1)}, u32[]{:S(2)}, u32[]{:S(2)}) collective-permute-start(bf16[1024,512]{1,0:T(8,128)(2,1)} %get-tuple-element.13), channel_id=1, source_target_pairs={{0,12},{4,0},{8,4},{12,8},{1,13},{5,1},{9,5},{13,9},{2,14},{6,2},{... | collective-permute-start | bytes 3145736 | tf_op jit(solution)/shard_map/move_weight/ppermute | solution.py:213
  95.0 23.9 %collective-permute-start.3 = (bf16[1024,512]{1,0:T(8,128)(2,1)}, bf16[1024,512]{1,0:T(8,128)(2,1)}, u32[]{:S(2)}, u32[]{:S(2)}) collective-permute-start(bf16[1024,512]{1,0:T(8,128)(2,1)} %get-tuple-element.14), channel_id=1, source_target_pairs={{0,4},{4,8},{8,12},{12,0},{1,5},{5,9},{9,13},{13,1},{2,6},{6,10},{... | collective-permute-start | bytes 3145736 | tf_op jit(solution)/shard_map/move_weight/ppermute | solution.py:213
  95.5 43.4 %collective-permute-start.4 = (bf16[1024,512]{1,0:T(8,128)(2,1)}, bf16[1024,512]{1,0:T(8,128)(2,1)}, u32[]{:S(2)}, u32[]{:S(2)}) collective-permute-start(bf16[1024,512]{1,0:T(8,128)(2,1)} %get-tuple-element.16), channel_id=1, source_target_pairs={{0,8},{4,12},{8,0},{12,4},{1,9},{5,13},{9,1},{13,5},{2,10},{6,14},... | collective-permute-start | bytes 3145736 | tf_op jit(solution)/shard_map/move_weight/ppermute | solution.py:213
  107.8 31.2 %all-to-all-start.3 = ((bf16[8,64,1024]{2,1,0:T(8,128)(2,1)}), bf16[8,64,1024]{2,1,0:T(8,128)(2,1)S(1)}, u32[]{:S(2)}, u32[]{:S(2)}) async-start(bf16[8,64,1024]{2,1,0:T(8,128)(2,1)} %settle.1), calls=%async_computation.3 | async-start | bytes 2097152 | tf_op jit(solution)/shard_map/move_attended/all_to_all | solution.py:209

commit v2 on v1

--- a/solution.py
+++ b/solution.py
@@ -16,6 +16,7 @@
 LOG2_SCALE = math.log2(math.e) / math.sqrt(HD)
 F32 = jnp.float32
 BF16 = jnp.bfloat16
+TINY = pl.CostEstimate(flops=1, bytes_accessed=1, transcendentals=0)
 VMEM = pl.BlockSpec(memory_space=pltpu.VMEM)
 SMEM = pl.BlockSpec(memory_space=pltpu.SMEM)
 
@@ -38,7 +39,7 @@
     for s in range(slots):
         counts = jnp.where(lane_id == s, live[s].astype(F32), counts)
     for k, out in enumerate(outs):
-        head = lax.rem(place[0] + k, 4) // 2
+        head = lax.rem(place[0] + k, 2)
         cols = pl.ds(pl.multiple_of(head * HD, HD), HD)
         for s in range(slots):
             part = pl.ds(s * SPAN, SPAN)
@@ -53,11 +54,12 @@
         out[1, rows + fresh :, :] = counts.astype(BF16)
 
 
-def attend_kernel(live, queries, kv0, kv1, kv2, kv3, pos_q, pos_n, out, kc, vc, kn, vn, scores, fresh_scores, peak, top, acc):
-    sources = (kv0, kv1, kv2, kv3)
-    slots = live.shape[0] // len(sources)
+def attend_kernel(live, here, queries, *refs):
+    near, far = refs[:4], refs[4:8]
+    pos_q, pos_n, out, kc, vc, kn, vn, scores, fresh_scores, peak, top, acc = refs[8:]
+    slots = live.shape[0] // len(near)
     rows = slots * SPAN
-    fresh = pos_n.shape[1] // len(sources) // 2
+    fresh = pos_n.shape[1] // len(near) // 2
     heads = queries.shape[1] // HD
     tokens = queries.shape[0]
     row_id = lax.broadcasted_iota(jnp.int32, (SPAN, HD), 0)
@@ -65,21 +67,32 @@
     kn[...] = jnp.zeros_like(kn)
     vn[:, :HD] = jnp.zeros((vn.shape[0], HD), BF16)
     vn[:, HD:] = jnp.ones((vn.shape[0], HD), BF16)
-    place = jnp.int32(0)
-    for i, kv in enumerate(sources):
-        kn[i * fresh : (i + 1) * fresh, :] = kv[0, rows : rows + fresh, :]
-        vn[i * fresh : (i + 1) * fresh, :HD] = kv[1, rows : rows + fresh, :]
-
-        def gather_slot(s, at, kv=kv, i=i):
-            count = live[i * slots + s]
-            source = pl.ds(pl.multiple_of(s * SPAN, SPAN), SPAN)
-            target = pl.ds(pl.multiple_of(at, 16), SPAN)
-            kc[target, :] = kv[0, source, :]
-            vc[target, :HD] = kv[1, source, :]
-            vc[target, HD:] = jnp.where(row_id < count, 1.0, 0.0).astype(BF16)
-            return at + ((count + 15) // 16) * 16
-
-        place = lax.fori_loop(0, slots, gather_slot, place)
+    def collect(sources):
+        place = jnp.int32(0)
+        for i, kv in enumerate(sources):
+            kn[i * fresh : (i + 1) * fresh, :] = kv[0, rows : rows + fresh, :]
+            vn[i * fresh : (i + 1) * fresh, :HD] = kv[1, rows : rows + fresh, :]
+
+            def gather_slot(s, at, kv=kv, i=i):
+                count = live[i * slots + s]
+                source = pl.ds(pl.multiple_of(s * SPAN, SPAN), SPAN)
+                target = pl.ds(pl.multiple_of(at, 16), SPAN)
+                kc[target, :] = kv[0, source, :]
+                vc[target, :HD] = kv[1, source, :]
+                vc[target, HD:] = jnp.where(row_id < count, 1.0, 0.0).astype(BF16)
+                return at + ((count + 15) // 16) * 16
+
+            place = lax.fori_loop(0, slots, gather_slot, place)
+
+    @pl.when(here[0] == 1)
+    def _():
+        collect(near)
+
+    @pl.when(here[0] != 1)
+    def _():
+        collect(far)
+
+    place = lax.fori_loop(0, live.shape[0], lambda s, at: at + ((live[s] + 15) // 16) * 16, jnp.int32(0))
     tail = pl.ds(pl.multiple_of(place, 16), KEY_BLOCK)
     spare = kc[:16, :].astype(F32)[:1]
     kc[tail, :] = jnp.broadcast_to(spare, (KEY_BLOCK, HD)).astype(BF16)
@@ -198,11 +211,14 @@
 
 
 def project_kernel(place, attended, w0, w1, w2, w3, out):
+    size = out.shape[2]
+    picked = [pl.ds(pl.multiple_of((2 * r + place[1]) * size, size), size) for r in range(out.shape[1])]
+    rows = jnp.concatenate([attended[p, :] for p in picked], axis=0)
     for k, w in enumerate((w0, w1, w2, w3)):
         target = lax.rem(place[0] + 4 - k, 4)
+        term = jnp.dot(rows, w[...], preferred_element_type=F32).astype(BF16)
         for r in range(out.shape[1]):
-            rows = slice(r * out.shape[2], (r + 1) * out.shape[2])
-            out[target, r] = jnp.dot(attended[rows, :], w[...], preferred_element_type=F32).astype(BF16)
+            out[target, r] = term[r * size : (r + 1) * size]
 
 
 def swap(x, axes):
@@ -211,6 +227,19 @@
 
 def along_y(x, distance):
     return lax.ppermute(x, "y", [(i, (i + distance) % 4) for i in range(4)])
+
+
+def to_other_core(x):
+    return lax.ppermute(x, "core", [(0, 1), (1, 0)])
+
+
+def to_chip(x, distance):
+    targets = [((i + distance) % 4) for i in range(4)]
+    return lax.ppermute(x, ("y", "core"), [(i * 2 + t // 2, t * 2 + t // 2) for i, t in enumerate(targets)])
+
+
+def to_sibling(x):
+    return lax.ppermute(x, ("y", "core"), [(t * 2 + t // 2, t * 2 + 1 - t // 2) for t in range(4)])
 
 
 def shards(
@@ -225,15 +254,26 @@
     offset,
     out_weight,
 ):
-    y = lax.axis_index("y")
+    y, core = lax.axis_index("y"), lax.axis_index("core")
     group = lax.axis_index("z") * 2 + lax.axis_index("x_hi")
     place = y[None].astype(jnp.int32)
+    here = (y // 2 == core).astype(jnp.int32)[None]
     groups = 8
     fresh, width = queries.shape
     slots = span_ids.shape[0]
     rows = slots * SPAN
     quarter = width // 4
     tokens = pos_ids.shape[0]
+
+    def on_core(mine, other):
+        return jnp.where(core == 0, jnp.stack([mine, other]), jnp.stack([other, mine]))
+
+    with jax.named_scope("move_queries"):
+        halves = queries.reshape(fresh, 2, 2, quarter).transpose(2, 1, 0, 3)
+        other = to_other_core(lax.dynamic_index_in_dim(halves, 1 - core, 0, False))
+        mine = on_core(lax.dynamic_index_in_dim(halves, core, 0, False), other)
+        mine = jnp.broadcast_to(mine.reshape(1, 4, fresh, quarter), (groups, 4, fresh, quarter))
+        mine = swap(mine.reshape(groups * 4, fresh, quarter), ("z", "x_hi", "y")).reshape(tokens, quarter)
 
     live = jnp.clip(jnp.minimum(valid_len, offset[0] - span_ids * SPAN), 0, SPAN)
     packet = jax.ShapeDtypeStruct((2, rows + fresh + 16, HD), BF16)
@@ -244,18 +284,18 @@
             in_specs=[SMEM, SMEM] + [VMEM] * 4,
             out_specs=[VMEM] * 4,
             compiler_params=grant(24),
-            cost_estimate=pl.CostEstimate(flops=0, bytes_accessed=4 << 20, transcendentals=0),
+            cost_estimate=TINY,
         )(place, live, cache_keys, cache_values, new_keys, new_values)
     with jax.named_scope("move_kv"):
-        kv = [packets[0]] + [along_y(packets[k], k) for k in range(1, 4)]
-
-    with jax.named_scope("move_queries"):
-        mine = swap(queries.reshape(fresh, 4, quarter).transpose(1, 0, 2), "y")
-        mine = mine.reshape(4 * fresh, quarter)
-        mine = swap(jnp.broadcast_to(mine[None], (groups,) + mine.shape), ("z", "x_hi"))
-        mine = mine.reshape(tokens, quarter)
-
-    lives = [live] + [kv[k][0, rows + fresh, :slots].astype(jnp.int32) for k in range(1, 4)]
+        near = [packets[0]] + [to_chip(packets[k], k) for k in range(1, 4)]
+        near, mine = lax.optimization_barrier((near, mine))
+        far = [to_sibling(p) for p in near]
+
+    def counts(k):
+        row = jnp.where(here[0] == 1, near[k][0, rows + fresh, :slots], far[k][0, rows + fresh, :slots])
+        return row.astype(jnp.int32)
+
+    lives = [counts(k) for k in range(4)]
     pos_n = [
         lax.dynamic_slice_in_dim(pos_ids, (group * 4 + lax.rem(y + 4 - k, 4)) * fresh, fresh) for k in range(4)
     ]
@@ -264,11 +304,18 @@
     all_live = jnp.concatenate(lives)
 
     with jax.named_scope("move_weight"):
-        late = jnp.minimum(sum(l[0] for l in lives), 0)
-        weights = [lax.dynamic_slice_in_dim(out_weight, y * quarter, quarter)]
-        for k in range(1, 4):
-            first = lax.rem(y + k, 4) * quarter + late
-            weights.append(along_y(lax.dynamic_slice_in_dim(out_weight, first, quarter), k))
+        halves = out_weight.reshape(2, 2, quarter, out_weight.shape[1])
+        other = to_other_core(lax.dynamic_index_in_dim(halves, 1 - core, 1, False))
+
+        def chunk(k):
+            chip = lax.rem(y + k, 4)
+            own = lax.dynamic_slice(halves, (chip % 2, core, 0, 0), (1, 1) + halves.shape[2:])[0, 0]
+            return jnp.where(chip // 2 == core, own, lax.dynamic_index_in_dim(other, chip % 2, 0, False))
+
+        chunks = [chunk(k) for k in range(4)]
+        late, _ = lax.optimization_barrier((chunks[1:], near[1:]))
+        weights = [chunks[0]] + [along_y(late[k - 1], k) for k in range(1, 4)]
+        mine, _ = lax.optimization_barrier((mine, late))
 
     capacity = 4 * rows + KEY_BLOCK
     most_blocks = -(-4 * rows // KEY_BLOCK)
@@ -277,7 +324,7 @@
         partial = pl.pallas_call(
             attend_kernel,
             out_shape=jax.ShapeDtypeStruct((tokens, quarter + HD), BF16),
-            in_specs=[SMEM] + [VMEM] * 7,
+            in_specs=[SMEM, SMEM] + [VMEM] * 11,
             out_specs=VMEM,
             scratch_shapes=[
                 pltpu.VMEM((capacity, HD), BF16),
@@ -291,10 +338,8 @@
                 pltpu.VMEM((tokens, 2 * HD), F32),
             ],
             compiler_params=grant(40),
-            cost_estimate=pl.CostEstimate(
-                flops=8 * tokens * quarter * rows, bytes_accessed=5 << 20, transcendentals=tokens * heads * rows * 2
-            ),
-        )(all_live, mine, *kv, pos_q, pos_n)
+            cost_estimate=TINY,
+        )(all_live, here, mine, *near, *far, pos_q, pos_n)
 
     with jax.named_scope("move_partials"):
         partial = swap(partial.reshape(groups, tokens // groups, quarter + HD), ("z", "x_hi"))
@@ -305,25 +350,28 @@
             in_specs=[VMEM],
             out_specs=VMEM,
             compiler_params=grant(24),
-            cost_estimate=pl.CostEstimate(flops=1 << 22, bytes_accessed=2 << 20, transcendentals=0),
+            cost_estimate=TINY,
         )(partial)
     with jax.named_scope("move_attended"):
         attended = swap(attended, ("z", "x_hi")).reshape(tokens, quarter)
 
-    with jax.named_scope("project"):
-        columns = out_weight.shape[1]
-        terms = pl.pallas_call(
+    columns = out_weight.shape[1]
+
+    def project(which):
+        return pl.pallas_call(
             project_kernel,
-            out_shape=jax.ShapeDtypeStruct((4, 4, tokens // 4, columns), BF16),
+            out_shape=jax.ShapeDtypeStruct((4, 2, tokens // 4, columns), BF16),
             in_specs=[SMEM] + [VMEM] * 5,
             out_specs=VMEM,
             compiler_params=grant(32),
-            cost_estimate=pl.CostEstimate(
-                flops=8 * tokens * quarter * columns, bytes_accessed=7 << 20, transcendentals=0
-            ),
-        )(place, attended, *weights)
+            cost_estimate=TINY,
+        )(jnp.stack([y, which]).astype(jnp.int32), attended, *weights)
+
+    with jax.named_scope("project"):
+        theirs = to_other_core(project(1 - core))
+        terms = (project(core).astype(F32) + theirs.astype(F32)).astype(BF16)
     with jax.named_scope("move_terms"):
-        terms = swap(terms.reshape(16, tokens // 4, columns), ("y", "x_lo", "core"))
+        terms = swap(terms.reshape(8, tokens // 4, columns), ("y", "x_lo"))
     return jnp.sum(terms.astype(F32), axis=0).astype(BF16)
 
 

time: 180 us -> 171 us (0.950)
  blocking collectives: 58.6 us -> 19 us
  starting transfers between devices: 22.4 us -> 40.3 us
  other arithmetic: 2.41 us -> 10 us
  Pallas kernels: 33.6 us -> 38 us
  waiting for transfers between devices: 50.5 us -> 54.8 us
  local copies, waits for them, and re-layouts: 10.2 us -> 7.04 us
    all_to_all x2 -> x1, blocking collectives: 58.6 us -> 19 us  [swap(): return lax.all_to_all(x, axes, split_axis=0, concat_axis=0, tiled=False)]
    ppermute x0 -> x10, starting transfers between devices: none -> 18.8 us  [the longest x3 9.86 us: to_chip(): lax.ppermute(x, ('y', 'core'), [(i * 2 + t // 2, t * 2 + t // 2) for i, t...]
    ppermute x0 -> x10, waiting for transfers between devices: none -> 16 us  [the longest x3 9.43 us: to_chip(): lax.ppermute(x, ('y', 'core'), [(i * 2 + t // 2, t * 2 + t // 2) for i, t...]
    ppermute x6 -> x3, waiting for transfers between devices: 38.9 us -> 24.5 us  [along_y(): return lax.ppermute(x, 'y', [(i, (i + distance) % 4) for i in range(4)])]
    select_n x0 -> x2, other arithmetic: none -> 5.95 us  [the longest x1 5.36 us: chunk(): jnp.where(chip // 2 == core, own, lax.dynamic_index_in_dim(other, chip %...]
    pallas_call x1, Pallas kernels: 25.5 us -> 30.1 us  [shards(): pl.pallas_call(attend_kernel, out_shape=jax.ShapeDtypeStruct((tokens, qua...]
    dynamic_slice x1 -> x2, local copies, waits for them, and re-layouts: 4.26 us -> 0.32 us  [the longest x1 0.28 us: shards(): mine = on_core(lax.dynamic_index_in_dim(halves, core, 0, False), other)]
    squeeze x0 -> x1, local copies, waits for them, and re-layouts: none -> 3.11 us  [shards(): other = to_other_core(lax.dynamic_index_in_dim(halves, 1 - core, 1, False))]
  transfers between devices with their start and end apart: 9 -> 16, of which waited for: 6 -> 11; matrix products, arithmetic and copies ran while one was open for 4% -> 4% of each run, Pallas kernels for 1% -> 3%
where the time goes in v2:
time: 171 us; the launch traced here: 170 us
  waiting for transfers between devices  54.8 us (32%)
  starting transfers between devices  40.3 us (24%)
  Pallas kernels  38 us (22%)
  blocking collectives  19 us (11%)
  other arithmetic  10 us (6%)
  local copies, waits for them, and re-layouts  7.04 us (4%)
    pallas_call x1, Pallas kernels, shards(): pl.pallas_call(attend_kernel, out_shape=jax.ShapeDtypeStruct((tokens, qua...  30.1 us
    ppermute x3, waiting for transfers between devices, along_y(): return lax.ppermute(x, 'y', [(i, (i + distance) % 4) for i in range(4)])  24.5 us
    all_to_all x1, blocking collectives, swap(): return lax.all_to_all(x, axes, split_axis=0, concat_axis=0, tiled=False)  19 us
    all_to_all x3, starting transfers between devices, swap(): return lax.all_to_all(x, axes, split_axis=0, concat_axis=0, tiled=False)  17.7 us
    all_to_all x3, waiting for transfers between devices, swap(): return lax.all_to_all(x, axes, split_axis=0, concat_axis=0, tiled=False)  14.4 us
    ppermute x3, starting transfers between devices, to_chip(): lax.ppermute(x, ('y', 'core'), [(i * 2 + t // 2, t * 2 + t // 2) for i, t...  9.86 us
    ppermute x3, waiting for transfers between devices, to_chip(): lax.ppermute(x, ('y', 'core'), [(i * 2 + t // 2, t * 2 + t // 2) for i, t...  9.43 us
    ppermute x4, waiting for transfers between devices, to_sibling(): lax.ppermute(x, ('y', 'core'), [(t * 2 + t // 2, t * 2 + 1 - t // 2) for...  5.61 us
  transfers between devices with their start and end apart: 16, of which 11 were waited for; matrix products, arithmetic and copies ran while one was open for 4% of the time, Pallas kernels for 3%

profile of v2, /device:TPU:1, one launch (start us, length us, event | category | flops | bytes accessed | tf_op | source)
XLA Modules:
  0.0 170.4 jit_solution(16939405084690690857)
XLA Ops:
  0.0 1.0 reshape.49
  1.0 0.3 dynamic-slice_bitcast_fusion.2
  1.3 1.5 collective-permute-start.3
  2.8 0.9 collective-permute-done.3
  3.7 0.1 copy.18
  3.8 0.6 broadcast_select_fusion
  4.5 1.1 broadcast_in_dim.18
  5.6 10.6 %all-to-all-start = ((bf16[32,16,1024]{2,1,0:T(8,128)(2,1)}), bf16[32,16,1024]{2,1,0:T(8,128)(2,1)S(1)}, u32[]{:S(2)}, u32[]{:S(2)}) async-start(bf16[32,16,1024]{2,1,0:T(8,128)(2,1)} %bitcast.8), calls=%async_computation | async-start | bytes 2097152 | tf_op jit(solution)/shard_map/move_queries/all_to_all | solution.py:225
  16.3 3.1 %dynamic-slice_bitcast_fusion = bf16[2,1024,512]{2,1,0:T(8,128)(2,1)} fusion(bf16[2,2,1024,512]{3,2,1,0:T(8,128)(2,1)} %bitcast.53, s32[]{:T(128)S(6)} %select_n.154), kind=kLoop, calls=%fused_computation.1 | loop fusion | bytes 4194308 | tf_op jit(solution)/shard_map/move_weight/jit(dynamic_index_in_dim)/squeeze | solution.py:308
  19.4 0.6 collective-permute-start.8
  20.8 1.0 pack.1
  21.8 0.7 collective-permute-start
  22.5 7.1 %collective-permute-start.1 = (bf16[2,1056,128]{2,1,0:T(8,128)(2,1)S(1)}, bf16[2,1056,128]{2,1,0:T(8,128)(2,1)S(1)}, u32[]{:S(2)}, u32[]{:S(2)}) collective-permute-start(bf16[2,1056,128]{2,1,0:T(8,128)(2,1)S(1)} %get-tuple-element.20), channel_id=1, source_target_pairs={{1,9},{5,13},{8,0},{12,4},{3,11},{7,15},{10,2},{14,6},{17,25},{21,... | collective-permute-start | bytes 1622024 | tf_op jit(solution)/shard_map/move_kv/ppermute | solution.py:238
  29.5 2.1 %collective-permute-start.2 = (bf16[2,1056,128]{2,1,0:T(8,128)(2,1)S(1)}, bf16[2,1056,128]{2,1,0:T(8,128)(2,1)}, u32[]{:S(2)}, u32[]{:S(2)}) collective-permute-start(bf16[2,1056,128]{2,1,0:T(8,128)(2,1)S(1)} %get-tuple-element.21), channel_id=1, source_target_pairs={{1,13},{4,0},{8,4},{13,9},{3,15},{6,2},{10,6},{15,11},{17,29},{20,... | collective-permute-start | bytes 1622024 | tf_op jit(solution)/shard_map/move_kv/ppermute | solution.py:238
  31.6 8.2 %collective-permute-done.1.refs_2_ = bf16[2,1056,128]{2,1,0:T(8,128)(2,1)S(1)} collective-permute-done((bf16[2,1056,128]{2,1,0:T(8,128)(2,1)S(1)}, bf16[2,1056,128]{2,1,0:T(8,128)(2,1)S(1)}, u32[]{:S(2)}, u32[]{:S(2)}) %collective-permute-start.1) | collective-permute-done | bytes 540704 | tf_op jit(solution)/shard_map/move_kv/ppermute | solution.py:238
  39.8 1.2 collective-permute-done.2.refs_3_
  41.1 1.3 collective-permute-start.4
  42.4 1.3 collective-permute-start.5
  43.9 0.1 copy.21.refs_8_
  44.1 1.3 collective-permute-start.6
  45.5 1.3 collective-permute-start.7
  46.8 0.9 collective-permute-done.4.refs_4_
  47.7 0.7 fusion
  48.4 1.4 collective-permute-done.5.refs_5_
  49.8 0.7 fusion.1
  50.5 1.6 collective-permute-done.6.refs_6_
  52.1 0.7 fusion.2
  52.8 1.7 collective-permute-done.7.refs_7_
  54.4 0.7 fusion.3
  55.2 5.4 %bitcast_select_fusion = (bf16[1024,512]{1,0:T(8,128)(2,1)S(1)}, bf16[1024,512]{1,0:T(8,128)(2,1)}, bf16[1024,512]{1,0:T(8,128)(2,1)}, bf16[1024,512]{1,0:T(8,128)(2,1)}) fusion(bf16[2,1024,512]{2,1,0:T(8,128)(2,1)} %collective-permute-done.8, s32[]{:T(128)S(6)} %select_n.183, bf16[2,2,1024,512]{3,2,1,0:T(8,128)(2,1)} %bitcast.54, s32[]{:T(128)S(6)} %select_n.153, ...), kind=kLoop, calls=%fused_computation.2 | loop fusion | flops 2097152 | bytes 12582936 | tf_op jit(solution)/shard_map/move_weight/jit(_where)/select_n | solution.py:313
  60.6 30.1 %attend.1 = bf16[512,1152]{1,0:T(8,128)(2,1)} custom-call(s32[32]{0:T(128)S(1)} %maximum_convert_fusion.live, s32[1]{0:T(128)} %bitcast.14.here, bf16[512,1024]{1,0:T(8,128)(2,1)S(1)} %bitcast.51, bf16[2,1056,128]{2,1,0:T(8,128)(2,1)S(1)} %get-tuple-element.22.refs_0_, bf16[2,1056,128]{2,1,0:T(8,128)(2,1)S(1)} %collective-permute-done.refs_1_, ...), custom_call_target="tpu_custom_call" | custom-call | flops 1 | bytes 1 | tf_op jit(solution)/shard_map/attend/pallas_call | solution.py:324
  90.7 3.6 %all-to-all-start.1 = ((bf16[8,64,1152]{2,1,0:T(8,128)(2,1)}), bf16[8,64,1152]{2,1,0:T(8,128)(2,1)S(1)}, u32[]{:S(2)}, u32[]{:S(2)}) async-start(bf16[8,64,1152]{2,1,0:T(8,128)(2,1)} %bitcast.25), calls=%async_computation.1 | async-start | bytes 2359296 | tf_op jit(solution)/shard_map/move_partials/all_to_all | solution.py:225
  94.3 1.2 collective-permute-start.9
  95.4 0.7 collective-permute-start.10
  96.1 2.0 %collective-permute-start.11 = (bf16[1024,512]{1,0:T(8,128)(2,1)}, bf16[1024,512]{1,0:T(8,128)(2,1)}, u32[]{:S(2)}, u32[]{:S(2)}) collective-permute-start(bf16[1024,512]{1,0:T(8,128)(2,1)} %get-tuple-element.29), channel_id=1, source_target_pairs={{0,12},{4,0},{8,4},{12,8},{1,13},{5,1},{9,5},{13,9},{2,14},{6,2},{... | collective-permute-start | bytes 3145736 | tf_op jit(solution)/shard_map/move_weight/ppermute | solution.py:229
  98.1 14.3 %all-to-all-done.1.parts = bf16[8,64,1152]{2,1,0:T(8,128)(2,1)S(1)} async-done(((bf16[8,64,1152]{2,1,0:T(8,128)(2,1)}), bf16[8,64,1152]{2,1,0:T(8,128)(2,1)S(1)}, u32[]{:S(2)}, u32[]{:S(2)}) %all-to-all-start.1) | async-done | bytes 1179680 | tf_op jit(solution)/shard_map/move_partials/all_to_all | solution.py:225
  112.4 1.4 settle.1
  113.8 1.0 copy-done
  114.8 3.6 %all-to-all-start.2 = ((bf16[8,64,1024]{2,1,0:T(8,128)(2,1)}), bf16[8,64,1024]{2,1,0:T(8,128)(2,1)S(1)}, u32[]{:S(2)}, u32[]{:S(2)}) async-start(bf16[8,64,1024]{2,1,0:T(8,128)(2,1)} %copy-done), calls=%async_computation.2 | async-start | bytes 2097152 | tf_op jit(solution)/shard_map/move_attended/all_to_all | solution.py:225
  118.4 2.1 %collective-permute-done.9.w1 = bf16[1024,512]{1,0:T(8,128)(2,1)S(1)} collective-permute-done((bf16[1024,512]{1,0:T(8,128)(2,1)}, bf16[1024,512]{1,0:T(8,128)(2,1)S(1)}, u32[]{:S(2)}, u32[]{:S(2)}) %collective-permute-start.9) | collective-permute-done | bytes 1048608 | tf_op jit(solution)/shard_map/move_weight/ppermute | solution.py:229
  120.5 21.6 %collective-permute-done.10.w2 = bf16[1024,512]{1,0:T(8,128)(2,1)} collective-permute-done((bf16[1024,512]{1,0:T(8,128)(2,1)}, bf16[1024,512]{1,0:T(8,128)(2,1)}, u32[]{:S(2)}, u32[]{:S(2)}) %collective-permute-start.10) | collective-permute-done | bytes 1048608 | tf_op jit(solution)/shard_map/move_weight/ppermute | solution.py:229
  142.1 0.8 collective-permute-done.11.w3
  143.0 2.8 %project.3 = bf16[4,2,128,512]{3,2,1,0:T(8,128)(2,1)S(1)} custom-call(s32[2]{0:T(128)S(1)} %pad_add_fusion.1.place, bf16[512,1024]{1,0:T(8,128)(2,1)S(1)} %bitcast.49, bf16[1024,512]{1,0:T(8,128)(2,1)S(1)} %get-tuple-element.31.w0, bf16[1024,512]{1,0:T(8,128)(2,1)S(1)} %collective-permute-done.9.w1, bf16[1024,512]{1,0:T(8,128)(2,1)} %collective-permute-done.10.w2, ...), custom_call_target="tpu_custom_call" | custom-call | flops 1 | bytes 1 | tf_op jit(solution)/shard_map/project/pallas_call | solution.py:361
  145.8 1.6 collective-permute-start.12
  147.5 2.8 %project.2 = bf16[4,2,128,512]{3,2,1,0:T(8,128)(2,1)S(1)} custom-call(s32[2]{0:T(128)S(1)} %pad_add_fusion.place, bf16[512,1024]{1,0:T(8,128)(2,1)S(1)} %bitcast.50, bf16[1024,512]{1,0:T(8,128)(2,1)S(1)} %get-tuple-element.31.w0, bf16[1024,512]{1,0:T(8,128)(2,1)S(1)} %collective-permute-done.9.w1, bf16[1024,512]{1,0:T(8,128)(2,1)} %collective-permute-done.10.w2, ...), custom_call_target="tpu_custom_call" | custom-call | flops 1 | bytes 1 | tf_op jit(solution)/shard_map/project/pallas_call | solution.py:361
  150.3 0.3 add_convert_fusion
  150.6 19.0 %all_to_all.20 = bf16[8,128,512]{2,1,0:T(8,128)(2,1)S(1)} all-to-all(bf16[8,128,512]{2,1,0:T(8,128)(2,1)S(1)} %bitcast.55), channel_id=1, replica_groups=mesh['z'=4,'x_hi'=2,'y'=4,'x_lo'=2,'core'=2] {'y','x_lo'}, dimensions={0} | all-to-all | bytes 2097152 | tf_op jit(solution)/shard_map/move_terms/all_to_all | solution.py:225
  169.6 0.8 reduce_sum.12
  (33 shorter events, 0.6 us)
Async XLA Ops:
  1.3 2.4 %collective-permute-start.3 = (bf16[2,16,1024]{2,1,0:T(8,128)(2,1)S(1)}, bf16[2,16,1024]{2,1,0:T(8,128)(2,1)S(1)}, u32[]{:S(2)}, u32[]{:S(2)}) collective-permute-start(bf16[2,16,1024]{2,1,0:T(8,128)(2,1)S(1)} %bitcast.57), channel_id=1, source_target_pairs={{0,1},{1,0},{2,3},{3,2},{4,5},{5,4},{6,7},{7,6},{8,9},{9,8},{10,11... | collective-permute-start | bytes 196616 | tf_op jit(solution)/shard_map/move_queries/ppermute | solution.py:233
  5.6 35.5 %all-to-all-start = ((bf16[32,16,1024]{2,1,0:T(8,128)(2,1)}), bf16[32,16,1024]{2,1,0:T(8,128)(2,1)S(1)}, u32[]{:S(2)}, u32[]{:S(2)}) async-start(bf16[32,16,1024]{2,1,0:T(8,128)(2,1)} %bitcast.8), calls=%async_computation | async-start | bytes 2097152 | tf_op jit(solution)/shard_map/move_queries/all_to_all | solution.py:225
  16.2 4.5 %copy-start.8 = (s32[8]{0:T(128)S(1)}, s32[8]{0:T(128)}, u32[]{:S(2)}) copy-start(s32[8]{0:T(128)} %param.16) | copy-start | bytes 100
  16.2 4.5 %copy-start.9 = (s32[8]{0:T(128)S(1)}, s32[8]{0:T(128)}, u32[]{:S(2)}) copy-start(s32[8]{0:T(128)} %param.15) | copy-start | bytes 100
  16.2 4.5 %copy-start.3 = (bf16[1024,256]{1,0:T(8,128)(2,1)S(1)}, bf16[1024,256]{1,0:T(8,128)(2,1)}, u32[]{:S(2)}) copy-start(bf16[1024,256]{1,0:T(8,128)(2,1)} %keys.1) | copy-start | bytes 1572868
  16.3 4.5 %copy-start.4 = (bf16[1024,256]{1,0:T(8,128)(2,1)S(1)}, bf16[1024,256]{1,0:T(8,128)(2,1)}, u32[]{:S(2)}) copy-start(bf16[1024,256]{1,0:T(8,128)(2,1)} %values.1) | copy-start | bytes 1572868
  16.3 4.5 %copy-start.5 = (bf16[16,256]{1,0:T(8,128)(2,1)S(1)}, bf16[16,256]{1,0:T(8,128)(2,1)}, u32[]{:S(2)}) copy-start(bf16[16,256]{1,0:T(8,128)(2,1)} %new_keys.1) | copy-start | bytes 24580
  16.3 4.5 %copy-start.6 = (bf16[16,256]{1,0:T(8,128)(2,1)S(1)}, bf16[16,256]{1,0:T(8,128)(2,1)}, u32[]{:S(2)}) copy-start(bf16[16,256]{1,0:T(8,128)(2,1)} %new_values.1) | copy-start | bytes 24580
  16.3 27.6 %copy-start.7 = (s32[512]{0:T(512)S(1)}, s32[512]{0:T(512)}, u32[]{:S(2)}) copy-start(s32[512]{0:T(512)} %param.17) | copy-start | bytes 6148
  19.4 35.8 %collective-permute-start.8 = (bf16[2,1024,512]{2,1,0:T(8,128)(2,1)}, bf16[2,1024,512]{2,1,0:T(8,128)(2,1)}, u32[]{:S(2)}, u32[]{:S(2)}) collective-permute-start(bf16[2,1024,512]{2,1,0:T(8,128)(2,1)} %dynamic-slice_bitcast_fusion), channel_id=1, source_target_pairs={{0,1},{1,0},{2,3},{3,2},{4,5},{5,4},{6,7},{7,6},{8,9},{9,8},{10,11... | collective-permute-start | bytes 6291464 | tf_op jit(solution)/shard_map/move_weight/ppermute | solution.py:233
  21.8 9.9 %collective-permute-start = (bf16[2,1056,128]{2,1,0:T(8,128)(2,1)S(1)}, bf16[2,1056,128]{2,1,0:T(8,128)(2,1)S(1)}, u32[]{:S(2)}, u32[]{:S(2)}) collective-permute-start(bf16[2,1056,128]{2,1,0:T(8,128)(2,1)S(1)} %get-tuple-element.19), channel_id=1, source_target_pairs={{0,4},{5,9},{9,13},{12,0},{2,6},{7,11},{11,15},{14,2},{16,20},{21,... | collective-permute-start | bytes 1622024 | tf_op jit(solution)/shard_map/move_kv/ppermute | solution.py:238
  22.5 17.4 %collective-permute-start.1 = (bf16[2,1056,128]{2,1,0:T(8,128)(2,1)S(1)}, bf16[2,1056,128]{2,1,0:T(8,128)(2,1)S(1)}, u32[]{:S(2)}, u32[]{:S(2)}) collective-permute-start(bf16[2,1056,128]{2,1,0:T(8,128)(2,1)S(1)} %get-tuple-element.20), channel_id=1, source_target_pairs={{1,9},{5,13},{8,0},{12,4},{3,11},{7,15},{10,2},{14,6},{17,25},{21,... | collective-permute-start | bytes 1622024 | tf_op jit(solution)/shard_map/move_kv/ppermute | solution.py:238
  29.5 11.6 %collective-permute-start.2 = (bf16[2,1056,128]{2,1,0:T(8,128)(2,1)S(1)}, bf16[2,1056,128]{2,1,0:T(8,128)(2,1)}, u32[]{:S(2)}, u32[]{:S(2)}) collective-permute-start(bf16[2,1056,128]{2,1,0:T(8,128)(2,1)S(1)} %get-tuple-element.21), channel_id=1, source_target_pairs={{1,13},{4,0},{8,4},{13,9},{3,15},{6,2},{10,6},{15,11},{17,29},{20,... | collective-permute-start | bytes 1622024 | tf_op jit(solution)/shard_map/move_kv/ppermute | solution.py:238
  39.8 15.4 %copy-start.1 = (bf16[2,1056,128]{2,1,0:T(8,128)(2,1)}, bf16[2,1056,128]{2,1,0:T(8,128)(2,1)S(1)}, u32[]{:S(2)}) copy-start(bf16[2,1056,128]{2,1,0:T(8,128)(2,1)S(1)} %collective-permute-done.1.refs_2_) | copy-start | bytes 1622020
  41.1 6.6 %collective-permute-start.4 = (bf16[2,1056,128]{2,1,0:T(8,128)(2,1)S(1)}, bf16[2,1056,128]{2,1,0:T(8,128)(2,1)}, u32[]{:S(2)}, u32[]{:S(2)}) collective-permute-start(bf16[2,1056,128]{2,1,0:T(8,128)(2,1)S(1)} %get-tuple-element.22.refs_0_), channel_id=1, source_target_pairs={{0,1},{4,5},{9,8},{13,12},{2,3},{6,7},{11,10},{15,14},{16,17},{20,... | collective-permute-start | bytes 1622024 | tf_op jit(solution)/shard_map/move_kv/ppermute | solution.py:242
  42.4 7.4 %collective-permute-start.5 = (bf16[2,1056,128]{2,1,0:T(8,128)(2,1)S(1)}, bf16[2,1056,128]{2,1,0:T(8,128)(2,1)}, u32[]{:S(2)}, u32[]{:S(2)}) collective-permute-start(bf16[2,1056,128]{2,1,0:T(8,128)(2,1)S(1)} %collective-permute-done.refs_1_), channel_id=1, source_target_pairs={{0,1},{4,5},{9,8},{13,12},{2,3},{6,7},{11,10},{15,14},{16,17},{20,... | collective-permute-start | bytes 1622024 | tf_op jit(solution)/shard_map/move_kv/ppermute | solution.py:242
  44.1 8.1 %collective-permute-start.6 = (bf16[2,1056,128]{2,1,0:T(8,128)(2,1)S(1)}, bf16[2,1056,128]{2,1,0:T(8,128)(2,1)}, u32[]{:S(2)}, u32[]{:S(2)}) collective-permute-start(bf16[2,1056,128]{2,1,0:T(8,128)(2,1)S(1)} %collective-permute-done.1.refs_2_), channel_id=1, source_target_pairs={{0,1},{4,5},{9,8},{13,12},{2,3},{6,7},{11,10},{15,14},{16,17},{20,... | collective-permute-start | bytes 1622024 | tf_op jit(solution)/shard_map/move_kv/ppermute | solution.py:242
  45.5 8.9 %collective-permute-start.7 = (bf16[2,1056,128]{2,1,0:T(8,128)(2,1)}, bf16[2,1056,128]{2,1,0:T(8,128)(2,1)S(1)}, u32[]{:S(2)}, u32[]{:S(2)}) collective-permute-start(bf16[2,1056,128]{2,1,0:T(8,128)(2,1)} %collective-permute-done.2.refs_3_), channel_id=1, source_target_pairs={{0,1},{4,5},{9,8},{13,12},{2,3},{6,7},{11,10},{15,14},{16,17},{20,... | collective-permute-start | bytes 1622024 | tf_op jit(solution)/shard_map/move_kv/ppermute | solution.py:242
  55.2 5.4 %copy-start.2 = (bf16[2,1056,128]{2,1,0:T(8,128)(2,1)S(1)}, bf16[2,1056,128]{2,1,0:T(8,128)(2,1)}, u32[]{:S(2)}) copy-start(bf16[2,1056,128]{2,1,0:T(8,128)(2,1)} %copy-done.1) | copy-start | bytes 1622020
  90.7 21.7 %all-to-all-start.1 = ((bf16[8,64,1152]{2,1,0:T(8,128)(2,1)}), bf16[8,64,1152]{2,1,0:T(8,128)(2,1)S(1)}, u32[]{:S(2)}, u32[]{:S(2)}) async-start(bf16[8,64,1152]{2,1,0:T(8,128)(2,1)} %bitcast.25), calls=%async_computation.1 | async-start | bytes 2359296 | tf_op jit(solution)/shard_map/move_partials/all_to_all | solution.py:225
  94.3 26.2 %collective-permute-start.9 = (bf16[1024,512]{1,0:T(8,128)(2,1)}, bf16[1024,512]{1,0:T(8,128)(2,1)S(1)}, u32[]{:S(2)}, u32[]{:S(2)}) collective-permute-start(bf16[1024,512]{1,0:T(8,128)(2,1)} %get-tuple-element.27), channel_id=1, source_target_pairs={{0,4},{4,8},{8,12},{12,0},{1,5},{5,9},{9,13},{13,1},{2,6},{6,10},{... | collective-permute-start | bytes 3145736 | tf_op jit(solution)/shard_map/move_weight/ppermute | solution.py:229
  95.4 46.7 %collective-permute-start.10 = (bf16[1024,512]{1,0:T(8,128)(2,1)}, bf16[1024,512]{1,0:T(8,128)(2,1)}, u32[]{:S(2)}, u32[]{:S(2)}) collective-permute-start(bf16[1024,512]{1,0:T(8,128)(2,1)} %get-tuple-element.28), channel_id=1, source_target_pairs={{0,8},{4,12},{8,0},{12,4},{1,9},{5,13},{9,1},{13,5},{2,10},{6,14},... | collective-permute-start | bytes 3145736 | tf_op jit(solution)/shard_map/move_weight/ppermute | solution.py:229
  96.1 46.9 %collective-permute-start.11 = (bf16[1024,512]{1,0:T(8,128)(2,1)}, bf16[1024,512]{1,0:T(8,128)(2,1)}, u32[]{:S(2)}, u32[]{:S(2)}) collective-permute-start(bf16[1024,512]{1,0:T(8,128)(2,1)} %get-tuple-element.29), channel_id=1, source_target_pairs={{0,12},{4,0},{8,4},{12,8},{1,13},{5,1},{9,5},{13,9},{2,14},{6,2},{... | collective-permute-start | bytes 3145736 | tf_op jit(solution)/shard_map/move_weight/ppermute | solution.py:229
  113.8 1.0 copy-start
  114.8 28.2 %all-to-all-start.2 = ((bf16[8,64,1024]{2,1,0:T(8,128)(2,1)}), bf16[8,64,1024]{2,1,0:T(8,128)(2,1)S(1)}, u32[]{:S(2)}, u32[]{:S(2)}) async-start(bf16[8,64,1024]{2,1,0:T(8,128)(2,1)} %copy-done), calls=%async_computation.2 | async-start | bytes 2097152 | tf_op jit(solution)/shard_map/move_attended/all_to_all | solution.py:225
  145.8 4.5 %collective-permute-start.12 = (bf16[4,2,128,512]{3,2,1,0:T(8,128)(2,1)S(1)}, bf16[4,2,128,512]{3,2,1,0:T(8,128)(2,1)S(1)}, u32[]{:S(2)}, u32[]{:S(2)}) collective-permute-start(bf16[4,2,128,512]{3,2,1,0:T(8,128)(2,1)S(1)} %project.3), channel_id=1, source_target_pairs={{0,1},{1,0},{2,3},{3,2},{4,5},{5,4},{6,7},{7,6},{8,9},{9,8},{10,11... | collective-permute-start | bytes 3145736 | tf_op jit(solution)/shard_map/project/ppermute | solution.py:233

commit v3 on v2

v3 whole, which is shorter than its diff:
```python
import functools
import math

import jax
import jax.numpy as jnp
import numpy as np
from jax import lax
from jax.experimental import pallas as pl
from jax.experimental.pallas import tpu as pltpu
from jax.sharding import Mesh
from jax.sharding import PartitionSpec as P

HD = 128
SPAN = 128
KEY_BLOCK = 512
FILL = -1e30
LOWEST = -1e20
LOG2_SCALE = math.log2(math.e) / math.sqrt(HD)
F32 = jnp.float32
BF16 = jnp.bfloat16
TINY = pl.CostEstimate(flops=1, bytes_accessed=1, transcendentals=0)
VMEM = pl.BlockSpec(memory_space=pltpu.VMEM)
SMEM = pl.BlockSpec(memory_space=pltpu.SMEM)
ANY = pl.BlockSpec(memory_space=pl.ANY)


def dot_nt(a, b):
    return lax.dot_general(a, b, (((1,), (1,)), ((), ())), preferred_element_type=F32)


def grant(mib):
    return pltpu.CompilerParams(vmem_limit_bytes=mib << 20)


def pack_kernel(place, live, keys_in, values_in, new_keys_in, new_values_in, *refs):
    outs, (keys, values, new_keys, new_values, sems) = refs[:4], refs[4:]
    copies = [
        pltpu.make_async_copy(source, target, sems.at[i])
        for i, (source, target) in enumerate(
            ((keys_in, keys), (values_in, values), (new_keys_in, new_keys), (new_values_in, new_values))
        )
    ]
    for copy in copies:
        copy.start()
    for copy in copies:
        copy.wait()
    slots = live.shape[0]
    rows = slots * SPAN
    fresh = new_keys.shape[0]
    row_id = lax.broadcasted_iota(jnp.int32, (SPAN, HD), 0)
    lane_id = lax.broadcasted_iota(jnp.int32, (16, HD), 1)
    counts = jnp.zeros((16, HD), F32)
    for s in range(slots):
        counts = jnp.where(lane_id == s, live[s].astype(F32), counts)
    for k, out in enumerate(outs):
        head = lax.rem(place[0] + k, 2)
        cols = pl.ds(pl.multiple_of(head * HD, HD), HD)
        for s in range(slots):
            part = pl.ds(s * SPAN, SPAN)
            visible = row_id < live[s]
            key = keys[part, cols].astype(F32)
            key = jnp.where(visible, key, jnp.broadcast_to(key[:1], key.shape))
            out[0, part, :] = key.astype(BF16)
            out[1, part, :] = jnp.where(visible, values[part, cols].astype(F32), 0.0).astype(BF16)
        out[0, rows : rows + fresh, :] = new_keys[:, cols]
        out[1, rows : rows + fresh, :] = new_values[:, cols]
        out[0, rows + fresh :, :] = counts.astype(BF16)
        out[1, rows + fresh :, :] = counts.astype(BF16)


def attend_kernel(live, here, queries, near, far, pos_q, pos_n, out, kc, vc, top, acc):
    slots = live.shape[0] // near.shape[0]
    rows = slots * SPAN
    fresh = near.shape[2] - rows - 16
    heads = queries.shape[1] // HD
    tokens = queries.shape[0]
    row_id = lax.broadcasted_iota(jnp.int32, (SPAN, HD), 0)
    start = near.shape[0] * fresh

    def rounded(count):
        return ((count + 15) // 16) * 16

    def collect(sources):
        place = jnp.int32(start)
        for i in range(sources.shape[0]):
            kv = sources.at[i]
            target = slice(i * fresh, (i + 1) * fresh)
            kc[target, :] = kv[0, rows : rows + fresh, :]
            vc[target, :HD] = kv[1, rows : rows + fresh, :]
            vc[target, HD:] = jnp.ones((fresh, HD), BF16)

            def gather_slot(s, at, kv=kv, i=i):
                count = live[i * slots + s]
                source = pl.ds(pl.multiple_of(s * SPAN, SPAN), SPAN)
                target = pl.ds(pl.multiple_of(at, 16), SPAN)
                kc[target, :] = kv[0, source, :]
                vc[target, :HD] = kv[1, source, :]
                vc[target, HD:] = jnp.where(row_id < count, 1.0, 0.0).astype(BF16)
                return at + rounded(count)

            place = lax.fori_loop(0, slots, gather_slot, place)

    pl.when(here[0] == 1)(functools.partial(collect, near))
    pl.when(here[0] != 1)(functools.partial(collect, far))

    place = lax.fori_loop(0, live.shape[0], lambda s, at: at + rounded(live[s]), jnp.int32(start))
    tail = pl.ds(pl.multiple_of(place, 16), KEY_BLOCK)
    spare = kc[start : start + 16, :].astype(F32)[:1]
    spare = jnp.where(place > start, spare, 0.0)
    kc[tail, :] = jnp.broadcast_to(spare, (KEY_BLOCK, HD)).astype(BF16)
    vc[tail, :] = jnp.zeros((KEY_BLOCK, 2 * HD), BF16)
    blocks = (place + KEY_BLOCK - 1) // KEY_BLOCK

    lane_id = lax.broadcasted_iota(jnp.int32, (tokens, HD), 1)
    key_id = lax.broadcasted_iota(jnp.int32, (1, KEY_BLOCK), 1)
    seen = jnp.where(key_id < place, pos_n[...], tokens) <= pos_q[...]
    lanes = [slice(j * HD, (j + 1) * HD) for j in range(KEY_BLOCK // HD)]

    def head_cols(h):
        return slice(h * HD, (h + 1) * HD)

    def rounded_max(s):
        high = functools.reduce(jnp.maximum, [s[:, g] for g in lanes])
        m = jnp.maximum(jnp.max(high, axis=1, keepdims=True) * LOG2_SCALE, LOWEST)
        return jnp.broadcast_to(m.astype(BF16).astype(F32), (tokens, HD))

    def score(h, part):
        return dot_nt(queries[:, head_cols(h)], kc[part, :])

    def sums(s, m, part):
        p = jnp.concatenate([jnp.exp2(s[:, g] * LOG2_SCALE - m).astype(BF16) for g in lanes], axis=1)
        return jnp.dot(p, vc[part, :], preferred_element_type=F32)

    def begin(h, part, s):
        s = jnp.where(seen, s, FILL)
        m = rounded_max(s)
        top[h] = m
        acc[h] = sums(s, m, part)

    def add(h, part, s):
        old = top[h]
        m = jnp.maximum(old, rounded_max(s))
        top[h] = m
        shrink = jnp.exp2(old - m)
        term = sums(s, m, part)
        acc[h, :, :HD] = acc[h, :, :HD] * shrink + term[:, :HD]
        acc[h, :, HD:] = acc[h, :, HD:] * shrink + term[:, HD:]

    def every_head(visit, part):
        s = score(0, part)
        for h in range(heads):
            following = score(h + 1, part) if h + 1 < heads else None
            visit(h, part, s)
            s = following

    every_head(begin, slice(0, KEY_BLOCK))

    def step(b, _):
        every_head(add, pl.ds(pl.multiple_of(b * KEY_BLOCK, KEY_BLOCK), KEY_BLOCK))
        return _

    lax.fori_loop(1, blocks, step, 0)

    notes = jnp.zeros((tokens, HD), F32)
    for h in range(heads):
        total = acc[h, :, HD:]
        high = total.astype(BF16).astype(F32)
        out[:, head_cols(h)] = acc[h, :, :HD].astype(BF16)
        notes = jnp.where(lane_id == h, top[h], notes)
        notes = jnp.where(lane_id == heads + h, high, notes)
        notes = jnp.where(lane_id == 2 * heads + h, total - high, notes)
    out[:, heads * HD :] = notes.astype(BF16)


def settle_kernel(parts, out):
    groups, tokens, width = parts.shape
    heads = width // HD - 1
    notes = [parts[g, :, heads * HD :].astype(F32) for g in range(groups)]
    highest = notes[0]
    for g in range(1, groups):
        highest = jnp.maximum(highest, notes[g])
    factors = [jnp.exp2(notes[g] - highest) for g in range(groups)]
    for h in range(heads):
        cols = slice(h * HD, (h + 1) * HD)
        numerator = jnp.zeros((tokens, HD), F32)
        total = jnp.zeros((tokens, 1), F32)
        for g in range(groups):
            factor = factors[g][:, h : h + 1]
            numerator += factor * parts[g, :, cols].astype(F32)
            total += factor * (
                notes[g][:, heads + h : heads + h + 1] + notes[g][:, 2 * heads + h : 2 * heads + h + 1]
            )
        attended = (numerator / total).astype(BF16)
        for g in range(groups):
            out[g, :, cols] = attended


def cut_kernel(place, mine, other, *refs):
    outs, held, arrived, left = refs[:8], refs[8], refs[9], refs[10]
    early, late = outs[0].shape[0], outs[1].shape[0]
    pieces = [(i // 2, (i % 2) * early, (early, late)[i % 2]) for i in range(8)]
    pages = [held.at[k, slice(start, start + size), :] for k, start, size in pieces]

    def arrivals(source):
        made = []
        for i, (k, start, size) in enumerate(pieces):
            chip = lax.rem(place[0] + k, 4)
            first = (lax.rem(chip, 2) * 2 + place[1]) * (early + late) + start
            part = pl.ds(pl.multiple_of(first, 16), size)
            made.append((chip // 2 == place[1], pltpu.make_async_copy(source.at[part, :], pages[i], arrived.at[i])))
        return made

    for here, copy in arrivals(mine):
        pl.when(here)(copy.start)
    for here, copy in arrivals(other):
        pl.when(jnp.logical_not(here))(copy.start)
    departures = [pltpu.make_async_copy(pages[i], outs[i], left.at[i]) for i in range(8)]
    for (_, copy), departure in zip(arrivals(mine), departures):
        copy.wait()
        departure.start()
    for departure in departures:
        departure.wait()


def project_kernel(place, attended, *refs):
    out = refs[8]
    size = out.shape[2]
    half = refs[0].shape[0]
    picked = [pl.ds(pl.multiple_of((2 * r + place[1]) * size, size), size) for r in range(out.shape[1])]
    rows = jnp.concatenate([attended[p, :] for p in picked], axis=0)
    for k in range(4):
        target = lax.rem(place[0] + 4 - k, 4)
        term = jnp.dot(rows[:, :half], refs[k][...], preferred_element_type=F32)
        term += jnp.dot(rows[:, half:], refs[4 + k][...], preferred_element_type=F32)
        term = term.astype(BF16)
        for r in range(out.shape[1]):
            out[target, r] = term[r * size : (r + 1) * size]


def swap(x, axes):
    return lax.all_to_all(x, axes, split_axis=0, concat_axis=0, tiled=False)


def along_y(x, distance):
    return lax.ppermute(x, "y", [(i, (i + distance) % 4) for i in range(4)])


def to_other_core(x):
    return lax.ppermute(x, "core", [(0, 1), (1, 0)])


def to_chip(x, distance):
    targets = [((i + distance) % 4) for i in range(4)]
    return lax.ppermute(x, ("y", "core"), [(i * 2 + t // 2, t * 2 + t // 2) for i, t in enumerate(targets)])


def to_sibling(x):
    return lax.ppermute(x, ("y", "core"), [(t * 2 + t // 2, t * 2 + 1 - t // 2) for t in range(4)])


def shards(
    queries,
    new_keys,
    new_values,
    cache_keys,
    cache_values,
    span_ids,
    valid_len,
    pos_ids,
    offset,
    out_weight,
):
    y, core = lax.axis_index("y"), lax.axis_index("core")
    group = lax.axis_index("z") * 2 + lax.axis_index("x_hi")
    place = y[None].astype(jnp.int32)
    here = (y // 2 == core).astype(jnp.int32)[None]
    groups = 8
    fresh, width = queries.shape
    slots = span_ids.shape[0]
    rows = slots * SPAN
    quarter = width // 4
    tokens = pos_ids.shape[0]

    live = jnp.clip(jnp.minimum(valid_len, offset[0] - span_ids * SPAN), 0, SPAN)
    packet = jax.ShapeDtypeStruct((2, rows + fresh + 16, HD), BF16)
    with jax.named_scope("pack"):
        packets = pl.pallas_call(
            pack_kernel,
            out_shape=[packet] * 4,
            in_specs=[SMEM, SMEM] + [ANY] * 4,
            out_specs=[VMEM] * 4,
            scratch_shapes=[
                pltpu.VMEM(cache_keys.shape, BF16),
                pltpu.VMEM(cache_keys.shape, BF16),
                pltpu.VMEM(new_keys.shape, BF16),
                pltpu.VMEM(new_keys.shape, BF16),
                pltpu.SemaphoreType.DMA((4,)),
            ],
            compiler_params=grant(56),
            cost_estimate=TINY,
        )(place, live, cache_keys, cache_values, new_keys, new_values)
    with jax.named_scope("move_queries"):
        halves = queries.reshape(fresh, 2, 2, quarter).transpose(1, 2, 0, 3)
        halves = jnp.broadcast_to(halves[None], (2, 2, 2, fresh, quarter)).reshape(8, fresh, quarter)
        halves = swap(halves, ("y", "core")).reshape(4, 2, fresh, quarter)
        halves, packets = lax.optimization_barrier((halves, packets))
        mine = lax.dynamic_index_in_dim(halves, y // 2, 1, False).reshape(4 * fresh, quarter)
        mine = jnp.broadcast_to(mine[None], (groups,) + mine.shape)
        mine = swap(mine, ("z", "x_hi")).reshape(tokens, quarter)

    with jax.named_scope("move_weight"):
        early = quarter // 2
        chunks = pl.pallas_call(
            cut_kernel,
            out_shape=[
                jax.ShapeDtypeStruct((size, out_weight.shape[1]), BF16) for size in (early, quarter - early) * 4
            ],
            in_specs=[SMEM, ANY, ANY],
            out_specs=[ANY] * 8,
            scratch_shapes=[
                pltpu.VMEM((4, quarter, out_weight.shape[1]), BF16),
                pltpu.SemaphoreType.DMA((8,)),
                pltpu.SemaphoreType.DMA((8,)),
            ],
            compiler_params=grant(56),
            cost_estimate=TINY,
        )(jnp.stack([y, core]).astype(jnp.int32), out_weight, to_other_core(out_weight))
    with jax.named_scope("move_kv"):
        near = [packets[0]] + [to_chip(packets[k], k) for k in range(1, 4)]
    with jax.named_scope("move_weight"):
        late, arrived = lax.optimization_barrier((chunks[2:], near[1:]))
        first = [chunks[0]] + [along_y(late[2 * k - 2], k) for k in range(1, 4)]
        second = [chunks[1]] + [along_y(late[2 * k - 1], k) for k in range(1, 4)]

    with jax.named_scope("move_kv"):
        near = jnp.stack(near)
        near, mine, chunks = lax.optimization_barrier((near, mine, chunks))
        far = to_sibling(near)
        rows_of_counts = jnp.where(here[0] == 1, near[:, 0, rows + fresh, :slots], far[:, 0, rows + fresh, :slots])
        all_live = rows_of_counts.astype(jnp.int32).reshape(-1)

        mine, _ = lax.optimization_barrier((mine, late))

    pos_n = [
        lax.dynamic_slice_in_dim(pos_ids, (group * 4 + lax.rem(y + 4 - k, 4)) * fresh, fresh) for k in range(4)
    ]
    pos_n = jnp.concatenate(pos_n + [jnp.full((KEY_BLOCK - 4 * fresh,), -1, jnp.int32)])[None]
    pos_q = pos_ids[:, None]

    capacity = 4 * (rows + fresh) + KEY_BLOCK
    heads = quarter // HD
    with jax.named_scope("attend"):
        partial = pl.pallas_call(
            attend_kernel,
            out_shape=jax.ShapeDtypeStruct((tokens, quarter + HD), BF16),
            in_specs=[SMEM, SMEM] + [VMEM] * 5,
            out_specs=VMEM,
            scratch_shapes=[
                pltpu.VMEM((capacity, HD), BF16),
                pltpu.VMEM((capacity, 2 * HD), BF16),
                pltpu.VMEM((heads, tokens, HD), F32),
                pltpu.VMEM((heads, tokens, 2 * HD), F32),
            ],
            compiler_params=grant(40),
            cost_estimate=TINY,
        )(all_live, here, mine, near, far, pos_q, pos_n)

    with jax.named_scope("move_partials"):
        partial, first = lax.optimization_barrier((partial, first))
        partial = swap(partial.reshape(groups, tokens // groups, quarter + HD), ("z", "x_hi"))
    with jax.named_scope("settle"):
        attended = pl.pallas_call(
            settle_kernel,
            out_shape=jax.ShapeDtypeStruct((groups, tokens // groups, quarter), BF16),
            in_specs=[VMEM],
            out_specs=VMEM,
            compiler_params=grant(24),
            cost_estimate=TINY,
        )(partial)
    with jax.named_scope("move_attended"):
        attended, second = lax.optimization_barrier((attended, second))
        attended = swap(attended, ("z", "x_hi")).reshape(tokens, quarter)

    columns = out_weight.shape[1]

    def project(which):
        return pl.pallas_call(
            project_kernel,
            out_shape=jax.ShapeDtypeStruct((4, 2, tokens // 4, columns), BF16),
            in_specs=[SMEM] + [VMEM] * 9,
            out_specs=VMEM,
            compiler_params=grant(32),
            cost_estimate=TINY,
        )(jnp.stack([y, which]).astype(jnp.int32), attended, *first, *second)

    with jax.named_scope("project"):
        theirs = to_other_core(project(1 - core))
        terms = (project(core).astype(F32) + theirs.astype(F32)).astype(BF16)
    with jax.named_scope("move_terms"):
        terms = swap(terms.reshape(8, tokens // 4, columns), ("y", "x_lo"))
    return jnp.sum(terms.astype(F32), axis=0).astype(BF16)


def solution(mesh):
    fine = Mesh(mesh.devices.reshape(4, 2, 4, 2, 2), ("z", "x_hi", "y", "x_lo", "core"))
    ctx, head = ("z", "x_hi", "y"), ("x_lo", "core")
    in_specs = (
        P(ctx, head),
        P(ctx, head),
        P(ctx, head),
        P(ctx, head),
        P(ctx, head),
        P(ctx),
        P(ctx),
        P(),
        P(),
        P(head, ctx),
    )
    return jax.shard_map(shards, mesh=fine, in_specs=in_specs, out_specs=P(head, ctx), check_vma=False)
```

time: 171 us -> 158 us (0.924)
  Pallas kernels: 38 us -> 29.1 us
  starting transfers between devices: 40.3 us -> 45.7 us
  other arithmetic: 10 us -> 5.59 us
  local copies, waits for them, and re-layouts: 7.04 us -> 4.3 us
    all_to_all x3 -> x4, waiting for transfers between devices: 14.4 us -> 35.4 us  [swap(): return lax.all_to_all(x, axes, split_axis=0, concat_axis=0, tiled=False)]
    pallas_call x1, Pallas kernels: 30.1 us -> 13.2 us  [shards(): pl.pallas_call(attend_kernel, out_shape=jax.ShapeDtypeStruct((tokens, qua...]
    ppermute x3, waiting for transfers between devices: 9.43 us -> 0.23 us  [to_chip(): lax.ppermute(x, ('y', 'core'), [(i * 2 + t // 2, t * 2 + t // 2) for i, t...]
    ppermute x3 -> x6, waiting for transfers between devices: 24.5 us -> 17.7 us  [along_y(): return lax.ppermute(x, 'y', [(i, (i + distance) % 4) for i in range(4)])]
    ppermute x3 -> x6, starting transfers between devices: 3.82 us -> 9.85 us  [along_y(): return lax.ppermute(x, 'y', [(i, (i + distance) % 4) for i in range(4)])]
    select_n x2 -> x0, other arithmetic: 5.95 us -> none  [the longest x1 5.36 us: chunk(): jnp.where(chip // 2 == core, own, lax.dynamic_index_in_dim(other, chip %...]
    ppermute x4 -> x1, waiting for transfers between devices: 5.61 us -> 0.01 us  [to_sibling(): lax.ppermute(x, ('y', 'core'), [(t * 2 + t // 2, t * 2 + 1 - t // 2) for...]
    pallas_call x0 -> x1, Pallas kernels: none -> 4.51 us  [shards(): pl.pallas_call(cut_kernel, out_shape=[jax.ShapeDtypeStruct((size, out_wei...]
  transfers between devices with their start and end apart: 16 -> 16, of which waited for: 11 -> 8; matrix products, arithmetic and copies ran while one was open for 4% -> 5% of each run, Pallas kernels for 3% -> 17%
where the time goes in v3:
time: 158 us; the launch traced here: 157 us
  waiting for transfers between devices  53.3 us (34%)
  starting transfers between devices  45.7 us (29%)
  Pallas kernels  29.1 us (18%)
  blocking collectives  18.3 us (12%)
  other arithmetic  5.59 us (4%)
  local copies, waits for them, and re-layouts  4.3 us (3%)
    all_to_all x4, waiting for transfers between devices, swap(): return lax.all_to_all(x, axes, split_axis=0, concat_axis=0, tiled=False)  35.4 us
    all_to_all x4, starting transfers between devices, swap(): return lax.all_to_all(x, axes, split_axis=0, concat_axis=0, tiled=False)  20.9 us
    all_to_all x1, blocking collectives, swap(): return lax.all_to_all(x, axes, split_axis=0, concat_axis=0, tiled=False)  18.3 us
    ppermute x6, waiting for transfers between devices, along_y(): return lax.ppermute(x, 'y', [(i, (i + distance) % 4) for i in range(4)])  17.7 us
    pallas_call x1, Pallas kernels, shards(): pl.pallas_call(attend_kernel, out_shape=jax.ShapeDtypeStruct((tokens, qua...  13.2 us
    ppermute x6, starting transfers between devices, along_y(): return lax.ppermute(x, 'y', [(i, (i + distance) % 4) for i in range(4)])  9.85 us
    ppermute x3, starting transfers between devices, to_chip(): lax.ppermute(x, ('y', 'core'), [(i * 2 + t // 2, t * 2 + t // 2) for i, t...  7.93 us
    ppermute x2, starting transfers between devices, to_other_core(): return lax.ppermute(x, 'core', [(0, 1), (1, 0)])  5.65 us
  transfers between devices with their start and end apart: 16, of which 8 were waited for; matrix products, arithmetic and copies ran while one was open for 5% of the time, Pallas kernels for 17%

profile of v3, /device:TPU:1, one launch (start us, length us, event | category | flops | bytes accessed | tf_op | source)
XLA Modules:
  0.0 157.1 jit_solution(6216290360738029080)
XLA Ops:
  0.0 1.4 collective-permute-start.3
  1.4 1.0 reshape.32
  2.5 0.8 broadcast_in_dim.26
  3.2 4.7 %all-to-all-start = ((bf16[8,16,1024]{2,1,0:T(8,128)(2,1)}), bf16[8,16,1024]{2,1,0:T(8,128)(2,1)S(1)}, u32[]{:S(2)}, u32[]{:S(2)}) async-start(bf16[8,16,1024]{2,1,0:T(8,128)(2,1)} %bitcast.3), calls=%async_computation | async-start | bytes 524288 | tf_op jit(solution)/shard_map/move_queries/all_to_all | solution.py:241
  8.5 1.3 minimum_clamp_fusion.live
  9.8 3.5 %pack.1 = (bf16[2,1056,128]{2,1,0:T(8,128)(2,1)}, bf16[2,1056,128]{2,1,0:T(8,128)(2,1)}, bf16[2,1056,128]{2,1,0:T(8,128)(2,1)}, bf16[2,1056,128]{2,1,0:T(8,128)(2,1)}) custom-call(s32[1]{0:T(128)} %bitcast.place, s32[8]{0:T(128)} %minimum_clamp_fusion.live, bf16[1024,256]{1,0:T(8,128)(2,1)} %keys_in.1, bf16[1024,256]{1,0:T(8,128)(2,1)} %values_in.1, ...), custom_call_target="tpu_custom_call" | custom-call | flops 1 | bytes 1 | tf_op jit(solution)/shard_map/pack/pallas_call | solution.py:287
  13.3 1.0 all-to-all-done
  14.4 0.7 collective-permute-start
  15.1 5.9 %collective-permute-start.1 = (bf16[2,1056,128]{2,1,0:T(8,128)(2,1)}, bf16[2,1056,128]{2,1,0:T(8,128)(2,1)S(1)}, u32[]{:S(2)}, u32[]{:S(2)}) collective-permute-start(bf16[2,1056,128]{2,1,0:T(8,128)(2,1)} %get-tuple-element.47), channel_id=1, source_target_pairs={{1,9},{5,13},{8,0},{12,4},{3,11},{7,15},{10,2},{14,6},{17,25},{21,... | collective-permute-start | bytes 1622024 | tf_op jit(solution)/shard_map/move_kv/ppermute | solution.py:254
  21.0 1.3 collective-permute-start.2
  22.4 1.1 broadcast_in_dim.28
  23.5 7.5 %all-to-all-start.1 = ((bf16[8,64,1024]{2,1,0:T(8,128)(2,1)}), bf16[8,64,1024]{2,1,0:T(8,128)(2,1)S(1)}, u32[]{:S(2)}, u32[]{:S(2)}) async-start(bf16[8,64,1024]{2,1,0:T(8,128)(2,1)} %broadcast_in_dim.28), calls=%async_computation.1 | async-start | bytes 2097152 | tf_op jit(solution)/shard_map/move_queries/all_to_all | solution.py:241
  31.0 0.6 pad_add_fusion.place
  31.6 0.0 collective-permute-done
  31.6 0.2 collective-permute-done.2
  31.9 0.6 copy-done.3
  32.4 0.2 copy-done.4
  32.6 0.2 copy-done.5
  32.8 1.8 %pad_maximum_fusion.near = bf16[4,2,1056,128]{3,2,1,0:T(8,128)(2,1)S(1)} fusion(bf16[1,2,1056,128]{3,2,1,0:T(8,128)(2,1)} %bitcast.29, bf16[1,2,1056,128]{3,2,1,0:T(8,128)(2,1)} %bitcast.28, bf16[1,2,1056,128]{3,2,1,0:T(8,128)(2,1)} %bitcast.27, bf16[1,2,1056,128]{3,2,1,0:T(8,128)(2,1)} %bitcast.26), kind=kLoop, calls=%fused_computation | loop fusion | flops 3244032 | bytes 4325376 | tf_op jit(solution)/shard_map/move_kv/stack | solution.py:336
  34.6 0.0 copy-start.6
  34.6 4.5 %move_weight.1 = (bf16[512,512]{1,0:T(8,128)(2,1)}, bf16[512,512]{1,0:T(8,128)(2,1)}, bf16[512,512]{1,0:T(8,128)(2,1)}, bf16[512,512]{1,0:T(8,128)(2,1)}, bf16[5...) custom-call(s32[2]{0:T(128)} %pad_add_fusion.place, ...), custom_call_target="tpu_custom_call" | custom-call | flops 1 | bytes 1 | tf_op jit(solution)/shard_map/move_weight/pallas_call | solution.py:313
  39.2 8.2 %all-to-all-done.1 = bf16[8,64,1024]{2,1,0:T(8,128)(2,1)S(1)} async-done(((bf16[8,64,1024]{2,1,0:T(8,128)(2,1)}), bf16[8,64,1024]{2,1,0:T(8,128)(2,1)S(1)}, u32[]{:S(2)}, u32[]{:S(2)}) %all-to-all-start.1) | async-done | bytes 1048608 | tf_op jit(solution)/shard_map/move_queries/all_to_all | solution.py:241
  47.4 1.3 collective-permute-start.4
  48.7 0.1 collective-permute-start.5
  48.8 5.1 %collective-permute-start.6 = (bf16[512,512]{1,0:T(8,128)(2,1)}, bf16[512,512]{1,0:T(8,128)(2,1)}, u32[]{:S(2)}, u32[]{:S(2)}) collective-permute-start(bf16[512,512]{1,0:T(8,128)(2,1)} %get-tuple-element.62), channel_id=1, source_target_pairs={{0,8},{4,12},{8,0},{12,4},{1,9},{5,13},{9,1},{13,5},{2,10},{6,14},... | collective-permute-start | bytes 1572872 | tf_op jit(solution)/shard_map/move_weight/ppermute | solution.py:245
  53.9 0.1 copy.13.pos_q
  54.0 0.1 fusion.2
  54.1 0.1 concatenate.3
  54.2 0.7 fusion.1
  54.9 0.1 reshape.39.live
  55.0 13.2 %attend.1 = bf16[512,1152]{1,0:T(8,128)(2,1)} custom-call(s32[32]{0:T(128)S(1)} %reshape.39.live, s32[1]{0:T(128)} %bitcast.12.here, bf16[512,1024]{1,0:T(8,128)(2,1)S(1)} %bitcast.22, bf16[4,2,1056,128]{3,2,1,0:T(8,128)(2,1)S(1)} %pad_maximum_fusion.near, bf16[4,2,1056,128]{3,2,1,0:T(8,128)(2,1)} %collective-permute-done.4.far, s32[512,1]{1,0:T(8,128)S(1)} %copy.13.pos_q, ...), custom_call_target="tpu_custom_call" | custom-call | flops 1 | bytes 1 | tf_op jit(solution)/shard_map/attend/pallas_call | solution.py:353
  68.2 8.1 %collective-permute-done.6.refs_2_ = bf16[512,512]{1,0:T(8,128)(2,1)} collective-permute-done((bf16[512,512]{1,0:T(8,128)(2,1)}, bf16[512,512]{1,0:T(8,128)(2,1)}, u32[]{:S(2)}, u32[]{:S(2)}) %collective-permute-start.6) | collective-permute-done | bytes 524320 | tf_op jit(solution)/shard_map/move_weight/ppermute | solution.py:245
  76.3 3.6 %all-to-all-start.2 = ((bf16[8,64,1152]{2,1,0:T(8,128)(2,1)}), bf16[8,64,1152]{2,1,0:T(8,128)(2,1)S(1)}, u32[]{:S(2)}, u32[]{:S(2)}) async-start(bf16[8,64,1152]{2,1,0:T(8,128)(2,1)} %bitcast.15), calls=%async_computation.2 | async-start | bytes 2359296 | tf_op jit(solution)/shard_map/move_partials/all_to_all | solution.py:241
  79.9 3.4 %collective-permute-start.10 = (bf16[512,512]{1,0:T(8,128)(2,1)}, bf16[512,512]{1,0:T(8,128)(2,1)S(1)}, u32[]{:S(2)}, u32[]{:S(2)}) collective-permute-start(bf16[512,512]{1,0:T(8,128)(2,1)} %get-tuple-element.65), channel_id=1, source_target_pairs={{0,12},{4,0},{8,4},{12,8},{1,13},{5,1},{9,5},{13,9},{2,14},{6,2},{... | collective-permute-start | bytes 1572872 | tf_op jit(solution)/shard_map/move_weight/ppermute | solution.py:245
  83.3 1.3 collective-permute-start.9
  84.5 12.1 %all-to-all-done.2.parts = bf16[8,64,1152]{2,1,0:T(8,128)(2,1)S(1)} async-done(((bf16[8,64,1152]{2,1,0:T(8,128)(2,1)}), bf16[8,64,1152]{2,1,0:T(8,128)(2,1)S(1)}, u32[]{:S(2)}, u32[]{:S(2)}) %all-to-all-start.2) | async-done | bytes 1179680 | tf_op jit(solution)/shard_map/move_partials/all_to_all | solution.py:241
  96.7 2.4 %settle.1 = bf16[8,64,1024]{2,1,0:T(8,128)(2,1)} custom-call(bf16[8,64,1152]{2,1,0:T(8,128)(2,1)S(1)} %all-to-all-done.2.parts), custom_call_target="tpu_custom_call" | custom-call | flops 1 | bytes 1 | tf_op jit(solution)/shard_map/settle/pallas_call | solution.py:372
  99.0 6.5 %collective-permute-done.10.refs_7_ = bf16[512,512]{1,0:T(8,128)(2,1)S(1)} collective-permute-done((bf16[512,512]{1,0:T(8,128)(2,1)}, bf16[512,512]{1,0:T(8,128)(2,1)S(1)}, u32[]{:S(2)}, u32[]{:S(2)}) %collective-permute-start.10) | collective-permute-done | bytes 524320 | tf_op jit(solution)/shard_map/move_weight/ppermute | solution.py:245
  105.5 3.1 %collective-permute-done.8.refs_5_ = bf16[512,512]{1,0:T(8,128)(2,1)S(1)} collective-permute-done((bf16[512,512]{1,0:T(8,128)(2,1)}, bf16[512,512]{1,0:T(8,128)(2,1)S(1)}, u32[]{:S(2)}, u32[]{:S(2)}) %collective-permute-start.8) | collective-permute-done | bytes 524320 | tf_op jit(solution)/shard_map/move_weight/ppermute | solution.py:245
  108.6 5.2 %all-to-all-start.3 = ((bf16[8,64,1024]{2,1,0:T(8,128)(2,1)}), bf16[8,64,1024]{2,1,0:T(8,128)(2,1)S(1)}, u32[]{:S(2)}, u32[]{:S(2)}) async-start(bf16[8,64,1024]{2,1,0:T(8,128)(2,1)} %settle.1), calls=%async_computation.3 | async-start | bytes 2097152 | tf_op jit(solution)/shard_map/move_attended/all_to_all | solution.py:241
  113.9 0.1 pad_add_fusion.1.place
  113.9 14.0 %all-to-all-done.3 = bf16[8,64,1024]{2,1,0:T(8,128)(2,1)S(1)} async-done(((bf16[8,64,1024]{2,1,0:T(8,128)(2,1)}), bf16[8,64,1024]{2,1,0:T(8,128)(2,1)S(1)}, u32[]{:S(2)}, u32[]{:S(2)}) %all-to-all-start.3) | async-done | bytes 1048608 | tf_op jit(solution)/shard_map/move_attended/all_to_all | solution.py:241
  127.9 2.8 %project.3 = bf16[4,2,128,512]{3,2,1,0:T(8,128)(2,1)S(1)} custom-call(s32[2]{0:T(128)S(1)} %pad_add_fusion.1.place, bf16[512,1024]{1,0:T(8,128)(2,1)S(1)} %bitcast.20, bf16[512,512]{1,0:T(8,128)(2,1)S(1)} %copy-done, bf16[512,512]{1,0:T(8,128)(2,1)} %collective-permute-done.5.refs_1_, bf16[512,512]{1,0:T(8,128)(2,1)} %collective-permute-done.6.refs_2_, ...), custom_call_target="tpu_custom_call" | custom-call | flops 1 | bytes 1 | tf_op jit(solution)/shard_map/project/pallas_call | solution.py:387
  130.7 4.2 %collective-permute-start.11 = (bf16[4,2,128,512]{3,2,1,0:T(8,128)(2,1)S(1)}, bf16[4,2,128,512]{3,2,1,0:T(8,128)(2,1)S(1)}, u32[]{:S(2)}, u32[]{:S(2)}) collective-permute-start(bf16[4,2,128,512]{3,2,1,0:T(8,128)(2,1)S(1)} %project.3), channel_id=1, source_target_pairs={{0,1},{1,0},{2,3},{3,2},{4,5},{5,4},{6,7},{7,6},{8,9},{9,8},{10,11... | collective-permute-start | bytes 3145736 | tf_op jit(solution)/shard_map/project/ppermute | solution.py:249
  134.9 2.8 %project.2 = bf16[4,2,128,512]{3,2,1,0:T(8,128)(2,1)S(1)} custom-call(s32[2]{0:T(128)S(1)} %copy-done.2, bf16[512,1024]{1,0:T(8,128)(2,1)S(1)} %bitcast.21, bf16[512,512]{1,0:T(8,128)(2,1)S(1)} %copy-done, bf16[512,512]{1,0:T(8,128)(2,1)} %collective-permute-done.5.refs_1_, bf16[512,512]{1,0:T(8,128)(2,1)} %collective-permute-done.6.refs_2_, ...), custom_call_target="tpu_custom_call" | custom-call | flops 1 | bytes 1 | tf_op jit(solution)/shard_map/project/pallas_call | solution.py:387
  137.7 0.3 add_convert_fusion
  138.0 18.3 %all_to_all.25 = bf16[8,128,512]{2,1,0:T(8,128)(2,1)S(1)} all-to-all(bf16[8,128,512]{2,1,0:T(8,128)(2,1)S(1)} %bitcast.24), channel_id=1, replica_groups=mesh['z'=4,'x_hi'=2,'y'=4,'x_lo'=2,'core'=2] {'y','x_lo'}, dimensions={0} | all-to-all | bytes 2097152 | tf_op jit(solution)/shard_map/move_terms/all_to_all | solution.py:241
  156.3 0.8 reduce_sum.12
  (22 shorter events, 0.1 us)
Async XLA Ops:
  0.0 34.6 %collective-permute-start.3 = (bf16[4096,512]{1,0:T(8,128)(2,1)}, bf16[4096,512]{1,0:T(8,128)(2,1)}, u32[]{:S(2)}, u32[]{:S(2)}) collective-permute-start(bf16[4096,512]{1,0:T(8,128)(2,1)} %mine.1), channel_id=1, source_target_pairs={{0,1},{1,0},{2,3},{3,2},{4,5},{5,4},{6,7},{7,6},{8,9},{9,8},{10,11... | collective-permute-start | bytes 12582920 | tf_op jit(solution)/shard_map/move_weight/ppermute | solution.py:249
  3.2 11.2 %all-to-all-start = ((bf16[8,16,1024]{2,1,0:T(8,128)(2,1)}), bf16[8,16,1024]{2,1,0:T(8,128)(2,1)S(1)}, u32[]{:S(2)}, u32[]{:S(2)}) async-start(bf16[8,16,1024]{2,1,0:T(8,128)(2,1)} %bitcast.3), calls=%async_computation | async-start | bytes 524288 | tf_op jit(solution)/shard_map/move_queries/all_to_all | solution.py:241
  14.4 17.2 %collective-permute-start = (bf16[2,1056,128]{2,1,0:T(8,128)(2,1)}, bf16[2,1056,128]{2,1,0:T(8,128)(2,1)S(1)}, u32[]{:S(2)}, u32[]{:S(2)}) collective-permute-start(bf16[2,1056,128]{2,1,0:T(8,128)(2,1)} %get-tuple-element.46), channel_id=1, source_target_pairs={{0,4},{5,9},{9,13},{12,0},{2,6},{7,11},{11,15},{14,2},{16,20},{21,... | collective-permute-start | bytes 1622024 | tf_op jit(solution)/shard_map/move_kv/ppermute | solution.py:254
  15.1 16.5 %collective-permute-start.1 = (bf16[2,1056,128]{2,1,0:T(8,128)(2,1)}, bf16[2,1056,128]{2,1,0:T(8,128)(2,1)S(1)}, u32[]{:S(2)}, u32[]{:S(2)}) collective-permute-start(bf16[2,1056,128]{2,1,0:T(8,128)(2,1)} %get-tuple-element.47), channel_id=1, source_target_pairs={{1,9},{5,13},{8,0},{12,4},{3,11},{7,15},{10,2},{14,6},{17,25},{21,... | collective-permute-start | bytes 1622024 | tf_op jit(solution)/shard_map/move_kv/ppermute | solution.py:254
  21.0 10.9 %collective-permute-start.2 = (bf16[2,1056,128]{2,1,0:T(8,128)(2,1)}, bf16[2,1056,128]{2,1,0:T(8,128)(2,1)S(1)}, u32[]{:S(2)}, u32[]{:S(2)}) collective-permute-start(bf16[2,1056,128]{2,1,0:T(8,128)(2,1)} %get-tuple-element.48), channel_id=1, source_target_pairs={{1,13},{4,0},{8,4},{13,9},{3,15},{6,2},{10,6},{15,11},{17,29},{20,... | collective-permute-start | bytes 1622024 | tf_op jit(solution)/shard_map/move_kv/ppermute | solution.py:254
  23.5 23.9 %all-to-all-start.1 = ((bf16[8,64,1024]{2,1,0:T(8,128)(2,1)}), bf16[8,64,1024]{2,1,0:T(8,128)(2,1)S(1)}, u32[]{:S(2)}, u32[]{:S(2)}) async-start(bf16[8,64,1024]{2,1,0:T(8,128)(2,1)} %broadcast_in_dim.28), calls=%async_computation.1 | async-start | bytes 2097152 | tf_op jit(solution)/shard_map/move_queries/all_to_all | solution.py:241
  31.6 0.8 copy-start.3
  31.6 1.0 copy-start.4
  31.9 0.9 copy-start.5
  34.6 19.3 %copy-start.6 = (s32[512]{0:T(512)S(1)}, s32[512]{0:T(512)}, u32[]{:S(2)}) copy-start(s32[512]{0:T(512)} %param.17) | copy-start | bytes 6148
  47.4 6.8 %collective-permute-start.4 = (bf16[4,2,1056,128]{3,2,1,0:T(8,128)(2,1)S(1)}, bf16[4,2,1056,128]{3,2,1,0:T(8,128)(2,1)}, u32[]{:S(2)}, u32[]{:S(2)}) collective-permute-start(bf16[4,2,1056,128]{3,2,1,0:T(8,128)(2,1)S(1)} %pad_maximum_fusion.near), channel_id=1, source_target_pairs={{0,1},{4,5},{9,8},{13,12},{2,3},{6,7},{11,10},{15,14},{16,17},{20,... | collective-permute-start | bytes 6488072 | tf_op jit(solution)/shard_map/move_kv/ppermute | solution.py:258
  48.7 19.5 %collective-permute-start.5 = (bf16[512,512]{1,0:T(8,128)(2,1)}, bf16[512,512]{1,0:T(8,128)(2,1)}, u32[]{:S(2)}, u32[]{:S(2)}) collective-permute-start(bf16[512,512]{1,0:T(8,128)(2,1)} %get-tuple-element.60), channel_id=1, source_target_pairs={{0,4},{4,8},{8,12},{12,0},{1,5},{5,9},{9,13},{13,1},{2,6},{6,10},{... | collective-permute-start | bytes 1572872 | tf_op jit(solution)/shard_map/move_weight/ppermute | solution.py:245
  48.8 27.5 %collective-permute-start.6 = (bf16[512,512]{1,0:T(8,128)(2,1)}, bf16[512,512]{1,0:T(8,128)(2,1)}, u32[]{:S(2)}, u32[]{:S(2)}) collective-permute-start(bf16[512,512]{1,0:T(8,128)(2,1)} %get-tuple-element.62), channel_id=1, source_target_pairs={{0,8},{4,12},{8,0},{12,4},{1,9},{5,13},{9,1},{13,5},{2,10},{6,14},... | collective-permute-start | bytes 1572872 | tf_op jit(solution)/shard_map/move_weight/ppermute | solution.py:245
  53.9 22.4 %collective-permute-start.7 = (bf16[512,512]{1,0:T(8,128)(2,1)}, bf16[512,512]{1,0:T(8,128)(2,1)}, u32[]{:S(2)}, u32[]{:S(2)}) collective-permute-start(bf16[512,512]{1,0:T(8,128)(2,1)} %get-tuple-element.64), channel_id=1, source_target_pairs={{0,12},{4,0},{8,4},{12,8},{1,13},{5,1},{9,5},{13,9},{2,14},{6,2},{... | collective-permute-start | bytes 1572872 | tf_op jit(solution)/shard_map/move_weight/ppermute | solution.py:245
  76.3 20.4 %all-to-all-start.2 = ((bf16[8,64,1152]{2,1,0:T(8,128)(2,1)}), bf16[8,64,1152]{2,1,0:T(8,128)(2,1)S(1)}, u32[]{:S(2)}, u32[]{:S(2)}) async-start(bf16[8,64,1152]{2,1,0:T(8,128)(2,1)} %bitcast.15), calls=%async_computation.2 | async-start | bytes 2359296 | tf_op jit(solution)/shard_map/move_partials/all_to_all | solution.py:241
  79.8 48.1 %copy-start = (bf16[512,512]{1,0:T(8,128)(2,1)S(1)}, bf16[512,512]{1,0:T(8,128)(2,1)}, u32[]{:S(2)}) copy-start(bf16[512,512]{1,0:T(8,128)(2,1)} %get-tuple-element.69.refs_0_) | copy-start | bytes 1572868
  79.8 48.1 %copy-start.1 = (bf16[512,512]{1,0:T(8,128)(2,1)S(1)}, bf16[512,512]{1,0:T(8,128)(2,1)}, u32[]{:S(2)}) copy-start(bf16[512,512]{1,0:T(8,128)(2,1)} %get-tuple-element.73.refs_4_) | copy-start | bytes 1572868
  79.9 25.7 %collective-permute-start.10 = (bf16[512,512]{1,0:T(8,128)(2,1)}, bf16[512,512]{1,0:T(8,128)(2,1)S(1)}, u32[]{:S(2)}, u32[]{:S(2)}) collective-permute-start(bf16[512,512]{1,0:T(8,128)(2,1)} %get-tuple-element.65), channel_id=1, source_target_pairs={{0,12},{4,0},{8,4},{12,8},{1,13},{5,1},{9,5},{13,9},{2,14},{6,2},{... | collective-permute-start | bytes 1572872 | tf_op jit(solution)/shard_map/move_weight/ppermute | solution.py:245
  83.3 25.4 %collective-permute-start.8 = (bf16[512,512]{1,0:T(8,128)(2,1)}, bf16[512,512]{1,0:T(8,128)(2,1)S(1)}, u32[]{:S(2)}, u32[]{:S(2)}) collective-permute-start(bf16[512,512]{1,0:T(8,128)(2,1)} %get-tuple-element.61), channel_id=1, source_target_pairs={{0,4},{4,8},{8,12},{12,0},{1,5},{5,9},{9,13},{13,1},{2,6},{6,10},{... | collective-permute-start | bytes 1572872 | tf_op jit(solution)/shard_map/move_weight/ppermute | solution.py:245
  83.3 25.4 %collective-permute-start.9 = (bf16[512,512]{1,0:T(8,128)(2,1)}, bf16[512,512]{1,0:T(8,128)(2,1)}, u32[]{:S(2)}, u32[]{:S(2)}) collective-permute-start(bf16[512,512]{1,0:T(8,128)(2,1)} %get-tuple-element.63), channel_id=1, source_target_pairs={{0,8},{4,12},{8,0},{12,4},{1,9},{5,13},{9,1},{13,5},{2,10},{6,14},... | collective-permute-start | bytes 1572872 | tf_op jit(solution)/shard_map/move_weight/ppermute | solution.py:245
  108.6 19.3 %all-to-all-start.3 = ((bf16[8,64,1024]{2,1,0:T(8,128)(2,1)}), bf16[8,64,1024]{2,1,0:T(8,128)(2,1)S(1)}, u32[]{:S(2)}, u32[]{:S(2)}) async-start(bf16[8,64,1024]{2,1,0:T(8,128)(2,1)} %settle.1), calls=%async_computation.3 | async-start | bytes 2097152 | tf_op jit(solution)/shard_map/move_attended/all_to_all | solution.py:241
  127.9 7.0 %copy-start.2 = (s32[2]{0:T(128)S(1)}, s32[2]{0:T(128)}, u32[]{:S(2)}) copy-start(s32[2]{0:T(128)} %pad_add_fusion.place) | copy-start | bytes 28
  130.7 7.0 %collective-permute-start.11 = (bf16[4,2,128,512]{3,2,1,0:T(8,128)(2,1)S(1)}, bf16[4,2,128,512]{3,2,1,0:T(8,128)(2,1)S(1)}, u32[]{:S(2)}, u32[]{:S(2)}) collective-permute-start(bf16[4,2,128,512]{3,2,1,0:T(8,128)(2,1)S(1)} %project.3), channel_id=1, source_target_pairs={{0,1},{1,0},{2,3},{3,2},{4,5},{5,4},{6,7},{7,6},{8,9},{9,8},{10,11... | collective-permute-start | bytes 3145736 | tf_op jit(solution)/shard_map/project/ppermute | solution.py:249

commit v4 on v3

v4 whole, which is shorter than its diff:
```python
import functools
import math

import jax
import jax.numpy as jnp
import numpy as np
from jax import lax
from jax.experimental import pallas as pl
from jax.experimental.pallas import tpu as pltpu
from jax.sharding import Mesh
from jax.sharding import PartitionSpec as P

HD = 128
SPAN = 128
KEY_BLOCK = 512
PIECES = 3
FILL = -1e30
LOWEST = -1e20
LOG2_SCALE = math.log2(math.e) / math.sqrt(HD)
F32 = jnp.float32
BF16 = jnp.bfloat16
TINY = pl.CostEstimate(flops=1, bytes_accessed=1, transcendentals=0)
VMEM = pl.BlockSpec(memory_space=pltpu.VMEM)
SMEM = pl.BlockSpec(memory_space=pltpu.SMEM)
ANY = pl.BlockSpec(memory_space=pl.ANY)


def dot_nt(a, b):
    return lax.dot_general(a, b, (((1,), (1,)), ((), ())), preferred_element_type=F32)


def grant(mib):
    return pltpu.CompilerParams(vmem_limit_bytes=mib << 20)


def pack_kernel(place, valid_len, span_ids, offset, keys_in, values_in, new_keys_in, new_values_in, *refs):
    outs, (keys, values, new_keys, new_values, heads, sems) = refs[:4], refs[4:]
    copies = [
        pltpu.make_async_copy(source, target, sems.at[i])
        for i, (source, target) in enumerate(
            ((keys_in, keys), (values_in, values), (new_keys_in, new_keys), (new_values_in, new_values))
        )
    ]
    for copy in copies:
        copy.start()
    slots = valid_len.shape[0]
    rows = slots * SPAN
    fresh = new_keys.shape[0]
    row_id = lax.broadcasted_iota(jnp.int32, (SPAN, HD), 0)
    lane_id = lax.broadcasted_iota(jnp.int32, (16, HD), 1)
    live = [
        jnp.clip(jnp.minimum(valid_len[s], offset[0] - span_ids[s] * SPAN), 0, SPAN) for s in range(slots)
    ]
    counts = jnp.zeros((16, HD), F32)
    for s in range(slots):
        counts = jnp.where(lane_id == s, live[s].astype(F32), counts)
    for copy in copies:
        copy.wait()
    for head in range(2):
        cols = slice(head * HD, (head + 1) * HD)
        for s in range(slots):
            part = slice(s * SPAN, (s + 1) * SPAN)
            visible = row_id < live[s]
            key = keys[part, cols].astype(F32)
            key = jnp.where(visible, key, jnp.broadcast_to(key[:1], key.shape))
            heads[head, 0, part, :] = key.astype(BF16)
            heads[head, 1, part, :] = jnp.where(visible, values[part, cols].astype(F32), 0.0).astype(BF16)
        heads[head, 0, rows : rows + fresh, :] = new_keys[:, cols]
        heads[head, 1, rows : rows + fresh, :] = new_values[:, cols]
        heads[head, 0, rows + fresh :, :] = counts.astype(BF16)
        heads[head, 1, rows + fresh :, :] = counts.astype(BF16)
    for k, out in enumerate(outs):
        out[...] = heads[lax.rem(place[0] + k, 4) // 2]


def attend_kernel(live, queries, kv0, kv1, kv2, kv3, pos_q, pos_n, out, kc, vc, top, acc):
    sources = (kv0, kv1, kv2, kv3)
    slots = live.shape[0] // len(sources)
    rows = slots * SPAN
    fresh = kv0.shape[1] - rows - 16
    heads = queries.shape[1] // HD
    tokens = queries.shape[0]
    row_id = lax.broadcasted_iota(jnp.int32, (SPAN, HD), 0)
    start = len(sources) * fresh

    def rounded(count):
        return ((count + 15) // 16) * 16

    place = jnp.int32(start)
    for i, kv in enumerate(sources):
        target = slice(i * fresh, (i + 1) * fresh)
        kc[target, :] = kv[0, rows : rows + fresh, :]
        vc[target, :HD] = kv[1, rows : rows + fresh, :]
        vc[target, HD:] = jnp.ones((fresh, HD), BF16)

        def gather_slot(s, at, kv=kv, i=i):
            count = live[i * slots + s]
            source = pl.ds(pl.multiple_of(s * SPAN, SPAN), SPAN)
            target = pl.ds(pl.multiple_of(at, 16), SPAN)
            kc[target, :] = kv[0, source, :]
            vc[target, :HD] = kv[1, source, :]
            vc[target, HD:] = jnp.where(row_id < count, 1.0, 0.0).astype(BF16)
            return at + rounded(count)

        place = lax.fori_loop(0, slots, gather_slot, place)
    tail = pl.ds(pl.multiple_of(place, 16), KEY_BLOCK)
    spare = kc[start : start + 16, :].astype(F32)[:1]
    spare = jnp.where(place > start, spare, 0.0)
    kc[tail, :] = jnp.broadcast_to(spare, (KEY_BLOCK, HD)).astype(BF16)
    vc[tail, :] = jnp.zeros((KEY_BLOCK, 2 * HD), BF16)
    blocks = (place + KEY_BLOCK - 1) // KEY_BLOCK

    lane_id = lax.broadcasted_iota(jnp.int32, (tokens, HD), 1)
    key_id = lax.broadcasted_iota(jnp.int32, (1, KEY_BLOCK), 1)
    seen = jnp.where(key_id < place, pos_n[...], tokens) <= pos_q[...]
    lanes = [slice(j * HD, (j + 1) * HD) for j in range(KEY_BLOCK // HD)]

    def head_cols(h):
        return slice(h * HD, (h + 1) * HD)

    def rounded_max(s):
        high = functools.reduce(jnp.maximum, [s[:, g] for g in lanes])
        m = jnp.maximum(jnp.max(high, axis=1, keepdims=True) * LOG2_SCALE, LOWEST)
        return jnp.broadcast_to(m.astype(BF16).astype(F32), (tokens, HD))

    def score(h, part):
        return dot_nt(queries[:, head_cols(h)], kc[part, :])

    def sums(s, m, part):
        p = jnp.concatenate([jnp.exp2(s[:, g] * LOG2_SCALE - m).astype(BF16) for g in lanes], axis=1)
        return jnp.dot(p, vc[part, :], preferred_element_type=F32)

    def begin(h, part, s):
        s = jnp.where(seen, s, FILL)
        m = rounded_max(s)
        top[h] = m
        acc[h] = sums(s, m, part)

    def add(h, part, s):
        old = top[h]
        m = jnp.maximum(old, rounded_max(s))
        top[h] = m
        shrink = jnp.exp2(old - m)
        term = sums(s, m, part)
        acc[h, :, :HD] = acc[h, :, :HD] * shrink + term[:, :HD]
        acc[h, :, HD:] = acc[h, :, HD:] * shrink + term[:, HD:]

    def every_head(visit, part):
        s = score(0, part)
        for h in range(heads):
            following = score(h + 1, part) if h + 1 < heads else None
            visit(h, part, s)
            s = following

    every_head(begin, slice(0, KEY_BLOCK))

    def step(b, _):
        every_head(add, pl.ds(pl.multiple_of(b * KEY_BLOCK, KEY_BLOCK), KEY_BLOCK))
        return _

    lax.fori_loop(1, blocks, step, 0)

    notes = jnp.zeros((tokens, HD), F32)
    for h in range(heads):
        total = acc[h, :, HD:]
        high = total.astype(BF16).astype(F32)
        out[:, head_cols(h)] = acc[h, :, :HD].astype(BF16)
        notes = jnp.where(lane_id == h, top[h], notes)
        notes = jnp.where(lane_id == heads + h, high, notes)
        notes = jnp.where(lane_id == 2 * heads + h, total - high, notes)
    out[:, heads * HD :] = notes.astype(BF16)


def settle_kernel(parts, out):
    groups, tokens, width = parts.shape
    heads = width // HD - 1
    notes = [parts[g, :, heads * HD :].astype(F32) for g in range(groups)]
    highest = notes[0]
    for g in range(1, groups):
        highest = jnp.maximum(highest, notes[g])
    factors = [jnp.exp2(notes[g] - highest) for g in range(groups)]
    for h in range(heads):
        cols = slice(h * HD, (h + 1) * HD)
        numerator = jnp.zeros((tokens, HD), F32)
        total = jnp.zeros((tokens, 1), F32)
        for g in range(groups):
            factor = factors[g][:, h : h + 1]
            numerator += factor * parts[g, :, cols].astype(F32)
            total += factor * (
                notes[g][:, heads + h : heads + h + 1] + notes[g][:, 2 * heads + h : 2 * heads + h + 1]
            )
        attended = (numerator / total).astype(BF16)
        for g in range(out.shape[0]):
            out[g, :, cols] = attended


def cut_kernel(place, weight, *refs):
    outs, (held, arrived, left) = refs[:-3], refs[-3:]
    rows = held.shape[1]
    copies = []
    for i, out in enumerate(outs):
        k, start = i // PIECES, sum(o.shape[0] for o in outs[i // PIECES * PIECES : i])
        page = held.at[k, slice(start, start + out.shape[0]), :]
        part = pl.ds(pl.multiple_of(lax.rem(place[0] + k, 4) * rows + start, 16), out.shape[0])
        copies.append(
            (
                pltpu.make_async_copy(weight.at[part, :], page, arrived.at[i]),
                pltpu.make_async_copy(page, out, left.at[i]),
            )
        )
        copies[i][0].start()
    for arrival, departure in copies:
        arrival.wait()
        departure.start()
    for _, departure in copies:
        departure.wait()


def project_kernel(place, attended, *refs):
    weights, out = refs[:-1], refs[-1]
    size = out.shape[2]
    picked = [pl.ds(pl.multiple_of((2 * r + place[1]) * size, size), size) for r in range(out.shape[1])]
    rows = jnp.concatenate([attended[p, :] for p in picked], axis=0)
    for k in range(4):
        target = lax.rem(place[0] + 4 - k, 4)
        weight = jnp.concatenate([w[...] for w in weights[k * PIECES : (k + 1) * PIECES]], axis=0)
        term = jnp.dot(rows, weight, preferred_element_type=F32).astype(BF16)
        for r in range(out.shape[1]):
            out[target, r] = term[r * size : (r + 1) * size]


def swap(x, axes):
    return lax.all_to_all(x, axes, split_axis=0, concat_axis=0, tiled=False)


def along_y(x, distance):
    return lax.ppermute(x, "y", [(i, (i + distance) % 4) for i in range(4)])


def to_other(x, axis):
    return lax.ppermute(x, axis, [(0, 1), (1, 0)])


def shards(
    queries,
    new_keys,
    new_values,
    cache_keys,
    cache_values,
    span_ids,
    valid_len,
    pos_ids,
    offset,
    out_weight,
):
    y, core = lax.axis_index("y"), lax.axis_index("core")
    group = lax.axis_index("z") * 2 + lax.axis_index("x_hi")
    place = y[None].astype(jnp.int32)
    groups = 8
    fresh, width = queries.shape
    slots = span_ids.shape[0]
    rows = slots * SPAN
    quarter = width // 4
    tokens = pos_ids.shape[0]

    packet = jax.ShapeDtypeStruct((2, rows + fresh + 16, HD), BF16)
    with jax.named_scope("pack"):
        packets = pl.pallas_call(
            pack_kernel,
            out_shape=[packet] * 4,
            in_specs=[SMEM] * 4 + [ANY] * 4,
            out_specs=[VMEM] * 4,
            scratch_shapes=[
                pltpu.VMEM(cache_keys.shape, BF16),
                pltpu.VMEM(cache_keys.shape, BF16),
                pltpu.VMEM(new_keys.shape, BF16),
                pltpu.VMEM(new_keys.shape, BF16),
                pltpu.VMEM((2,) + packet.shape, BF16),
                pltpu.SemaphoreType.DMA((4,)),
            ],
            compiler_params=grant(56),
            cost_estimate=TINY,
        )(place, valid_len, span_ids, offset, cache_keys, cache_values, new_keys, new_values)
    with jax.named_scope("move_queries"):
        mine = swap(queries.reshape(fresh, 4, quarter).transpose(1, 0, 2), "y")
        mine, packets = lax.optimization_barrier((mine, packets))
        mine = mine.reshape(4 * fresh, quarter)
        mine = swap(jnp.broadcast_to(mine[None], (groups,) + mine.shape), ("z", "x_hi")).reshape(tokens, quarter)
    with jax.named_scope("move_kv"):
        kv = [packets[0]] + [along_y(packets[k], k) for k in range(1, 4)]
        all_live = jnp.stack([packet[0, rows + fresh, :slots] for packet in kv]).astype(jnp.int32).reshape(-1)

    columns = out_weight.shape[1]
    with jax.named_scope("move_weight"):
        sizes = (448, 288, 288)
        chunks = pl.pallas_call(
            cut_kernel,
            out_shape=[jax.ShapeDtypeStruct((size, columns), BF16) for size in sizes * 4],
            in_specs=[SMEM, ANY],
            out_specs=[ANY] * (4 * PIECES),
            scratch_shapes=[
                pltpu.VMEM((4, quarter, columns), BF16),
                pltpu.SemaphoreType.DMA((4 * PIECES,)),
                pltpu.SemaphoreType.DMA((4 * PIECES,)),
            ],
            compiler_params=grant(56),
            cost_estimate=TINY,
        )(place, lax.optimization_barrier((out_weight, packets))[0])

        def pieces(j, after):
            ready, _ = lax.optimization_barrier(([chunks[k * PIECES + j] for k in range(4)], after))
            return [ready[0]] + [along_y(ready[k], k) for k in range(1, 4)]

        weights = [pieces(j, kv) for j in range(PIECES)]
        mine, chunks = lax.optimization_barrier((mine, chunks))

    pos_n = [
        lax.dynamic_slice_in_dim(pos_ids, (group * 4 + lax.rem(y + 4 - k, 4)) * fresh, fresh) for k in range(4)
    ]
    pos_n = jnp.concatenate(pos_n + [jnp.full((KEY_BLOCK - 4 * fresh,), -1, jnp.int32)])[None]
    pos_q = pos_ids[:, None]

    capacity = 4 * (rows + fresh) + KEY_BLOCK
    heads = quarter // HD
    with jax.named_scope("attend"):
        partial = pl.pallas_call(
            attend_kernel,
            out_shape=jax.ShapeDtypeStruct((tokens, quarter + HD), BF16),
            in_specs=[SMEM] + [VMEM] * 7,
            out_specs=VMEM,
            scratch_shapes=[
                pltpu.VMEM((capacity, HD), BF16),
                pltpu.VMEM((capacity, 2 * HD), BF16),
                pltpu.VMEM((heads, tokens, HD), F32),
                pltpu.VMEM((heads, tokens, 2 * HD), F32),
            ],
            compiler_params=grant(40),
            cost_estimate=TINY,
        )(all_live, mine, *kv, pos_q, pos_n)

    with jax.named_scope("move_partials"):
        partial, weights[0] = lax.optimization_barrier((partial, weights[0]))
        partial = swap(partial.reshape(groups, tokens // groups, quarter + HD), ("z", "x_hi"))
    with jax.named_scope("settle"):
        attended = pl.pallas_call(
            settle_kernel,
            out_shape=jax.ShapeDtypeStruct((groups, tokens // groups, quarter), BF16),
            in_specs=[VMEM],
            out_specs=VMEM,
            compiler_params=grant(24),
            cost_estimate=TINY,
        )(partial)
    with jax.named_scope("move_attended"):
        attended, weights[1] = lax.optimization_barrier((attended, weights[1]))
        attended = swap(attended, ("z", "x_hi")).reshape(tokens, quarter)


    def project(which):
        return pl.pallas_call(
            project_kernel,
            out_shape=jax.ShapeDtypeStruct((4, 2, tokens // 4, columns), BF16),
            in_specs=[SMEM] + [VMEM] * (1 + 4 * PIECES),
            out_specs=VMEM,
            compiler_params=grant(32),
            cost_estimate=TINY,
        )(jnp.stack([y, which]).astype(jnp.int32), attended, *[w[k] for k in range(4) for w in weights])

    with jax.named_scope("project"):
        theirs = to_other(project(1 - core), "core")
        terms = (project(core).astype(F32) + theirs.astype(F32)).astype(BF16)
    with jax.named_scope("move_terms"):
        terms = swap(terms.reshape(8, tokens // 4, columns), ("y", "x_lo"))
    return jnp.sum(terms.astype(F32), axis=0).astype(BF16)


def solution(mesh):
    fine = Mesh(mesh.devices.reshape(4, 2, 4, 2, 2), ("z", "x_hi", "y", "x_lo", "core"))
    ctx, head = ("z", "x_hi", "y"), ("x_lo", "core")
    in_specs = (
        P(ctx, head),
        P(ctx, head),
        P(ctx, head),
        P(ctx, head),
        P(ctx, head),
        P(ctx),
        P(ctx),
        P(),
        P(),
        P(head, ctx),
    )
    return jax.shard_map(shards, mesh=fine, in_specs=in_specs, out_specs=P(head, ctx), check_vma=False)
```

time: 158 us -> 143 us (0.905)
  waiting for transfers between devices: 53.3 us -> 33.6 us
  local copies, waits for them, and re-layouts: 4.3 us -> 9.09 us
  other arithmetic: 5.59 us -> 1.27 us
    all_to_all x4, waiting for transfers between devices: 35.4 us -> 12.7 us  [swap(): return lax.all_to_all(x, axes, split_axis=0, concat_axis=0, tiled=False)]
    ppermute x6 -> x1, starting transfers between devices: 14.9 us -> 2.54 us  [to_other(): return lax.ppermute(x, axis, [(0, 1), (1, 0)])]
    ppermute x6 -> x12, starting transfers between devices: 9.85 us -> 18.3 us  [along_y(): return lax.ppermute(x, 'y', [(i, (i + distance) % 4) for i in range(4)])]
    all_to_all x4, starting transfers between devices: 20.9 us -> 26.2 us  [swap(): return lax.all_to_all(x, axes, split_axis=0, concat_axis=0, tiled=False)]
    ppermute x6 -> x12, waiting for transfers between devices: 17.7 us -> 20.9 us  [along_y(): return lax.ppermute(x, 'y', [(i, (i + distance) % 4) for i in range(4)])]
    pallas_call x1, Pallas kernels: 13.2 us -> 15.4 us  [shards(): pl.pallas_call(attend_kernel, out_shape=jax.ShapeDtypeStruct((tokens, qua...]
    unnamed x14 -> x20, local copies, waits for them, and re-layouts: 0.97 us -> 3.2 us
    squeeze x0 -> x4, local copies, waits for them, and re-layouts: none -> 2.01 us  [shards(): jnp.stack([packet[0, rows + fresh, :slots] for packet in kv])]
  transfers between devices with their start and end apart: 16 -> 17, of which waited for: 8 -> 7; matrix products, arithmetic and copies ran while one was open for 5% -> 3% of each run, Pallas kernels for 17% -> 20%
where the time goes in v4:
time: 143 us; the launch traced here: 141 us
  starting transfers between devices  47 us (33%)
  waiting for transfers between devices  33.6 us (23%)
  Pallas kernels  30.3 us (21%)
  blocking collectives  19 us (13%)
  local copies, waits for them, and re-layouts  9.09 us (6%)
    all_to_all x4, starting transfers between devices, swap(): return lax.all_to_all(x, axes, split_axis=0, concat_axis=0, tiled=False)  26.2 us
    ppermute x12, waiting for transfers between devices, along_y(): return lax.ppermute(x, 'y', [(i, (i + distance) % 4) for i in range(4)])  20.9 us
    all_to_all x1, blocking collectives, swap(): return lax.all_to_all(x, axes, split_axis=0, concat_axis=0, tiled=False)  19 us
    ppermute x12, starting transfers between devices, along_y(): return lax.ppermute(x, 'y', [(i, (i + distance) % 4) for i in range(4)])  18.3 us
    pallas_call x1, Pallas kernels, shards(): pl.pallas_call(attend_kernel, out_shape=jax.ShapeDtypeStruct((tokens, qua...  15.4 us
    all_to_all x4, waiting for transfers between devices, swap(): return lax.all_to_all(x, axes, split_axis=0, concat_axis=0, tiled=False)  12.7 us
    pallas_call x2, Pallas kernels, project(): pl.pallas_call(project_kernel, out_shape=jax.ShapeDtypeStruct((4, 2, toke...  5.32 us
    pallas_call x1, Pallas kernels, shards(): pl.pallas_call(cut_kernel, out_shape=[jax.ShapeDtypeStruct((size, columns...  3.69 us
  transfers between devices with their start and end apart: 17, of which 7 were waited for; matrix products, arithmetic and copies ran while one was open for 3% of the time, Pallas kernels for 20%

profile of v4, /device:TPU:1, one launch (start us, length us, event | category | flops | bytes accessed | tf_op | source)
XLA Modules:
  0.0 141.1 jit_solution(9675865278158883817)
XLA Ops:
  0.0 1.0 reshape.21
  1.0 0.7 copy.14
  1.7 5.0 %all-to-all-start = ((bf16[4,16,1024]{2,1,0:T(8,128)(2,1)}), bf16[4,16,1024]{2,1,0:T(8,128)(2,1)S(1)}, u32[]{:S(2)}, u32[]{:S(2)}) async-start(bf16[4,16,1024]{2,1,0:T(8,128)(2,1)} %copy.14), calls=%async_computation | async-start | bytes 262144 | tf_op jit(solution)/shard_map/move_queries/all_to_all | solution.py:233
  7.4 3.5 %pack.1 = (bf16[2,1056,128]{2,1,0:T(8,128)(2,1)}, bf16[2,1056,128]{2,1,0:T(8,128)(2,1)}, bf16[2,1056,128]{2,1,0:T(8,128)(2,1)}, bf16[2,1056,128]{2,1,0:T(8,128)(2,1)}) custom-call(s32[1]{0:T(128)} %bitcast.place, s32[8]{0:T(128)} %valid_len.1, s32[8]{0:T(128)} %span_ids.1, s32[1]{0:T(128)S(6)} %copy.16.offset, bf16[1024,256]{1,0:T(8,128)(2,1)} %keys_in.1, ...), custom_call_target="tpu_custom_call" | custom-call | flops 1 | bytes 1 | tf_op jit(solution)/shard_map/pack/pallas_call | solution.py:268
  10.9 0.6 all-to-all-done
  11.5 0.9 collective-permute-start
  12.5 2.4 %collective-permute-start.1 = (bf16[2,1056,128]{2,1,0:T(8,128)(2,1)}, bf16[2,1056,128]{2,1,0:T(8,128)(2,1)S(1)}, u32[]{:S(2)}, u32[]{:S(2)}) collective-permute-start(bf16[2,1056,128]{2,1,0:T(8,128)(2,1)} %get-tuple-element.56), channel_id=1, source_target_pairs={{0,8},{4,12},{8,0},{12,4},{1,9},{5,13},{9,1},{13,5},{2,10},{6,14},... | collective-permute-start | bytes 1622024 | tf_op jit(solution)/shard_map/move_kv/ppermute | solution.py:237
  14.9 1.2 collective-permute-start.2
  16.0 0.8 copy.15.pos_q
  16.9 0.1 fusion
  17.0 0.1 concatenate.3
  17.1 1.1 broadcast_in_dim.18
  18.2 7.5 %all-to-all-start.1 = ((bf16[8,64,1024]{2,1,0:T(8,128)(2,1)}), bf16[8,64,1024]{2,1,0:T(8,128)(2,1)S(1)}, u32[]{:S(2)}, u32[]{:S(2)}) async-start(bf16[8,64,1024]{2,1,0:T(8,128)(2,1)} %broadcast_in_dim.18), calls=%async_computation.1 | async-start | bytes 2097152 | tf_op jit(solution)/shard_map/move_queries/all_to_all | solution.py:233
  25.7 3.7 %move_weight.1 = (bf16[448,512]{1,0:T(8,128)(2,1)}, bf16[288,512]{1,0:T(8,128)(2,1)}, bf16[288,512]{1,0:T(8,128)(2,1)}, bf16[448,512]{1,0:T(8,128)(2,1)}, bf16[2...) custom-call(s32[1]{0:T(128)} %bitcast.place, ...), custom_call_target="tpu_custom_call" | custom-call | flops 1 | bytes 1 | tf_op jit(solution)/shard_map/move_weight/pallas_call | solution.py:296
  29.4 8.3 %collective-permute-done.1.kv2 = bf16[2,1056,128]{2,1,0:T(8,128)(2,1)S(1)} collective-permute-done((bf16[2,1056,128]{2,1,0:T(8,128)(2,1)}, bf16[2,1056,128]{2,1,0:T(8,128)(2,1)S(1)}, u32[]{:S(2)}, u32[]{:S(2)}) %collective-permute-start.1) | collective-permute-done | bytes 540704 | tf_op jit(solution)/shard_map/move_kv/ppermute | solution.py:237
  37.7 0.7 collective-permute-done.2.kv3
  38.4 0.1 copy-done.6
  38.5 1.9 %collective-permute-start.3 = (bf16[448,512]{1,0:T(8,128)(2,1)}, bf16[448,512]{1,0:T(8,128)(2,1)S(1)}, u32[]{:S(2)}, u32[]{:S(2)}) collective-permute-start(bf16[448,512]{1,0:T(8,128)(2,1)} %get-tuple-element.74), channel_id=1, source_target_pairs={{0,4},{4,8},{8,12},{12,0},{1,5},{5,9},{9,13},{13,1},{2,6},{6,10},{... | collective-permute-start | bytes 1376264 | tf_op jit(solution)/shard_map/move_weight/ppermute | solution.py:237
  40.5 2.5 %collective-permute-start.4 = (bf16[448,512]{1,0:T(8,128)(2,1)}, bf16[448,512]{1,0:T(8,128)(2,1)S(1)}, u32[]{:S(2)}, u32[]{:S(2)}) collective-permute-start(bf16[448,512]{1,0:T(8,128)(2,1)} %get-tuple-element.75), channel_id=1, source_target_pairs={{0,8},{4,12},{8,0},{12,4},{1,9},{5,13},{9,1},{13,5},{2,10},{6,14},... | collective-permute-start | bytes 1376264 | tf_op jit(solution)/shard_map/move_weight/ppermute | solution.py:237
  43.0 0.7 slice_bitcast_fusion.2
  43.7 0.7 slice_bitcast_fusion.1
  44.3 0.7 slice_bitcast_fusion
  45.0 0.1 reshape.26.live
  45.1 1.0 copy-done.5
  46.2 1.0 copy-done.7
  47.2 15.4 %attend.1 = bf16[512,1152]{1,0:T(8,128)(2,1)} custom-call(s32[32]{0:T(128)S(1)} %reshape.26.live, bf16[512,1024]{1,0:T(8,128)(2,1)S(1)} %bitcast.21, bf16[2,1056,128]{2,1,0:T(8,128)(2,1)S(1)} %copy-done.3, bf16[2,1056,128]{2,1,0:T(8,128)(2,1)S(1)} %copy-done.5, bf16[2,1056,128]{2,1,0:T(8,128)(2,1)S(1)} %copy-done.7, ...), custom_call_target="tpu_custom_call" | custom-call | flops 1 | bytes 1 | tf_op jit(solution)/shard_map/attend/pallas_call | solution.py:326
  62.6 0.6 collective-permute-done.4.refs_6_
  63.2 9.9 %all-to-all-start.2 = ((bf16[8,64,1152]{2,1,0:T(8,128)(2,1)}), bf16[8,64,1152]{2,1,0:T(8,128)(2,1)S(1)}, u32[]{:S(2)}, u32[]{:S(2)}) async-start(bf16[8,64,1152]{2,1,0:T(8,128)(2,1)} %bitcast.11), calls=%async_computation.2 | async-start | bytes 2359296 | tf_op jit(solution)/shard_map/move_partials/all_to_all | solution.py:233
  73.1 1.5 %collective-permute-start.6 = (bf16[288,512]{1,0:T(8,128)(2,1)}, bf16[288,512]{1,0:T(8,128)(2,1)}, u32[]{:S(2)}, u32[]{:S(2)}) collective-permute-start(bf16[288,512]{1,0:T(8,128)(2,1)} %get-tuple-element.79), channel_id=1, source_target_pairs={{0,4},{4,8},{8,12},{12,0},{1,5},{5,9},{9,13},{13,1},{2,6},{6,10},{... | collective-permute-start | bytes 884744 | tf_op jit(solution)/shard_map/move_weight/ppermute | solution.py:237
  74.6 0.4 collective-permute-start.7
  75.1 2.0 %collective-permute-start.8 = (bf16[288,512]{1,0:T(8,128)(2,1)}, bf16[288,512]{1,0:T(8,128)(2,1)}, u32[]{:S(2)}, u32[]{:S(2)}) collective-permute-start(bf16[288,512]{1,0:T(8,128)(2,1)} %get-tuple-element.81), channel_id=1, source_target_pairs={{0,12},{4,0},{8,4},{12,8},{1,13},{5,1},{9,5},{13,9},{2,14},{6,2},{... | collective-permute-start | bytes 884744 | tf_op jit(solution)/shard_map/move_weight/ppermute | solution.py:237
  77.1 12.0 %all-to-all-done.2.parts = bf16[8,64,1152]{2,1,0:T(8,128)(2,1)S(1)} async-done(((bf16[8,64,1152]{2,1,0:T(8,128)(2,1)}), bf16[8,64,1152]{2,1,0:T(8,128)(2,1)S(1)}, u32[]{:S(2)}, u32[]{:S(2)}) %all-to-all-start.2) | async-done | bytes 1179680 | tf_op jit(solution)/shard_map/move_partials/all_to_all | solution.py:233
  89.2 2.4 %settle.1 = bf16[8,64,1024]{2,1,0:T(8,128)(2,1)} custom-call(bf16[8,64,1152]{2,1,0:T(8,128)(2,1)S(1)} %all-to-all-done.2.parts), custom_call_target="tpu_custom_call" | custom-call | flops 1 | bytes 1 | tf_op jit(solution)/shard_map/settle/pallas_call | solution.py:345
  91.5 3.8 %all-to-all-start.3 = ((bf16[8,64,1024]{2,1,0:T(8,128)(2,1)}), bf16[8,64,1024]{2,1,0:T(8,128)(2,1)S(1)}, u32[]{:S(2)}, u32[]{:S(2)}) async-start(bf16[8,64,1024]{2,1,0:T(8,128)(2,1)} %settle.1), calls=%async_computation.3 | async-start | bytes 2097152 | tf_op jit(solution)/shard_map/move_attended/all_to_all | solution.py:233
  95.3 2.8 %collective-permute-start.9 = (bf16[288,512]{1,0:T(8,128)(2,1)}, bf16[288,512]{1,0:T(8,128)(2,1)}, u32[]{:S(2)}, u32[]{:S(2)}) collective-permute-start(bf16[288,512]{1,0:T(8,128)(2,1)} %get-tuple-element.88), channel_id=1, source_target_pairs={{0,4},{4,8},{8,12},{12,0},{1,5},{5,9},{9,13},{13,1},{2,6},{6,10},{... | collective-permute-start | bytes 884744 | tf_op jit(solution)/shard_map/move_weight/ppermute | solution.py:237
  98.1 1.8 %collective-permute-start.10 = (bf16[288,512]{1,0:T(8,128)(2,1)}, bf16[288,512]{1,0:T(8,128)(2,1)}, u32[]{:S(2)}, u32[]{:S(2)}) collective-permute-start(bf16[288,512]{1,0:T(8,128)(2,1)} %get-tuple-element.91), channel_id=1, source_target_pairs={{0,8},{4,12},{8,0},{12,4},{1,9},{5,13},{9,1},{13,5},{2,10},{6,14},... | collective-permute-start | bytes 884744 | tf_op jit(solution)/shard_map/move_weight/ppermute | solution.py:237
  99.9 0.7 collective-permute-start.11
  100.6 0.1 pad_add_fusion.1.place
  100.7 2.6 %collective-permute-done.9.refs_5_ = bf16[288,512]{1,0:T(8,128)(2,1)} collective-permute-done((bf16[288,512]{1,0:T(8,128)(2,1)}, bf16[288,512]{1,0:T(8,128)(2,1)}, u32[]{:S(2)}, u32[]{:S(2)}) %collective-permute-start.9) | collective-permute-done | bytes 294944 | tf_op jit(solution)/shard_map/move_weight/ppermute | solution.py:237
  103.3 8.7 %collective-permute-done.10.refs_8_ = bf16[288,512]{1,0:T(8,128)(2,1)} collective-permute-done((bf16[288,512]{1,0:T(8,128)(2,1)}, bf16[288,512]{1,0:T(8,128)(2,1)}, u32[]{:S(2)}, u32[]{:S(2)}) %collective-permute-start.10) | collective-permute-done | bytes 294944 | tf_op jit(solution)/shard_map/move_weight/ppermute | solution.py:237
  112.1 1.0 copy-done.2
  113.0 2.7 %project.3 = bf16[4,2,128,512]{3,2,1,0:T(8,128)(2,1)S(1)} custom-call(s32[2]{0:T(128)S(1)} %pad_add_fusion.1.place, bf16[512,1024]{1,0:T(8,128)(2,1)S(1)} %bitcast.19, bf16[448,512]{1,0:T(8,128)(2,1)S(1)} %copy-done, bf16[288,512]{1,0:T(8,128)(2,1)S(1)} %copy-done.1, bf16[288,512]{1,0:T(8,128)(2,1)S(1)} %copy-done.2, ...), custom_call_target="tpu_custom_call" | custom-call | flops 1 | bytes 1 | tf_op jit(solution)/shard_map/project/pallas_call | solution.py:359
  115.7 2.5 %collective-permute-start.12 = (bf16[4,2,128,512]{3,2,1,0:T(8,128)(2,1)S(1)}, bf16[4,2,128,512]{3,2,1,0:T(8,128)(2,1)S(1)}, u32[]{:S(2)}, u32[]{:S(2)}) collective-permute-start(bf16[4,2,128,512]{3,2,1,0:T(8,128)(2,1)S(1)} %project.3), channel_id=1, source_target_pairs={{0,1},{1,0},{2,3},{3,2},{4,5},{5,4},{6,7},{7,6},{8,9},{9,8},{10,11... | collective-permute-start | bytes 3145736 | tf_op jit(solution)/shard_map/project/ppermute | solution.py:241
  118.2 0.1 pad_add_fusion.place
  118.3 2.7 %project.2 = bf16[4,2,128,512]{3,2,1,0:T(8,128)(2,1)S(1)} custom-call(s32[2]{0:T(128)S(1)} %pad_add_fusion.place, bf16[512,1024]{1,0:T(8,128)(2,1)S(1)} %bitcast.20, bf16[448,512]{1,0:T(8,128)(2,1)S(1)} %copy-done, bf16[288,512]{1,0:T(8,128)(2,1)S(1)} %copy-done.1, bf16[288,512]{1,0:T(8,128)(2,1)S(1)} %copy-done.2, ...), custom_call_target="tpu_custom_call" | custom-call | flops 1 | bytes 1 | tf_op jit(solution)/shard_map/project/pallas_call | solution.py:359
  121.0 0.3 add_convert_fusion
  121.3 19.0 %all_to_all.25 = bf16[8,128,512]{2,1,0:T(8,128)(2,1)S(1)} all-to-all(bf16[8,128,512]{2,1,0:T(8,128)(2,1)S(1)} %bitcast.23), channel_id=1, replica_groups=mesh['z'=4,'x_hi'=2,'y'=4,'x_lo'=2,'core'=2] {'y','x_lo'}, dimensions={0} | all-to-all | bytes 2097152 | tf_op jit(solution)/shard_map/move_terms/all_to_all | solution.py:233
  140.3 0.8 reduce_sum.12
  (30 shorter events, 0.1 us)
Async XLA Ops:
  0.0 16.9 %copy-start.8 = (s32[512]{0:T(512)S(1)}, s32[512]{0:T(512)}, u32[]{:S(2)}) copy-start(s32[512]{0:T(512)} %param.17) | copy-start | bytes 6148
  1.7 9.8 %all-to-all-start = ((bf16[4,16,1024]{2,1,0:T(8,128)(2,1)}), bf16[4,16,1024]{2,1,0:T(8,128)(2,1)S(1)}, u32[]{:S(2)}, u32[]{:S(2)}) async-start(bf16[4,16,1024]{2,1,0:T(8,128)(2,1)} %copy.14), calls=%async_computation | async-start | bytes 262144 | tf_op jit(solution)/shard_map/move_queries/all_to_all | solution.py:233
  11.5 17.9 %collective-permute-start = (bf16[2,1056,128]{2,1,0:T(8,128)(2,1)}, bf16[2,1056,128]{2,1,0:T(8,128)(2,1)S(1)}, u32[]{:S(2)}, u32[]{:S(2)}) collective-permute-start(bf16[2,1056,128]{2,1,0:T(8,128)(2,1)} %get-tuple-element.55), channel_id=1, source_target_pairs={{0,4},{4,8},{8,12},{12,0},{1,5},{5,9},{9,13},{13,1},{2,6},{6,10},{... | collective-permute-start | bytes 1622024 | tf_op jit(solution)/shard_map/move_kv/ppermute | solution.py:237
  12.5 25.3 %collective-permute-start.1 = (bf16[2,1056,128]{2,1,0:T(8,128)(2,1)}, bf16[2,1056,128]{2,1,0:T(8,128)(2,1)S(1)}, u32[]{:S(2)}, u32[]{:S(2)}) collective-permute-start(bf16[2,1056,128]{2,1,0:T(8,128)(2,1)} %get-tuple-element.56), channel_id=1, source_target_pairs={{0,8},{4,12},{8,0},{12,4},{1,9},{5,13},{9,1},{13,5},{2,10},{6,14},... | collective-permute-start | bytes 1622024 | tf_op jit(solution)/shard_map/move_kv/ppermute | solution.py:237
  14.9 23.6 %collective-permute-start.2 = (bf16[2,1056,128]{2,1,0:T(8,128)(2,1)}, bf16[2,1056,128]{2,1,0:T(8,128)(2,1)}, u32[]{:S(2)}, u32[]{:S(2)}) collective-permute-start(bf16[2,1056,128]{2,1,0:T(8,128)(2,1)} %get-tuple-element.57), channel_id=1, source_target_pairs={{0,12},{4,0},{8,4},{12,8},{1,13},{5,1},{9,5},{13,9},{2,14},{6,2},{... | collective-permute-start | bytes 1622024 | tf_op jit(solution)/shard_map/move_kv/ppermute | solution.py:237
  18.2 26.9 %all-to-all-start.1 = ((bf16[8,64,1024]{2,1,0:T(8,128)(2,1)}), bf16[8,64,1024]{2,1,0:T(8,128)(2,1)S(1)}, u32[]{:S(2)}, u32[]{:S(2)}) async-start(bf16[8,64,1024]{2,1,0:T(8,128)(2,1)} %broadcast_in_dim.18), calls=%async_computation.1 | async-start | bytes 2097152 | tf_op jit(solution)/shard_map/move_queries/all_to_all | solution.py:233
  25.7 3.7 %copy-start.3 = (bf16[2,1056,128]{2,1,0:T(8,128)(2,1)S(1)}, bf16[2,1056,128]{2,1,0:T(8,128)(2,1)}, u32[]{:S(2)}) copy-start(bf16[2,1056,128]{2,1,0:T(8,128)(2,1)} %get-tuple-element.54.kv0) | copy-start | bytes 1622020
  29.4 9.0 %copy-start.4 = (bf16[2,1056,128]{2,1,0:T(8,128)(2,1)}, bf16[2,1056,128]{2,1,0:T(8,128)(2,1)S(1)}, u32[]{:S(2)}) copy-start(bf16[2,1056,128]{2,1,0:T(8,128)(2,1)S(1)} %collective-permute-done.kv1) | copy-start | bytes 1622020
  37.7 0.8 copy-start.6
  38.5 24.1 %collective-permute-start.3 = (bf16[448,512]{1,0:T(8,128)(2,1)}, bf16[448,512]{1,0:T(8,128)(2,1)S(1)}, u32[]{:S(2)}, u32[]{:S(2)}) collective-permute-start(bf16[448,512]{1,0:T(8,128)(2,1)} %get-tuple-element.74), channel_id=1, source_target_pairs={{0,4},{4,8},{8,12},{12,0},{1,5},{5,9},{9,13},{13,1},{2,6},{6,10},{... | collective-permute-start | bytes 1376264 | tf_op jit(solution)/shard_map/move_weight/ppermute | solution.py:237
  40.5 22.7 %collective-permute-start.4 = (bf16[448,512]{1,0:T(8,128)(2,1)}, bf16[448,512]{1,0:T(8,128)(2,1)S(1)}, u32[]{:S(2)}, u32[]{:S(2)}) collective-permute-start(bf16[448,512]{1,0:T(8,128)(2,1)} %get-tuple-element.75), channel_id=1, source_target_pairs={{0,8},{4,12},{8,0},{12,4},{1,9},{5,13},{9,1},{13,5},{2,10},{6,14},... | collective-permute-start | bytes 1376264 | tf_op jit(solution)/shard_map/move_weight/ppermute | solution.py:237
  43.0 20.2 %collective-permute-start.5 = (bf16[448,512]{1,0:T(8,128)(2,1)}, bf16[448,512]{1,0:T(8,128)(2,1)S(1)}, u32[]{:S(2)}, u32[]{:S(2)}) collective-permute-start(bf16[448,512]{1,0:T(8,128)(2,1)} %get-tuple-element.76), channel_id=1, source_target_pairs={{0,12},{4,0},{8,4},{12,8},{1,13},{5,1},{9,5},{13,9},{2,14},{6,2},{... | collective-permute-start | bytes 1376264 | tf_op jit(solution)/shard_map/move_weight/ppermute | solution.py:237
  45.1 1.1 copy-start.5
  46.2 1.0 copy-start.7
  63.2 26.0 %all-to-all-start.2 = ((bf16[8,64,1152]{2,1,0:T(8,128)(2,1)}), bf16[8,64,1152]{2,1,0:T(8,128)(2,1)S(1)}, u32[]{:S(2)}, u32[]{:S(2)}) async-start(bf16[8,64,1152]{2,1,0:T(8,128)(2,1)} %bitcast.11), calls=%async_computation.2 | async-start | bytes 2359296 | tf_op jit(solution)/shard_map/move_partials/all_to_all | solution.py:233
  73.1 39.0 %copy-start = (bf16[448,512]{1,0:T(8,128)(2,1)S(1)}, bf16[448,512]{1,0:T(8,128)(2,1)}, u32[]{:S(2)}) copy-start(bf16[448,512]{1,0:T(8,128)(2,1)} %get-tuple-element.83.refs_0_) | copy-start | bytes 1376260
  73.1 39.0 %copy-start.1 = (bf16[288,512]{1,0:T(8,128)(2,1)S(1)}, bf16[288,512]{1,0:T(8,128)(2,1)}, u32[]{:S(2)}) copy-start(bf16[288,512]{1,0:T(8,128)(2,1)} %get-tuple-element.84.refs_1_) | copy-start | bytes 884740
  73.1 18.4 %collective-permute-start.6 = (bf16[288,512]{1,0:T(8,128)(2,1)}, bf16[288,512]{1,0:T(8,128)(2,1)}, u32[]{:S(2)}, u32[]{:S(2)}) collective-permute-start(bf16[288,512]{1,0:T(8,128)(2,1)} %get-tuple-element.79), channel_id=1, source_target_pairs={{0,4},{4,8},{8,12},{12,0},{1,5},{5,9},{9,13},{13,1},{2,6},{6,10},{... | collective-permute-start | bytes 884744 | tf_op jit(solution)/shard_map/move_weight/ppermute | solution.py:237
  74.6 16.9 %collective-permute-start.7 = (bf16[288,512]{1,0:T(8,128)(2,1)}, bf16[288,512]{1,0:T(8,128)(2,1)}, u32[]{:S(2)}, u32[]{:S(2)}) collective-permute-start(bf16[288,512]{1,0:T(8,128)(2,1)} %get-tuple-element.80), channel_id=1, source_target_pairs={{0,8},{4,12},{8,0},{12,4},{1,9},{5,13},{9,1},{13,5},{2,10},{6,14},... | collective-permute-start | bytes 884744 | tf_op jit(solution)/shard_map/move_weight/ppermute | solution.py:237
  75.1 16.4 %collective-permute-start.8 = (bf16[288,512]{1,0:T(8,128)(2,1)}, bf16[288,512]{1,0:T(8,128)(2,1)}, u32[]{:S(2)}, u32[]{:S(2)}) collective-permute-start(bf16[288,512]{1,0:T(8,128)(2,1)} %get-tuple-element.81), channel_id=1, source_target_pairs={{0,12},{4,0},{8,4},{12,8},{1,13},{5,1},{9,5},{13,9},{2,14},{6,2},{... | collective-permute-start | bytes 884744 | tf_op jit(solution)/shard_map/move_weight/ppermute | solution.py:237
  91.5 8.4 %copy-start.9 = (bf16[288,512]{1,0:T(8,128)(2,1)S(1)}, bf16[288,512]{1,0:T(8,128)(2,1)}, u32[]{:S(2)}) copy-start(bf16[288,512]{1,0:T(8,128)(2,1)} %get-tuple-element.94) | copy-start | bytes 884740
  91.5 20.5 %all-to-all-start.3 = ((bf16[8,64,1024]{2,1,0:T(8,128)(2,1)}), bf16[8,64,1024]{2,1,0:T(8,128)(2,1)S(1)}, u32[]{:S(2)}, u32[]{:S(2)}) async-start(bf16[8,64,1024]{2,1,0:T(8,128)(2,1)} %settle.1), calls=%async_computation.3 | async-start | bytes 2097152 | tf_op jit(solution)/shard_map/move_attended/all_to_all | solution.py:233
  95.3 8.0 %collective-permute-start.9 = (bf16[288,512]{1,0:T(8,128)(2,1)}, bf16[288,512]{1,0:T(8,128)(2,1)}, u32[]{:S(2)}, u32[]{:S(2)}) collective-permute-start(bf16[288,512]{1,0:T(8,128)(2,1)} %get-tuple-element.88), channel_id=1, source_target_pairs={{0,4},{4,8},{8,12},{12,0},{1,5},{5,9},{9,13},{13,1},{2,6},{6,10},{... | collective-permute-start | bytes 884744 | tf_op jit(solution)/shard_map/move_weight/ppermute | solution.py:237
  98.1 13.9 %collective-permute-start.10 = (bf16[288,512]{1,0:T(8,128)(2,1)}, bf16[288,512]{1,0:T(8,128)(2,1)}, u32[]{:S(2)}, u32[]{:S(2)}) collective-permute-start(bf16[288,512]{1,0:T(8,128)(2,1)} %get-tuple-element.91), channel_id=1, source_target_pairs={{0,8},{4,12},{8,0},{12,4},{1,9},{5,13},{9,1},{13,5},{2,10},{6,14},... | collective-permute-start | bytes 884744 | tf_op jit(solution)/shard_map/move_weight/ppermute | solution.py:237
  99.9 12.1 %collective-permute-start.11 = (bf16[288,512]{1,0:T(8,128)(2,1)S(1)}, bf16[288,512]{1,0:T(8,128)(2,1)}, u32[]{:S(2)}, u32[]{:S(2)}) collective-permute-start(bf16[288,512]{1,0:T(8,128)(2,1)S(1)} %copy-done.9), channel_id=1, source_target_pairs={{0,12},{4,0},{8,4},{12,8},{1,13},{5,1},{9,5},{13,9},{2,14},{6,2},{... | collective-permute-start | bytes 884744 | tf_op jit(solution)/shard_map/move_weight/ppermute | solution.py:237
  112.1 1.0 copy-start.2
  115.7 5.3 %collective-permute-start.12 = (bf16[4,2,128,512]{3,2,1,0:T(8,128)(2,1)S(1)}, bf16[4,2,128,512]{3,2,1,0:T(8,128)(2,1)S(1)}, u32[]{:S(2)}, u32[]{:S(2)}) collective-permute-start(bf16[4,2,128,512]{3,2,1,0:T(8,128)(2,1)S(1)} %project.3), channel_id=1, source_target_pairs={{0,1},{1,0},{2,3},{3,2},{4,5},{5,4},{6,7},{7,6},{8,9},{9,8},{10,11... | collective-permute-start | bytes 3145736 | tf_op jit(solution)/shard_map/project/ppermute | solution.py:241

commit v5 on v4

--- a/solution.py
+++ b/solution.py
@@ -33,7 +33,7 @@
     return pltpu.CompilerParams(vmem_limit_bytes=mib << 20)
 
 
-def pack_kernel(place, valid_len, span_ids, offset, keys_in, values_in, new_keys_in, new_values_in, *refs):
+def pack_kernel(place, valid_len, span_ids, offset, pos_ids, keys_in, values_in, new_keys_in, new_values_in, *refs):
     outs, (keys, values, new_keys, new_values, heads, sems) = refs[:4], refs[4:]
     copies = [
         pltpu.make_async_copy(source, target, sems.at[i])
@@ -54,6 +54,10 @@
     counts = jnp.zeros((16, HD), F32)
     for s in range(slots):
         counts = jnp.where(lane_id == s, live[s].astype(F32), counts)
+    for j in range(fresh):
+        position = pos_ids[place[1] * fresh + j]
+        counts = jnp.where(lane_id == fresh + j, (position >> 4).astype(F32), counts)
+        counts = jnp.where(lane_id == 2 * fresh + j, (position & 15).astype(F32), counts)
     for copy in copies:
         copy.wait()
     for head in range(2):
@@ -73,11 +77,14 @@
         out[...] = heads[lax.rem(place[0] + k, 4) // 2]
 
 
-def attend_kernel(live, queries, kv0, kv1, kv2, kv3, pos_q, pos_n, out, kc, vc, top, acc):
+def attend_kernel(queries, kv0, kv1, kv2, kv3, pos_q, out, kc, vc, top, acc, held, table, live, sems):
     sources = (kv0, kv1, kv2, kv3)
-    slots = live.shape[0] // len(sources)
-    rows = slots * SPAN
-    fresh = kv0.shape[1] - rows - 16
+    copies = [pltpu.make_async_copy(kv, held.at[i], sems.at[i]) for i, kv in enumerate(sources)]
+    for copy in copies:
+        copy.start()
+    fresh = 16
+    rows = kv0.shape[1] - 2 * fresh
+    slots = rows // SPAN
     heads = queries.shape[1] // HD
     tokens = queries.shape[0]
     row_id = lax.broadcasted_iota(jnp.int32, (SPAN, HD), 0)
@@ -86,15 +93,31 @@
     def rounded(count):
         return ((count + 15) // 16) * 16
 
+    for copy in copies:
+        copy.wait()
+    notes = [held[i, 0, rows + fresh :, :].astype(F32) for i in range(len(sources))]
+    for i, note in enumerate(notes):
+        table[i] = note[:8].astype(jnp.int32)
+    counts = pltpu.make_async_copy(table, live, sems.at[len(sources)])
+    counts.start()
+    lane = lax.broadcasted_iota(jnp.int32, (8, HD), 1)
+    pos_fresh = jnp.full((8, HD), -1.0, F32)
+    for i, note in enumerate(notes):
+        high = pltpu.roll(note[:8], (i - 1) * fresh % HD, 1)
+        low = pltpu.roll(note[:8], (i - 2) * fresh % HD, 1)
+        pos_fresh = jnp.where(lane // fresh == i, high * 16.0 + low, pos_fresh)
+    pos_column = jnp.transpose(jnp.broadcast_to(pos_q[...].astype(F32), (HD, tokens)))
+    counts.wait()
     place = jnp.int32(start)
-    for i, kv in enumerate(sources):
+    for i in range(len(sources)):
+        kv = held.at[i]
         target = slice(i * fresh, (i + 1) * fresh)
         kc[target, :] = kv[0, rows : rows + fresh, :]
         vc[target, :HD] = kv[1, rows : rows + fresh, :]
         vc[target, HD:] = jnp.ones((fresh, HD), BF16)
 
         def gather_slot(s, at, kv=kv, i=i):
-            count = live[i * slots + s]
+            count = live[i, 0, s]
             source = pl.ds(pl.multiple_of(s * SPAN, SPAN), SPAN)
             target = pl.ds(pl.multiple_of(at, 16), SPAN)
             kc[target, :] = kv[0, source, :]
@@ -111,9 +134,11 @@
     blocks = (place + KEY_BLOCK - 1) // KEY_BLOCK
 
     lane_id = lax.broadcasted_iota(jnp.int32, (tokens, HD), 1)
-    key_id = lax.broadcasted_iota(jnp.int32, (1, KEY_BLOCK), 1)
-    seen = jnp.where(key_id < place, pos_n[...], tokens) <= pos_q[...]
     lanes = [slice(j * HD, (j + 1) * HD) for j in range(KEY_BLOCK // HD)]
+    pos_key = [
+        jnp.where(lane[:1] + j * HD < place, pos_fresh[:1] if j == 0 else -1.0, float(tokens))
+        for j in range(KEY_BLOCK // HD)
+    ]
 
     def head_cols(h):
         return slice(h * HD, (h + 1) * HD)
@@ -131,7 +156,7 @@
         return jnp.dot(p, vc[part, :], preferred_element_type=F32)
 
     def begin(h, part, s):
-        s = jnp.where(seen, s, FILL)
+        s = jnp.concatenate([jnp.where(p <= pos_column, s[:, g], FILL) for p, g in zip(pos_key, lanes)], axis=1)
         m = rounded_max(s)
         top[h] = m
         acc[h] = sums(s, m, part)
@@ -174,22 +199,20 @@
 def settle_kernel(parts, out):
     groups, tokens, width = parts.shape
     heads = width // HD - 1
+    lane_id = lax.broadcasted_iota(jnp.int32, (tokens, HD), 1)
     notes = [parts[g, :, heads * HD :].astype(F32) for g in range(groups)]
-    highest = notes[0]
-    for g in range(1, groups):
-        highest = jnp.maximum(highest, notes[g])
-    factors = [jnp.exp2(notes[g] - highest) for g in range(groups)]
+    highest = functools.reduce(jnp.maximum, notes)
+    factors = [jnp.exp2(jnp.where(lane_id < heads, n - highest, 0.0)) for n in notes]
+    total = 0.0
+    for factor, n in zip(factors, notes):
+        total += factor * (pltpu.roll(n, HD - heads, 1) + pltpu.roll(n, HD - 2 * heads, 1))
+    shares = [factor / jnp.where(lane_id < heads, total, 1.0) for factor in factors]
     for h in range(heads):
         cols = slice(h * HD, (h + 1) * HD)
-        numerator = jnp.zeros((tokens, HD), F32)
-        total = jnp.zeros((tokens, 1), F32)
+        attended = 0.0
         for g in range(groups):
-            factor = factors[g][:, h : h + 1]
-            numerator += factor * parts[g, :, cols].astype(F32)
-            total += factor * (
-                notes[g][:, heads + h : heads + h + 1] + notes[g][:, 2 * heads + h : 2 * heads + h + 1]
-            )
-        attended = (numerator / total).astype(BF16)
+            attended += shares[g][:, h : h + 1] * parts[g, :, cols].astype(F32)
+        attended = attended.astype(BF16)
         for g in range(out.shape[0]):
             out[g, :, cols] = attended
 
@@ -223,8 +246,11 @@
     rows = jnp.concatenate([attended[p, :] for p in picked], axis=0)
     for k in range(4):
         target = lax.rem(place[0] + 4 - k, 4)
-        weight = jnp.concatenate([w[...] for w in weights[k * PIECES : (k + 1) * PIECES]], axis=0)
-        term = jnp.dot(rows, weight, preferred_element_type=F32).astype(BF16)
+        term, start = 0.0, 0
+        for w in weights[k * PIECES : (k + 1) * PIECES]:
+            term += jnp.dot(rows[:, start : start + w.shape[0]], w[...], preferred_element_type=F32)
+            start += w.shape[0]
+        term = term.astype(BF16)
         for r in range(out.shape[1]):
             out[target, r] = term[r * size : (r + 1) * size]
 
@@ -268,7 +294,7 @@
         packets = pl.pallas_call(
             pack_kernel,
             out_shape=[packet] * 4,
-            in_specs=[SMEM] * 4 + [ANY] * 4,
+            in_specs=[SMEM] * 5 + [ANY] * 4,
             out_specs=[VMEM] * 4,
             scratch_shapes=[
                 pltpu.VMEM(cache_keys.shape, BF16),
@@ -280,7 +306,7 @@
             ],
             compiler_params=grant(56),
             cost_estimate=TINY,
-        )(place, valid_len, span_ids, offset, cache_keys, cache_values, new_keys, new_values)
+        )(jnp.stack([y, group * 4 + y]).astype(jnp.int32), valid_len, span_ids, offset, pos_ids, cache_keys, cache_values, new_keys, new_values)
     with jax.named_scope("move_queries"):
         mine = swap(queries.reshape(fresh, 4, quarter).transpose(1, 0, 2), "y")
         mine, packets = lax.optimization_barrier((mine, packets))
@@ -288,11 +314,10 @@
         mine = swap(jnp.broadcast_to(mine[None], (groups,) + mine.shape), ("z", "x_hi")).reshape(tokens, quarter)
     with jax.named_scope("move_kv"):
         kv = [packets[0]] + [along_y(packets[k], k) for k in range(1, 4)]
-        all_live = jnp.stack([packet[0, rows + fresh, :slots] for packet in kv]).astype(jnp.int32).reshape(-1)
 
     columns = out_weight.shape[1]
     with jax.named_scope("move_weight"):
-        sizes = (448, 288, 288)
+        sizes = (448, 320, 256)
         chunks = pl.pallas_call(
             cut_kernel,
             out_shape=[jax.ShapeDtypeStruct((size, columns), BF16) for size in sizes * 4],
@@ -307,18 +332,12 @@
             cost_estimate=TINY,
         )(place, lax.optimization_barrier((out_weight, packets))[0])
 
-        def pieces(j, after):
-            ready, _ = lax.optimization_barrier(([chunks[k * PIECES + j] for k in range(4)], after))
+        def pieces(j):
+            ready, _ = lax.optimization_barrier(([chunks[k * PIECES + j] for k in range(4)], kv[1:3]))
             return [ready[0]] + [along_y(ready[k], k) for k in range(1, 4)]
 
-        weights = [pieces(j, kv) for j in range(PIECES)]
+        weights = [pieces(j) for j in range(PIECES)]
         mine, chunks = lax.optimization_barrier((mine, chunks))
-
-    pos_n = [
-        lax.dynamic_slice_in_dim(pos_ids, (group * 4 + lax.rem(y + 4 - k, 4)) * fresh, fresh) for k in range(4)
-    ]
-    pos_n = jnp.concatenate(pos_n + [jnp.full((KEY_BLOCK - 4 * fresh,), -1, jnp.int32)])[None]
-    pos_q = pos_ids[:, None]
 
     capacity = 4 * (rows + fresh) + KEY_BLOCK
     heads = quarter // HD
@@ -326,17 +345,21 @@
         partial = pl.pallas_call(
             attend_kernel,
             out_shape=jax.ShapeDtypeStruct((tokens, quarter + HD), BF16),
-            in_specs=[SMEM] + [VMEM] * 7,
+            in_specs=[VMEM] + [ANY] * 4 + [VMEM],
             out_specs=VMEM,
             scratch_shapes=[
                 pltpu.VMEM((capacity, HD), BF16),
                 pltpu.VMEM((capacity, 2 * HD), BF16),
                 pltpu.VMEM((heads, tokens, HD), F32),
                 pltpu.VMEM((heads, tokens, 2 * HD), F32),
+                pltpu.VMEM((4,) + packet.shape, BF16),
+                pltpu.VMEM((4, 8, HD), jnp.int32),
+                pltpu.SMEM((4, 8, HD), jnp.int32),
+                pltpu.SemaphoreType.DMA((5,)),
             ],
-            compiler_params=grant(40),
+            compiler_params=grant(24),
             cost_estimate=TINY,
-        )(all_live, mine, *kv, pos_q, pos_n)
+        )(mine, *kv, pos_ids[None])
 
     with jax.named_scope("move_partials"):
         partial, weights[0] = lax.optimization_barrier((partial, weights[0]))

time: 143 us -> 142 us (level)
  Pallas kernels: 30.3 us -> 37.2 us
  waiting for transfers between devices: 33.6 us -> 28.9 us
  local copies, waits for them, and re-layouts: 9.09 us -> 6.29 us
  starting transfers between devices: 47 us -> 44.8 us
  blocking collectives: 19 us -> 21 us
    pallas_call x1, Pallas kernels: 15.4 us -> 22 us  [shards(): pl.pallas_call(attend_kernel, out_shape=jax.ShapeDtypeStruct((tokens, qua...]
    all_to_all x4, starting transfers between devices: 26.2 us -> 23 us  [swap(): return lax.all_to_all(x, axes, split_axis=0, concat_axis=0, tiled=False)]
    ppermute x12, waiting for transfers between devices: 20.9 us -> 18 us  [along_y(): return lax.ppermute(x, 'y', [(i, (i + distance) % 4) for i in range(4)])]
    squeeze x4 -> x0, local copies, waits for them, and re-layouts: 2.01 us -> none  [shards(): jnp.stack([packet[0, rows + fresh, :slots] for packet in kv])]
    all_to_all x1, blocking collectives: 19 us -> 21 us  [swap(): return lax.all_to_all(x, axes, split_axis=0, concat_axis=0, tiled=False)]
    all_to_all x4, waiting for transfers between devices: 12.7 us -> 10.9 us  [swap(): return lax.all_to_all(x, axes, split_axis=0, concat_axis=0, tiled=False)]
    unnamed x20 -> x16, local copies, waits for them, and re-layouts: 3.2 us -> 3.47 us
  transfers between devices with their start and end apart: 17 -> 17, of which waited for: 7 -> 4; matrix products, arithmetic and copies ran while one was open for 3% -> 1% of each run, Pallas kernels for 20% -> 24%
where the time goes in v5:
time: 142 us; the launch traced here: 141 us
  starting transfers between devices  44.8 us (32%)
  Pallas kernels  37.2 us (26%)
  waiting for transfers between devices  28.9 us (20%)
  blocking collectives  21 us (15%)
  local copies, waits for them, and re-layouts  6.29 us (4%)
  other arithmetic  1.91 us (1%)
    all_to_all x4, starting transfers between devices, swap(): return lax.all_to_all(x, axes, split_axis=0, concat_axis=0, tiled=False)  23 us
    pallas_call x1, Pallas kernels, shards(): pl.pallas_call(attend_kernel, out_shape=jax.ShapeDtypeStruct((tokens, qua...  22 us
    all_to_all x1, blocking collectives, swap(): return lax.all_to_all(x, axes, split_axis=0, concat_axis=0, tiled=False)  21 us
    ppermute x12, waiting for transfers between devices, along_y(): return lax.ppermute(x, 'y', [(i, (i + distance) % 4) for i in range(4)])  18 us
    ppermute x12, starting transfers between devices, along_y(): return lax.ppermute(x, 'y', [(i, (i + distance) % 4) for i in range(4)])  18 us
    all_to_all x4, waiting for transfers between devices, swap(): return lax.all_to_all(x, axes, split_axis=0, concat_axis=0, tiled=False)  10.9 us
    pallas_call x2, Pallas kernels, project(): pl.pallas_call(project_kernel, out_shape=jax.ShapeDtypeStruct((4, 2, toke...  5.96 us
    ppermute x1, starting transfers between devices, to_other(): return lax.ppermute(x, axis, [(0, 1), (1, 0)])  3.88 us
  transfers between devices with their start and end apart: 17, of which 4 were waited for; matrix products, arithmetic and copies ran while one was open for 1% of the time, Pallas kernels for 24%

profile of v5, /device:TPU:1, one launch (start us, length us, event | category | flops | bytes accessed | tf_op | source)
XLA Modules:
  0.0 140.9 jit_solution(1641939995420754659)
XLA Ops:
  0.0 1.0 reshape.17
  1.0 0.7 copy.12
  1.7 5.0 %all-to-all-start = ((bf16[4,16,1024]{2,1,0:T(8,128)(2,1)}), bf16[4,16,1024]{2,1,0:T(8,128)(2,1)S(1)}, u32[]{:S(2)}, u32[]{:S(2)}) async-start(bf16[4,16,1024]{2,1,0:T(8,128)(2,1)} %copy.12), calls=%async_computation | async-start | bytes 262144 | tf_op jit(solution)/shard_map/move_queries/all_to_all | solution.py:259
  7.3 0.7 pad_add_fusion.1.place
  8.0 3.6 %pack.1 = (bf16[2,1056,128]{2,1,0:T(8,128)(2,1)}, bf16[2,1056,128]{2,1,0:T(8,128)(2,1)}, bf16[2,1056,128]{2,1,0:T(8,128)(2,1)}, bf16[2,1056,128]{2,1,0:T(8,128)(2,1)}) custom-call(s32[2]{0:T(128)} %pad_add_fusion.1.place, s32[8]{0:T(128)} %valid_len.1, s32[8]{0:T(128)} %span_ids.1, s32[1]{0:T(128)S(6)} %copy.13.offset, s32[512]{0:T(512)} %pos_ids.1, ...), custom_call_target="tpu_custom_call" | custom-call | flops 1 | bytes 1 | tf_op jit(solution)/shard_map/pack/pallas_call | solution.py:294
  11.6 0.0 all-to-all-done
  11.6 1.5 %collective-permute-start = (bf16[2,1056,128]{2,1,0:T(8,128)(2,1)}, bf16[2,1056,128]{2,1,0:T(8,128)(2,1)S(1)}, u32[]{:S(2)}, u32[]{:S(2)}) collective-permute-start(bf16[2,1056,128]{2,1,0:T(8,128)(2,1)} %get-tuple-element.56), channel_id=1, source_target_pairs={{0,4},{4,8},{8,12},{12,0},{1,5},{5,9},{9,13},{13,1},{2,6},{6,10},{... | collective-permute-start | bytes 1622024 | tf_op jit(solution)/shard_map/move_kv/ppermute | solution.py:263
  13.2 2.4 %collective-permute-start.1 = (bf16[2,1056,128]{2,1,0:T(8,128)(2,1)}, bf16[2,1056,128]{2,1,0:T(8,128)(2,1)S(1)}, u32[]{:S(2)}, u32[]{:S(2)}) collective-permute-start(bf16[2,1056,128]{2,1,0:T(8,128)(2,1)} %get-tuple-element.57), channel_id=1, source_target_pairs={{0,8},{4,12},{8,0},{12,4},{1,9},{5,13},{9,1},{13,5},{2,10},{6,14},... | collective-permute-start | bytes 1622024 | tf_op jit(solution)/shard_map/move_kv/ppermute | solution.py:263
  15.6 1.1 broadcast_in_dim.12
  16.7 7.5 %all-to-all-start.1 = ((bf16[8,64,1024]{2,1,0:T(8,128)(2,1)}), bf16[8,64,1024]{2,1,0:T(8,128)(2,1)S(1)}, u32[]{:S(2)}, u32[]{:S(2)}) async-start(bf16[8,64,1024]{2,1,0:T(8,128)(2,1)} %broadcast_in_dim.12), calls=%async_computation.1 | async-start | bytes 2097152 | tf_op jit(solution)/shard_map/move_queries/all_to_all | solution.py:259
  24.2 1.3 collective-permute-start.2
  25.5 3.6 %move_weight.1 = (bf16[448,512]{1,0:T(8,128)(2,1)}, bf16[320,512]{1,0:T(8,128)(2,1)}, bf16[256,512]{1,0:T(8,128)(2,1)}, bf16[448,512]{1,0:T(8,128)(2,1)}, bf16[3...) custom-call(s32[1]{0:T(128)} %bitcast.place, ...), custom_call_target="tpu_custom_call" | custom-call | flops 1 | bytes 1 | tf_op jit(solution)/shard_map/move_weight/pallas_call | solution.py:321
  29.1 9.3 %collective-permute-done.1.kv2 = bf16[2,1056,128]{2,1,0:T(8,128)(2,1)S(1)} collective-permute-done((bf16[2,1056,128]{2,1,0:T(8,128)(2,1)}, bf16[2,1056,128]{2,1,0:T(8,128)(2,1)S(1)}, u32[]{:S(2)}, u32[]{:S(2)}) %collective-permute-start.1) | collective-permute-done | bytes 540704 | tf_op jit(solution)/shard_map/move_kv/ppermute | solution.py:263
  38.4 0.8 copy-done.4
  39.2 0.6 collective-permute-start.4
  39.8 2.1 %collective-permute-start.5 = (bf16[448,512]{1,0:T(8,128)(2,1)}, bf16[448,512]{1,0:T(8,128)(2,1)S(1)}, u32[]{:S(2)}, u32[]{:S(2)}) collective-permute-start(bf16[448,512]{1,0:T(8,128)(2,1)} %get-tuple-element.76), channel_id=1, source_target_pairs={{0,12},{4,0},{8,4},{12,8},{1,13},{5,1},{9,5},{13,9},{2,14},{6,2},{... | collective-permute-start | bytes 1376264 | tf_op jit(solution)/shard_map/move_weight/ppermute | solution.py:263
  41.9 0.0 all-to-all-done.1
  41.9 0.0 collective-permute-done.2.kv3
  41.9 1.0 copy-done.5
  43.0 0.7 copy-done.6
  43.6 22.0 %attend.1 = bf16[512,1152]{1,0:T(8,128)(2,1)} custom-call(bf16[512,1024]{1,0:T(8,128)(2,1)S(1)} %bitcast.13, bf16[2,1056,128]{2,1,0:T(8,128)(2,1)S(1)} %copy-done.3, bf16[2,1056,128]{2,1,0:T(8,128)(2,1)S(1)} %collective-permute-done.kv1, bf16[2,1056,128]{2,1,0:T(8,128)(2,1)S(1)} %copy-done.5, bf16[2,1056,128]{2,1,0:T(8,128)(2,1)} %collective-permute-done.2.kv3, ...), custom_call_target="tpu_custom_call" | custom-call | flops 1 | bytes 1 | tf_op jit(solution)/shard_map/attend/pallas_call | solution.py:345
  65.7 0.0 collective-permute-done.5.refs_9_
  65.7 5.1 %all-to-all-start.2 = ((bf16[8,64,1152]{2,1,0:T(8,128)(2,1)}), bf16[8,64,1152]{2,1,0:T(8,128)(2,1)S(1)}, u32[]{:S(2)}, u32[]{:S(2)}) async-start(bf16[8,64,1152]{2,1,0:T(8,128)(2,1)} %bitcast.7), calls=%async_computation.2 | async-start | bytes 2359296 | tf_op jit(solution)/shard_map/move_partials/all_to_all | solution.py:259
  70.8 0.7 collective-permute-start.6
  71.4 2.6 %collective-permute-start.7 = (bf16[320,512]{1,0:T(8,128)(2,1)}, bf16[320,512]{1,0:T(8,128)(2,1)}, u32[]{:S(2)}, u32[]{:S(2)}) collective-permute-start(bf16[320,512]{1,0:T(8,128)(2,1)} %get-tuple-element.80), channel_id=1, source_target_pairs={{0,8},{4,12},{8,0},{12,4},{1,9},{5,13},{9,1},{13,5},{2,10},{6,14},... | collective-permute-start | bytes 983048 | tf_op jit(solution)/shard_map/move_weight/ppermute | solution.py:263
  74.0 1.3 collective-permute-start.8
  75.3 10.9 %all-to-all-done.2.parts = bf16[8,64,1152]{2,1,0:T(8,128)(2,1)S(1)} async-done(((bf16[8,64,1152]{2,1,0:T(8,128)(2,1)}), bf16[8,64,1152]{2,1,0:T(8,128)(2,1)S(1)}, u32[]{:S(2)}, u32[]{:S(2)}) %all-to-all-start.2) | async-done | bytes 1179680 | tf_op jit(solution)/shard_map/move_partials/all_to_all | solution.py:259
  86.2 1.9 %settle.1 = bf16[8,64,1024]{2,1,0:T(8,128)(2,1)} custom-call(bf16[8,64,1152]{2,1,0:T(8,128)(2,1)S(1)} %all-to-all-done.2.parts), custom_call_target="tpu_custom_call" | custom-call | flops 1 | bytes 1 | tf_op jit(solution)/shard_map/settle/pallas_call | solution.py:368
  88.1 0.0 collective-permute-done.6.refs_4_
  88.1 0.0 collective-permute-done.7.refs_7_
  88.1 5.4 %all-to-all-start.3 = ((bf16[8,64,1024]{2,1,0:T(8,128)(2,1)}), bf16[8,64,1024]{2,1,0:T(8,128)(2,1)S(1)}, u32[]{:S(2)}, u32[]{:S(2)}) async-start(bf16[8,64,1024]{2,1,0:T(8,128)(2,1)} %settle.1), calls=%async_computation.3 | async-start | bytes 2097152 | tf_op jit(solution)/shard_map/move_attended/all_to_all | solution.py:259
  93.5 3.1 %collective-permute-start.9 = (bf16[256,512]{1,0:T(8,128)(2,1)}, bf16[256,512]{1,0:T(8,128)(2,1)}, u32[]{:S(2)}, u32[]{:S(2)}) collective-permute-start(bf16[256,512]{1,0:T(8,128)(2,1)} %get-tuple-element.88), channel_id=1, source_target_pairs={{0,4},{4,8},{8,12},{12,0},{1,5},{5,9},{9,13},{13,1},{2,6},{6,10},{... | collective-permute-start | bytes 786440 | tf_op jit(solution)/shard_map/move_weight/ppermute | solution.py:263
  96.6 1.5 %collective-permute-start.10 = (bf16[256,512]{1,0:T(8,128)(2,1)}, bf16[256,512]{1,0:T(8,128)(2,1)}, u32[]{:S(2)}, u32[]{:S(2)}) collective-permute-start(bf16[256,512]{1,0:T(8,128)(2,1)} %get-tuple-element.91), channel_id=1, source_target_pairs={{0,8},{4,12},{8,0},{12,4},{1,9},{5,13},{9,1},{13,5},{2,10},{6,14},... | collective-permute-start | bytes 786440 | tf_op jit(solution)/shard_map/move_weight/ppermute | solution.py:263
  98.1 1.0 collective-permute-start.11
  99.1 0.1 pad_add_fusion.2.place
  99.2 1.8 %collective-permute-done.9.refs_5_ = bf16[256,512]{1,0:T(8,128)(2,1)} collective-permute-done((bf16[256,512]{1,0:T(8,128)(2,1)}, bf16[256,512]{1,0:T(8,128)(2,1)}, u32[]{:S(2)}, u32[]{:S(2)}) %collective-permute-start.9) | collective-permute-done | bytes 262176 | tf_op jit(solution)/shard_map/move_weight/ppermute | solution.py:263
  101.0 6.8 %collective-permute-done.10.refs_8_ = bf16[256,512]{1,0:T(8,128)(2,1)} collective-permute-done((bf16[256,512]{1,0:T(8,128)(2,1)}, bf16[256,512]{1,0:T(8,128)(2,1)}, u32[]{:S(2)}, u32[]{:S(2)}) %collective-permute-start.10) | collective-permute-done | bytes 262176 | tf_op jit(solution)/shard_map/move_weight/ppermute | solution.py:263
  107.9 0.0 collective-permute-done.11.refs_11_
  107.9 0.0 all-to-all-done.3
  107.9 0.9 copy-done.2
  108.8 3.0 %project.3 = bf16[4,2,128,512]{3,2,1,0:T(8,128)(2,1)S(1)} custom-call(s32[2]{0:T(128)S(1)} %pad_add_fusion.2.place, bf16[512,1024]{1,0:T(8,128)(2,1)S(1)} %bitcast.11, bf16[448,512]{1,0:T(8,128)(2,1)S(1)} %copy-done, bf16[320,512]{1,0:T(8,128)(2,1)S(1)} %copy-done.1, bf16[256,512]{1,0:T(8,128)(2,1)S(1)} %copy-done.2, ...), custom_call_target="tpu_custom_call" | custom-call | flops 1 | bytes 1 | tf_op jit(solution)/shard_map/project/pallas_call | solution.py:382
  111.8 3.9 %collective-permute-start.12 = (bf16[4,2,128,512]{3,2,1,0:T(8,128)(2,1)S(1)}, bf16[4,2,128,512]{3,2,1,0:T(8,128)(2,1)S(1)}, u32[]{:S(2)}, u32[]{:S(2)}) collective-permute-start(bf16[4,2,128,512]{3,2,1,0:T(8,128)(2,1)S(1)} %project.3), channel_id=1, source_target_pairs={{0,1},{1,0},{2,3},{3,2},{4,5},{5,4},{6,7},{7,6},{8,9},{9,8},{10,11... | collective-permute-start | bytes 3145736 | tf_op jit(solution)/shard_map/project/ppermute | solution.py:267
  115.7 0.1 pad_add_fusion.place
  115.8 3.0 %project.2 = bf16[4,2,128,512]{3,2,1,0:T(8,128)(2,1)S(1)} custom-call(s32[2]{0:T(128)S(1)} %pad_add_fusion.place, bf16[512,1024]{1,0:T(8,128)(2,1)S(1)} %bitcast.12, bf16[448,512]{1,0:T(8,128)(2,1)S(1)} %copy-done, bf16[320,512]{1,0:T(8,128)(2,1)S(1)} %copy-done.1, bf16[256,512]{1,0:T(8,128)(2,1)S(1)} %copy-done.2, ...), custom_call_target="tpu_custom_call" | custom-call | flops 1 | bytes 1 | tf_op jit(solution)/shard_map/project/pallas_call | solution.py:382
  118.8 0.0 collective-permute-done.12
  118.8 0.3 add_convert_fusion
  119.1 21.0 %all_to_all.25 = bf16[8,128,512]{2,1,0:T(8,128)(2,1)S(1)} all-to-all(bf16[8,128,512]{2,1,0:T(8,128)(2,1)S(1)} %bitcast.15), channel_id=1, replica_groups=mesh['z'=4,'x_hi'=2,'y'=4,'x_lo'=2,'core'=2] {'y','x_lo'}, dimensions={0} | all-to-all | bytes 2097152 | tf_op jit(solution)/shard_map/move_terms/all_to_all | solution.py:259
  140.1 0.8 reduce_sum.12
  (17 shorter events, 0.0 us)
Async XLA Ops:
  1.7 10.0 %all-to-all-start = ((bf16[4,16,1024]{2,1,0:T(8,128)(2,1)}), bf16[4,16,1024]{2,1,0:T(8,128)(2,1)S(1)}, u32[]{:S(2)}, u32[]{:S(2)}) async-start(bf16[4,16,1024]{2,1,0:T(8,128)(2,1)} %copy.12), calls=%async_computation | async-start | bytes 262144 | tf_op jit(solution)/shard_map/move_queries/all_to_all | solution.py:259
  11.6 17.5 %collective-permute-start = (bf16[2,1056,128]{2,1,0:T(8,128)(2,1)}, bf16[2,1056,128]{2,1,0:T(8,128)(2,1)S(1)}, u32[]{:S(2)}, u32[]{:S(2)}) collective-permute-start(bf16[2,1056,128]{2,1,0:T(8,128)(2,1)} %get-tuple-element.56), channel_id=1, source_target_pairs={{0,4},{4,8},{8,12},{12,0},{1,5},{5,9},{9,13},{13,1},{2,6},{6,10},{... | collective-permute-start | bytes 1622024 | tf_op jit(solution)/shard_map/move_kv/ppermute | solution.py:263
  13.2 25.3 %collective-permute-start.1 = (bf16[2,1056,128]{2,1,0:T(8,128)(2,1)}, bf16[2,1056,128]{2,1,0:T(8,128)(2,1)S(1)}, u32[]{:S(2)}, u32[]{:S(2)}) collective-permute-start(bf16[2,1056,128]{2,1,0:T(8,128)(2,1)} %get-tuple-element.57), channel_id=1, source_target_pairs={{0,8},{4,12},{8,0},{12,4},{1,9},{5,13},{9,1},{13,5},{2,10},{6,14},... | collective-permute-start | bytes 1622024 | tf_op jit(solution)/shard_map/move_kv/ppermute | solution.py:263
  16.7 25.2 %all-to-all-start.1 = ((bf16[8,64,1024]{2,1,0:T(8,128)(2,1)}), bf16[8,64,1024]{2,1,0:T(8,128)(2,1)S(1)}, u32[]{:S(2)}, u32[]{:S(2)}) async-start(bf16[8,64,1024]{2,1,0:T(8,128)(2,1)} %broadcast_in_dim.12), calls=%async_computation.1 | async-start | bytes 2097152 | tf_op jit(solution)/shard_map/move_queries/all_to_all | solution.py:259
  24.2 17.7 %copy-start.3 = (bf16[2,1056,128]{2,1,0:T(8,128)(2,1)S(1)}, bf16[2,1056,128]{2,1,0:T(8,128)(2,1)}, u32[]{:S(2)}) copy-start(bf16[2,1056,128]{2,1,0:T(8,128)(2,1)} %get-tuple-element.55.kv0) | copy-start | bytes 1622020
  24.2 17.7 %collective-permute-start.2 = (bf16[2,1056,128]{2,1,0:T(8,128)(2,1)}, bf16[2,1056,128]{2,1,0:T(8,128)(2,1)}, u32[]{:S(2)}, u32[]{:S(2)}) collective-permute-start(bf16[2,1056,128]{2,1,0:T(8,128)(2,1)} %get-tuple-element.58), channel_id=1, source_target_pairs={{0,12},{4,0},{8,4},{12,8},{1,13},{5,1},{9,5},{13,9},{2,14},{6,2},{... | collective-permute-start | bytes 1622024 | tf_op jit(solution)/shard_map/move_kv/ppermute | solution.py:263
  38.4 0.8 copy-start.4
  39.2 26.5 %collective-permute-start.3 = (bf16[448,512]{1,0:T(8,128)(2,1)}, bf16[448,512]{1,0:T(8,128)(2,1)S(1)}, u32[]{:S(2)}, u32[]{:S(2)}) collective-permute-start(bf16[448,512]{1,0:T(8,128)(2,1)} %get-tuple-element.74), channel_id=1, source_target_pairs={{0,4},{4,8},{8,12},{12,0},{1,5},{5,9},{9,13},{13,1},{2,6},{6,10},{... | collective-permute-start | bytes 1376264 | tf_op jit(solution)/shard_map/move_weight/ppermute | solution.py:263
  39.2 26.5 %collective-permute-start.4 = (bf16[448,512]{1,0:T(8,128)(2,1)}, bf16[448,512]{1,0:T(8,128)(2,1)S(1)}, u32[]{:S(2)}, u32[]{:S(2)}) collective-permute-start(bf16[448,512]{1,0:T(8,128)(2,1)} %get-tuple-element.75), channel_id=1, source_target_pairs={{0,8},{4,12},{8,0},{12,4},{1,9},{5,13},{9,1},{13,5},{2,10},{6,14},... | collective-permute-start | bytes 1376264 | tf_op jit(solution)/shard_map/move_weight/ppermute | solution.py:263
  39.8 25.9 %collective-permute-start.5 = (bf16[448,512]{1,0:T(8,128)(2,1)}, bf16[448,512]{1,0:T(8,128)(2,1)S(1)}, u32[]{:S(2)}, u32[]{:S(2)}) collective-permute-start(bf16[448,512]{1,0:T(8,128)(2,1)} %get-tuple-element.76), channel_id=1, source_target_pairs={{0,12},{4,0},{8,4},{12,8},{1,13},{5,1},{9,5},{13,9},{2,14},{6,2},{... | collective-permute-start | bytes 1376264 | tf_op jit(solution)/shard_map/move_weight/ppermute | solution.py:263
  41.9 1.0 copy-start.5
  43.0 0.7 copy-start.6
  65.7 20.4 %all-to-all-start.2 = ((bf16[8,64,1152]{2,1,0:T(8,128)(2,1)}), bf16[8,64,1152]{2,1,0:T(8,128)(2,1)S(1)}, u32[]{:S(2)}, u32[]{:S(2)}) async-start(bf16[8,64,1152]{2,1,0:T(8,128)(2,1)} %bitcast.7), calls=%async_computation.2 | async-start | bytes 2359296 | tf_op jit(solution)/shard_map/move_partials/all_to_all | solution.py:259
  70.8 37.1 %copy-start = (bf16[448,512]{1,0:T(8,128)(2,1)S(1)}, bf16[448,512]{1,0:T(8,128)(2,1)}, u32[]{:S(2)}) copy-start(bf16[448,512]{1,0:T(8,128)(2,1)} %get-tuple-element.83.refs_0_) | copy-start | bytes 1376260
  70.8 37.1 %copy-start.1 = (bf16[320,512]{1,0:T(8,128)(2,1)S(1)}, bf16[320,512]{1,0:T(8,128)(2,1)}, u32[]{:S(2)}) copy-start(bf16[320,512]{1,0:T(8,128)(2,1)} %get-tuple-element.84.refs_1_) | copy-start | bytes 983044
  70.8 17.3 %collective-permute-start.6 = (bf16[320,512]{1,0:T(8,128)(2,1)}, bf16[320,512]{1,0:T(8,128)(2,1)}, u32[]{:S(2)}, u32[]{:S(2)}) collective-permute-start(bf16[320,512]{1,0:T(8,128)(2,1)} %get-tuple-element.79), channel_id=1, source_target_pairs={{0,4},{4,8},{8,12},{12,0},{1,5},{5,9},{9,13},{13,1},{2,6},{6,10},{... | collective-permute-start | bytes 983048 | tf_op jit(solution)/shard_map/move_weight/ppermute | solution.py:263
  71.4 16.7 %collective-permute-start.7 = (bf16[320,512]{1,0:T(8,128)(2,1)}, bf16[320,512]{1,0:T(8,128)(2,1)}, u32[]{:S(2)}, u32[]{:S(2)}) collective-permute-start(bf16[320,512]{1,0:T(8,128)(2,1)} %get-tuple-element.80), channel_id=1, source_target_pairs={{0,8},{4,12},{8,0},{12,4},{1,9},{5,13},{9,1},{13,5},{2,10},{6,14},... | collective-permute-start | bytes 983048 | tf_op jit(solution)/shard_map/move_weight/ppermute | solution.py:263
  74.0 14.1 %collective-permute-start.8 = (bf16[320,512]{1,0:T(8,128)(2,1)}, bf16[320,512]{1,0:T(8,128)(2,1)}, u32[]{:S(2)}, u32[]{:S(2)}) collective-permute-start(bf16[320,512]{1,0:T(8,128)(2,1)} %get-tuple-element.81), channel_id=1, source_target_pairs={{0,12},{4,0},{8,4},{12,8},{1,13},{5,1},{9,5},{13,9},{2,14},{6,2},{... | collective-permute-start | bytes 983048 | tf_op jit(solution)/shard_map/move_weight/ppermute | solution.py:263
  88.1 10.0 %copy-start.7 = (bf16[256,512]{1,0:T(8,128)(2,1)S(1)}, bf16[256,512]{1,0:T(8,128)(2,1)}, u32[]{:S(2)}) copy-start(bf16[256,512]{1,0:T(8,128)(2,1)} %get-tuple-element.94) | copy-start | bytes 786436
  88.1 19.8 %all-to-all-start.3 = ((bf16[8,64,1024]{2,1,0:T(8,128)(2,1)}), bf16[8,64,1024]{2,1,0:T(8,128)(2,1)S(1)}, u32[]{:S(2)}, u32[]{:S(2)}) async-start(bf16[8,64,1024]{2,1,0:T(8,128)(2,1)} %settle.1), calls=%async_computation.3 | async-start | bytes 2097152 | tf_op jit(solution)/shard_map/move_attended/all_to_all | solution.py:259
  93.5 7.5 %collective-permute-start.9 = (bf16[256,512]{1,0:T(8,128)(2,1)}, bf16[256,512]{1,0:T(8,128)(2,1)}, u32[]{:S(2)}, u32[]{:S(2)}) collective-permute-start(bf16[256,512]{1,0:T(8,128)(2,1)} %get-tuple-element.88), channel_id=1, source_target_pairs={{0,4},{4,8},{8,12},{12,0},{1,5},{5,9},{9,13},{13,1},{2,6},{6,10},{... | collective-permute-start | bytes 786440 | tf_op jit(solution)/shard_map/move_weight/ppermute | solution.py:263
  96.6 11.2 %collective-permute-start.10 = (bf16[256,512]{1,0:T(8,128)(2,1)}, bf16[256,512]{1,0:T(8,128)(2,1)}, u32[]{:S(2)}, u32[]{:S(2)}) collective-permute-start(bf16[256,512]{1,0:T(8,128)(2,1)} %get-tuple-element.91), channel_id=1, source_target_pairs={{0,8},{4,12},{8,0},{12,4},{1,9},{5,13},{9,1},{13,5},{2,10},{6,14},... | collective-permute-start | bytes 786440 | tf_op jit(solution)/shard_map/move_weight/ppermute | solution.py:263
  98.1 9.7 %collective-permute-start.11 = (bf16[256,512]{1,0:T(8,128)(2,1)S(1)}, bf16[256,512]{1,0:T(8,128)(2,1)}, u32[]{:S(2)}, u32[]{:S(2)}) collective-permute-start(bf16[256,512]{1,0:T(8,128)(2,1)S(1)} %copy-done.7), channel_id=1, source_target_pairs={{0,12},{4,0},{8,4},{12,8},{1,13},{5,1},{9,5},{13,9},{2,14},{6,2},{... | collective-permute-start | bytes 786440 | tf_op jit(solution)/shard_map/move_weight/ppermute | solution.py:263
  107.9 1.0 copy-start.2
  111.8 7.0 %collective-permute-start.12 = (bf16[4,2,128,512]{3,2,1,0:T(8,128)(2,1)S(1)}, bf16[4,2,128,512]{3,2,1,0:T(8,128)(2,1)S(1)}, u32[]{:S(2)}, u32[]{:S(2)}) collective-permute-start(bf16[4,2,128,512]{3,2,1,0:T(8,128)(2,1)S(1)} %project.3), channel_id=1, source_target_pairs={{0,1},{1,0},{2,3},{3,2},{4,5},{5,4},{6,7},{7,6},{8,9},{9,8},{10,11... | collective-permute-start | bytes 3145736 | tf_op jit(solution)/shard_map/project/ppermute | solution.py:267

commit v6 on v4

--- a/solution.py
+++ b/solution.py
@@ -174,22 +174,20 @@
 def settle_kernel(parts, out):
     groups, tokens, width = parts.shape
     heads = width // HD - 1
+    lane_id = lax.broadcasted_iota(jnp.int32, (tokens, HD), 1)
     notes = [parts[g, :, heads * HD :].astype(F32) for g in range(groups)]
-    highest = notes[0]
-    for g in range(1, groups):
-        highest = jnp.maximum(highest, notes[g])
-    factors = [jnp.exp2(notes[g] - highest) for g in range(groups)]
+    highest = functools.reduce(jnp.maximum, notes)
+    factors = [jnp.exp2(jnp.where(lane_id < heads, n - highest, 0.0)) for n in notes]
+    total = 0.0
+    for factor, n in zip(factors, notes):
+        total += factor * (pltpu.roll(n, HD - heads, 1) + pltpu.roll(n, HD - 2 * heads, 1))
+    shares = [factor / jnp.where(lane_id < heads, total, 1.0) for factor in factors]
     for h in range(heads):
         cols = slice(h * HD, (h + 1) * HD)
-        numerator = jnp.zeros((tokens, HD), F32)
-        total = jnp.zeros((tokens, 1), F32)
+        attended = 0.0
         for g in range(groups):
-            factor = factors[g][:, h : h + 1]
-            numerator += factor * parts[g, :, cols].astype(F32)
-            total += factor * (
-                notes[g][:, heads + h : heads + h + 1] + notes[g][:, 2 * heads + h : 2 * heads + h + 1]
-            )
-        attended = (numerator / total).astype(BF16)
+            attended += shares[g][:, h : h + 1] * parts[g, :, cols].astype(F32)
+        attended = attended.astype(BF16)
         for g in range(out.shape[0]):
             out[g, :, cols] = attended
 
@@ -303,7 +301,7 @@
                 pltpu.SemaphoreType.DMA((4 * PIECES,)),
                 pltpu.SemaphoreType.DMA((4 * PIECES,)),
             ],
-            compiler_params=grant(56),
+            compiler_params=grant(40),
             cost_estimate=TINY,
         )(place, lax.optimization_barrier((out_weight, packets))[0])
 
@@ -311,9 +309,10 @@
             ready, _ = lax.optimization_barrier(([chunks[k * PIECES + j] for k in range(4)], after))
             return [ready[0]] + [along_y(ready[k], k) for k in range(1, 4)]
 
-        weights = [pieces(j, kv) for j in range(PIECES)]
+        weights = [pieces(j, kv[1:3]) for j in range(PIECES)]
         mine, chunks = lax.optimization_barrier((mine, chunks))
 
+    pos_ids, chunks = lax.optimization_barrier((pos_ids, chunks))
     pos_n = [
         lax.dynamic_slice_in_dim(pos_ids, (group * 4 + lax.rem(y + 4 - k, 4)) * fresh, fresh) for k in range(4)
     ]
@@ -334,7 +333,7 @@
                 pltpu.VMEM((heads, tokens, HD), F32),
                 pltpu.VMEM((heads, tokens, 2 * HD), F32),
             ],
-            compiler_params=grant(40),
+            compiler_params=grant(22),
             cost_estimate=TINY,
         )(all_live, mine, *kv, pos_q, pos_n)
 

time: 143 us -> 138 us (0.965)
  waiting for transfers between devices: 33.6 us -> 24.5 us
  local copies, waits for them, and re-layouts: 9.09 us -> 17.5 us
  starting transfers between devices: 47 us -> 44.5 us
    ppermute x12, waiting for transfers between devices: 20.9 us -> 12.8 us  [along_y(): return lax.ppermute(x, 'y', [(i, (i + distance) % 4) for i in range(4)])]
    unnamed x20 -> x26, local copies, waits for them, and re-layouts: 3.2 us -> 10.1 us
    ppermute x12, starting transfers between devices: 18.3 us -> 16.3 us  [along_y(): return lax.ppermute(x, 'y', [(i, (i + distance) % 4) for i in range(4)])]
  transfers between devices with their start and end apart: 17 -> 17, of which waited for: 7 -> 7; matrix products, arithmetic and copies ran while one was open for 3% -> 4% of each run, Pallas kernels for 20% -> 20%
where the time goes in v6:
time: 138 us; the launch traced here: 137 us
  starting transfers between devices  44.5 us (32%)
  Pallas kernels  29.8 us (22%)
  waiting for transfers between devices  24.5 us (18%)
  blocking collectives  19 us (14%)
  local copies, waits for them, and re-layouts  17.5 us (13%)
    all_to_all x4, starting transfers between devices, swap(): return lax.all_to_all(x, axes, split_axis=0, concat_axis=0, tiled=False)  25.9 us
    all_to_all x1, blocking collectives, swap(): return lax.all_to_all(x, axes, split_axis=0, concat_axis=0, tiled=False)  19 us
    ppermute x12, starting transfers between devices, along_y(): return lax.ppermute(x, 'y', [(i, (i + distance) % 4) for i in range(4)])  16.3 us
    pallas_call x1, Pallas kernels, shards(): pl.pallas_call(attend_kernel, out_shape=jax.ShapeDtypeStruct((tokens, qua...  15.7 us
    ppermute x12, waiting for transfers between devices, along_y(): return lax.ppermute(x, 'y', [(i, (i + distance) % 4) for i in range(4)])  12.8 us
    all_to_all x4, waiting for transfers between devices, swap(): return lax.all_to_all(x, axes, split_axis=0, concat_axis=0, tiled=False)  11.7 us
    unnamed x26, local copies, waits for them, and re-layouts  10.1 us
    pallas_call x2, Pallas kernels, project(): pl.pallas_call(project_kernel, out_shape=jax.ShapeDtypeStruct((4, 2, toke...  5.32 us
  transfers between devices with their start and end apart: 17, of which 7 were waited for; matrix products, arithmetic and copies ran while one was open for 4% of the time, Pallas kernels for 20%

profile of v6, /device:TPU:1, one launch (start us, length us, event | category | flops | bytes accessed | tf_op | source)
XLA Modules:
  0.0 137.3 jit_solution(3743497849564520576)
XLA Ops:
  0.0 1.0 reshape.21
  1.0 0.7 copy.14
  1.7 5.0 %all-to-all-start = ((bf16[4,16,1024]{2,1,0:T(8,128)(2,1)}), bf16[4,16,1024]{2,1,0:T(8,128)(2,1)S(1)}, u32[]{:S(2)}, u32[]{:S(2)}) async-start(bf16[4,16,1024]{2,1,0:T(8,128)(2,1)} %copy.14), calls=%async_computation | async-start | bytes 262144 | tf_op jit(solution)/shard_map/move_queries/all_to_all | solution.py:231
  7.4 3.6 %pack.1 = (bf16[2,1056,128]{2,1,0:T(8,128)(2,1)}, bf16[2,1056,128]{2,1,0:T(8,128)(2,1)}, bf16[2,1056,128]{2,1,0:T(8,128)(2,1)}, bf16[2,1056,128]{2,1,0:T(8,128)(2,1)}) custom-call(s32[1]{0:T(128)} %bitcast.place, s32[8]{0:T(128)} %valid_len.1, s32[8]{0:T(128)} %span_ids.1, s32[1]{0:T(128)S(6)} %copy.16.offset, bf16[1024,256]{1,0:T(8,128)(2,1)} %keys_in.1, ...), custom_call_target="tpu_custom_call" | custom-call | flops 1 | bytes 1 | tf_op jit(solution)/shard_map/pack/pallas_call | solution.py:266
  10.9 0.6 all-to-all-done
  11.5 0.9 collective-permute-start
  12.5 2.4 %collective-permute-start.1 = (bf16[2,1056,128]{2,1,0:T(8,128)(2,1)}, bf16[2,1056,128]{2,1,0:T(8,128)(2,1)}, u32[]{:S(2)}, u32[]{:S(2)}) collective-permute-start(bf16[2,1056,128]{2,1,0:T(8,128)(2,1)} %get-tuple-element.56), channel_id=1, source_target_pairs={{0,8},{4,12},{8,0},{12,4},{1,9},{5,13},{9,1},{13,5},{2,10},{6,14},... | collective-permute-start | bytes 1622024 | tf_op jit(solution)/shard_map/move_kv/ppermute | solution.py:235
  14.9 1.5 %copy.15.pos_q = s32[512,1]{1,0:T(8,128)} copy(s32[512,1]{0,1:T(1,128)} %bitcast.26) | data formatting | bytes 4096 | tf_op jit(solution)/shard_map/broadcast_in_dim | solution.py:320
  16.6 1.2 collective-permute-start.2
  17.7 1.2 broadcast_in_dim.18
  18.9 7.5 %all-to-all-start.1 = ((bf16[8,64,1024]{2,1,0:T(8,128)(2,1)}), bf16[8,64,1024]{2,1,0:T(8,128)(2,1)S(1)}, u32[]{:S(2)}, u32[]{:S(2)}) async-start(bf16[8,64,1024]{2,1,0:T(8,128)(2,1)} %broadcast_in_dim.18), calls=%async_computation.1 | async-start | bytes 2097152 | tf_op jit(solution)/shard_map/move_queries/all_to_all | solution.py:231
  26.4 0.7 slice_bitcast_fusion.3
  27.1 2.2 %copy-done = bf16[4096,512]{1,0:T(8,128)(2,1)S(1)} copy-done((bf16[4096,512]{1,0:T(8,128)(2,1)S(1)}, bf16[4096,512]{1,0:T(8,128)(2,1)}, u32[]{:S(2)}) %copy-start) | copy-done | bytes 4194328
  29.3 3.4 %move_weight.1 = (bf16[448,512]{1,0:T(8,128)(2,1)S(1)}, bf16[288,512]{1,0:T(8,128)(2,1)S(1)}, bf16[288,512]{1,0:T(8,128)(2,1)S(1)}, bf16[448,512]{1,0:T(8,128)(2...) custom-call(s32[1]{0:T(128)} %bitcast.place, ...), custom_call_target="tpu_custom_call" | custom-call | flops 1 | bytes 1 | tf_op jit(solution)/shard_map/move_weight/pallas_call | solution.py:294
  32.7 0.7 copy-done.1
  33.4 0.7 copy-done.5
  34.1 0.7 copy-done.7
  34.8 0.7 copy-done.8
  35.5 0.7 copy-done.9
  36.2 0.7 copy-done.10
  37.0 0.7 copy-done.11
  37.9 0.9 collective-permute-start.4
  38.9 1.6 %collective-permute-start.5 = (bf16[448,512]{1,0:T(8,128)(2,1)}, bf16[448,512]{1,0:T(8,128)(2,1)S(1)}, u32[]{:S(2)}, u32[]{:S(2)}) collective-permute-start(bf16[448,512]{1,0:T(8,128)(2,1)} %get-tuple-element.76), channel_id=1, source_target_pairs={{0,12},{4,0},{8,4},{12,8},{1,13},{5,1},{9,5},{13,9},{2,14},{6,2},{... | collective-permute-start | bytes 1376264 | tf_op jit(solution)/shard_map/move_weight/ppermute | solution.py:235
  40.5 0.7 slice_bitcast_fusion.2
  41.2 0.7 slice_bitcast_fusion.1
  41.8 0.7 slice_bitcast_fusion
  42.6 1.0 copy-done.3
  43.6 1.0 copy-done.4
  44.6 15.7 %attend.1 = bf16[512,1152]{1,0:T(8,128)(2,1)} custom-call(s32[32]{0:T(128)S(1)} %reshape.26.live, bf16[512,1024]{1,0:T(8,128)(2,1)S(1)} %bitcast.21, bf16[2,1056,128]{2,1,0:T(8,128)(2,1)S(1)} %copy-done.4, bf16[2,1056,128]{2,1,0:T(8,128)(2,1)} %collective-permute-done.kv1, bf16[2,1056,128]{2,1,0:T(8,128)(2,1)} %collective-permute-done.1.kv2, ...), custom_call_target="tpu_custom_call" | custom-call | flops 1 | bytes 1 | tf_op jit(solution)/shard_map/attend/pallas_call | solution.py:325
  60.3 0.2 collective-permute-done.5.refs_9_
  60.5 7.5 %all-to-all-start.2 = ((bf16[8,64,1152]{2,1,0:T(8,128)(2,1)}), bf16[8,64,1152]{2,1,0:T(8,128)(2,1)S(1)}, u32[]{:S(2)}, u32[]{:S(2)}) async-start(bf16[8,64,1152]{2,1,0:T(8,128)(2,1)} %bitcast.11), calls=%async_computation.2 | async-start | bytes 2359296 | tf_op jit(solution)/shard_map/move_partials/all_to_all | solution.py:231
  68.0 1.6 %collective-permute-start.6 = (bf16[288,512]{1,0:T(8,128)(2,1)}, bf16[288,512]{1,0:T(8,128)(2,1)}, u32[]{:S(2)}, u32[]{:S(2)}) collective-permute-start(bf16[288,512]{1,0:T(8,128)(2,1)} %copy-done.11), channel_id=1, source_target_pairs={{0,4},{4,8},{8,12},{12,0},{1,5},{5,9},{9,13},{13,1},{2,6},{6,10},{... | collective-permute-start | bytes 884744 | tf_op jit(solution)/shard_map/move_weight/ppermute | solution.py:235
  69.6 2.9 %collective-permute-start.7 = (bf16[288,512]{1,0:T(8,128)(2,1)}, bf16[288,512]{1,0:T(8,128)(2,1)}, u32[]{:S(2)}, u32[]{:S(2)}) collective-permute-start(bf16[288,512]{1,0:T(8,128)(2,1)} %copy-done.10), channel_id=1, source_target_pairs={{0,8},{4,12},{8,0},{12,4},{1,9},{5,13},{9,1},{13,5},{2,10},{6,14},... | collective-permute-start | bytes 884744 | tf_op jit(solution)/shard_map/move_weight/ppermute | solution.py:235
  72.5 11.1 %all-to-all-done.2.parts = bf16[8,64,1152]{2,1,0:T(8,128)(2,1)S(1)} async-done(((bf16[8,64,1152]{2,1,0:T(8,128)(2,1)}), bf16[8,64,1152]{2,1,0:T(8,128)(2,1)S(1)}, u32[]{:S(2)}, u32[]{:S(2)}) %all-to-all-start.2) | async-done | bytes 1179680 | tf_op jit(solution)/shard_map/move_partials/all_to_all | solution.py:231
  83.6 1.9 %settle.1 = bf16[8,64,1024]{2,1,0:T(8,128)(2,1)} custom-call(bf16[8,64,1152]{2,1,0:T(8,128)(2,1)S(1)} %all-to-all-done.2.parts), custom_call_target="tpu_custom_call" | custom-call | flops 1 | bytes 1 | tf_op jit(solution)/shard_map/settle/pallas_call | solution.py:344
  85.5 5.9 %all-to-all-start.3 = ((bf16[8,64,1024]{2,1,0:T(8,128)(2,1)}), bf16[8,64,1024]{2,1,0:T(8,128)(2,1)S(1)}, u32[]{:S(2)}, u32[]{:S(2)}) async-start(bf16[8,64,1024]{2,1,0:T(8,128)(2,1)} %settle.1), calls=%async_computation.3 | async-start | bytes 2097152 | tf_op jit(solution)/shard_map/move_attended/all_to_all | solution.py:231
  91.4 1.1 collective-permute-start.9
  92.5 3.6 %collective-permute-start.10 = (bf16[288,512]{1,0:T(8,128)(2,1)}, bf16[288,512]{1,0:T(8,128)(2,1)}, u32[]{:S(2)}, u32[]{:S(2)}) collective-permute-start(bf16[288,512]{1,0:T(8,128)(2,1)} %copy-done.7), channel_id=1, source_target_pairs={{0,8},{4,12},{8,0},{12,4},{1,9},{5,13},{9,1},{13,5},{2,10},{6,14},... | collective-permute-start | bytes 884744 | tf_op jit(solution)/shard_map/move_weight/ppermute | solution.py:235
  96.2 4.3 %collective-permute-done.9.refs_5_ = bf16[288,512]{1,0:T(8,128)(2,1)} collective-permute-done((bf16[288,512]{1,0:T(8,128)(2,1)}, bf16[288,512]{1,0:T(8,128)(2,1)}, u32[]{:S(2)}, u32[]{:S(2)}) %collective-permute-start.9) | collective-permute-done | bytes 294944 | tf_op jit(solution)/shard_map/move_weight/ppermute | solution.py:235
  100.5 7.6 %collective-permute-done.10.refs_8_ = bf16[288,512]{1,0:T(8,128)(2,1)} collective-permute-done((bf16[288,512]{1,0:T(8,128)(2,1)}, bf16[288,512]{1,0:T(8,128)(2,1)}, u32[]{:S(2)}, u32[]{:S(2)}) %collective-permute-start.10) | collective-permute-done | bytes 294944 | tf_op jit(solution)/shard_map/move_weight/ppermute | solution.py:235
  108.1 0.5 collective-permute-done.11.refs_11_
  108.6 1.0 copy-done.2
  109.5 2.7 %project.3 = bf16[4,2,128,512]{3,2,1,0:T(8,128)(2,1)S(1)} custom-call(s32[2]{0:T(128)S(1)} %pad_add_fusion.1.place, bf16[512,1024]{1,0:T(8,128)(2,1)S(1)} %bitcast.19, bf16[448,512]{1,0:T(8,128)(2,1)S(1)} %get-tuple-element.83.refs_0_, bf16[288,512]{1,0:T(8,128)(2,1)S(1)} %get-tuple-element.84.refs_1_, bf16[288,512]{1,0:T(8,128)(2,1)S(1)} %copy-done.2, ...), custom_call_target="tpu_custom_call" | custom-call | flops 1 | bytes 1 | tf_op jit(solution)/shard_map/project/pallas_call | solution.py:358
  112.2 2.2 %collective-permute-start.12 = (bf16[4,2,128,512]{3,2,1,0:T(8,128)(2,1)S(1)}, bf16[4,2,128,512]{3,2,1,0:T(8,128)(2,1)S(1)}, u32[]{:S(2)}, u32[]{:S(2)}) collective-permute-start(bf16[4,2,128,512]{3,2,1,0:T(8,128)(2,1)S(1)} %project.3), channel_id=1, source_target_pairs={{0,1},{1,0},{2,3},{3,2},{4,5},{5,4},{6,7},{7,6},{8,9},{9,8},{10,11... | collective-permute-start | bytes 3145736 | tf_op jit(solution)/shard_map/project/ppermute | solution.py:239
  114.5 2.7 %project.2 = bf16[4,2,128,512]{3,2,1,0:T(8,128)(2,1)S(1)} custom-call(s32[2]{0:T(128)S(1)} %pad_add_fusion.place, bf16[512,1024]{1,0:T(8,128)(2,1)S(1)} %bitcast.20, bf16[448,512]{1,0:T(8,128)(2,1)S(1)} %get-tuple-element.83.refs_0_, bf16[288,512]{1,0:T(8,128)(2,1)S(1)} %get-tuple-element.84.refs_1_, bf16[288,512]{1,0:T(8,128)(2,1)S(1)} %copy-done.2, ...), custom_call_target="tpu_custom_call" | custom-call | flops 1 | bytes 1 | tf_op jit(solution)/shard_map/project/pallas_call | solution.py:358
  117.2 0.3 add_convert_fusion
  117.5 19.0 %all_to_all.25 = bf16[8,128,512]{2,1,0:T(8,128)(2,1)S(1)} all-to-all(bf16[8,128,512]{2,1,0:T(8,128)(2,1)S(1)} %bitcast.23), channel_id=1, replica_groups=mesh['z'=4,'x_hi'=2,'y'=4,'x_lo'=2,'core'=2] {'y','x_lo'}, dimensions={0} | all-to-all | bytes 2097152 | tf_op jit(solution)/shard_map/move_terms/all_to_all | solution.py:231
  136.5 0.8 reduce_sum.12
  (36 shorter events, 0.8 us)
Async XLA Ops:
  0.0 16.4 %copy-start.12 = (s32[512]{0:T(512)S(1)}, s32[512]{0:T(512)}, u32[]{:S(2)}) copy-start(s32[512]{0:T(512)} %param.17) | copy-start | bytes 6148
  1.7 9.8 %all-to-all-start = ((bf16[4,16,1024]{2,1,0:T(8,128)(2,1)}), bf16[4,16,1024]{2,1,0:T(8,128)(2,1)S(1)}, u32[]{:S(2)}, u32[]{:S(2)}) async-start(bf16[4,16,1024]{2,1,0:T(8,128)(2,1)} %copy.14), calls=%async_computation | async-start | bytes 262144 | tf_op jit(solution)/shard_map/move_queries/all_to_all | solution.py:231
  11.5 26.1 %collective-permute-start = (bf16[2,1056,128]{2,1,0:T(8,128)(2,1)}, bf16[2,1056,128]{2,1,0:T(8,128)(2,1)}, u32[]{:S(2)}, u32[]{:S(2)}) collective-permute-start(bf16[2,1056,128]{2,1,0:T(8,128)(2,1)} %get-tuple-element.55), channel_id=1, source_target_pairs={{0,4},{4,8},{8,12},{12,0},{1,5},{5,9},{9,13},{13,1},{2,6},{6,10},{... | collective-permute-start | bytes 1622024 | tf_op jit(solution)/shard_map/move_kv/ppermute | solution.py:235
  12.5 25.4 %collective-permute-start.1 = (bf16[2,1056,128]{2,1,0:T(8,128)(2,1)}, bf16[2,1056,128]{2,1,0:T(8,128)(2,1)}, u32[]{:S(2)}, u32[]{:S(2)}) collective-permute-start(bf16[2,1056,128]{2,1,0:T(8,128)(2,1)} %get-tuple-element.56), channel_id=1, source_target_pairs={{0,8},{4,12},{8,0},{12,4},{1,9},{5,13},{9,1},{13,5},{2,10},{6,14},... | collective-permute-start | bytes 1622024 | tf_op jit(solution)/shard_map/move_kv/ppermute | solution.py:235
  16.6 25.3 %collective-permute-start.2 = (bf16[2,1056,128]{2,1,0:T(8,128)(2,1)}, bf16[2,1056,128]{2,1,0:T(8,128)(2,1)}, u32[]{:S(2)}, u32[]{:S(2)}) collective-permute-start(bf16[2,1056,128]{2,1,0:T(8,128)(2,1)} %get-tuple-element.57), channel_id=1, source_target_pairs={{0,12},{4,0},{8,4},{12,8},{1,13},{5,1},{9,5},{13,9},{2,14},{6,2},{... | collective-permute-start | bytes 1622024 | tf_op jit(solution)/shard_map/move_kv/ppermute | solution.py:235
  18.9 23.7 %all-to-all-start.1 = ((bf16[8,64,1024]{2,1,0:T(8,128)(2,1)}), bf16[8,64,1024]{2,1,0:T(8,128)(2,1)S(1)}, u32[]{:S(2)}, u32[]{:S(2)}) async-start(bf16[8,64,1024]{2,1,0:T(8,128)(2,1)} %broadcast_in_dim.18), calls=%async_computation.1 | async-start | bytes 2097152 | tf_op jit(solution)/shard_map/move_queries/all_to_all | solution.py:231
  27.1 2.2 %copy-start = (bf16[4096,512]{1,0:T(8,128)(2,1)S(1)}, bf16[4096,512]{1,0:T(8,128)(2,1)}, u32[]{:S(2)}) copy-start(bf16[4096,512]{1,0:T(8,128)(2,1)} %weight) | copy-start | bytes 12582916
  32.7 0.7 copy-start.1
  33.4 0.7 copy-start.5
  34.1 0.7 copy-start.7
  34.8 0.7 copy-start.8
  35.5 0.7 copy-start.9
  36.2 0.7 copy-start.10
  36.9 0.7 copy-start.11
  37.8 22.5 %collective-permute-start.3 = (bf16[448,512]{1,0:T(8,128)(2,1)}, bf16[448,512]{1,0:T(8,128)(2,1)S(1)}, u32[]{:S(2)}, u32[]{:S(2)}) collective-permute-start(bf16[448,512]{1,0:T(8,128)(2,1)} %get-tuple-element.74), channel_id=1, source_target_pairs={{0,4},{4,8},{8,12},{12,0},{1,5},{5,9},{9,13},{13,1},{2,6},{6,10},{... | collective-permute-start | bytes 1376264 | tf_op jit(solution)/shard_map/move_weight/ppermute | solution.py:235
  37.9 22.4 %collective-permute-start.4 = (bf16[448,512]{1,0:T(8,128)(2,1)}, bf16[448,512]{1,0:T(8,128)(2,1)S(1)}, u32[]{:S(2)}, u32[]{:S(2)}) collective-permute-start(bf16[448,512]{1,0:T(8,128)(2,1)} %get-tuple-element.75), channel_id=1, source_target_pairs={{0,8},{4,12},{8,0},{12,4},{1,9},{5,13},{9,1},{13,5},{2,10},{6,14},... | collective-permute-start | bytes 1376264 | tf_op jit(solution)/shard_map/move_weight/ppermute | solution.py:235
  38.9 21.7 %collective-permute-start.5 = (bf16[448,512]{1,0:T(8,128)(2,1)}, bf16[448,512]{1,0:T(8,128)(2,1)S(1)}, u32[]{:S(2)}, u32[]{:S(2)}) collective-permute-start(bf16[448,512]{1,0:T(8,128)(2,1)} %get-tuple-element.76), channel_id=1, source_target_pairs={{0,12},{4,0},{8,4},{12,8},{1,13},{5,1},{9,5},{13,9},{2,14},{6,2},{... | collective-permute-start | bytes 1376264 | tf_op jit(solution)/shard_map/move_weight/ppermute | solution.py:235
  42.6 1.0 copy-start.3
  43.6 1.0 copy-start.4
  60.5 23.1 %all-to-all-start.2 = ((bf16[8,64,1152]{2,1,0:T(8,128)(2,1)}), bf16[8,64,1152]{2,1,0:T(8,128)(2,1)S(1)}, u32[]{:S(2)}, u32[]{:S(2)}) async-start(bf16[8,64,1152]{2,1,0:T(8,128)(2,1)} %bitcast.11), calls=%async_computation.2 | async-start | bytes 2359296 | tf_op jit(solution)/shard_map/move_partials/all_to_all | solution.py:231
  68.0 17.5 %collective-permute-start.6 = (bf16[288,512]{1,0:T(8,128)(2,1)}, bf16[288,512]{1,0:T(8,128)(2,1)}, u32[]{:S(2)}, u32[]{:S(2)}) collective-permute-start(bf16[288,512]{1,0:T(8,128)(2,1)} %copy-done.11), channel_id=1, source_target_pairs={{0,4},{4,8},{8,12},{12,0},{1,5},{5,9},{9,13},{13,1},{2,6},{6,10},{... | collective-permute-start | bytes 884744 | tf_op jit(solution)/shard_map/move_weight/ppermute | solution.py:235
  69.6 15.9 %collective-permute-start.7 = (bf16[288,512]{1,0:T(8,128)(2,1)}, bf16[288,512]{1,0:T(8,128)(2,1)}, u32[]{:S(2)}, u32[]{:S(2)}) collective-permute-start(bf16[288,512]{1,0:T(8,128)(2,1)} %copy-done.10), channel_id=1, source_target_pairs={{0,8},{4,12},{8,0},{12,4},{1,9},{5,13},{9,1},{13,5},{2,10},{6,14},... | collective-permute-start | bytes 884744 | tf_op jit(solution)/shard_map/move_weight/ppermute | solution.py:235
  72.5 13.0 %collective-permute-start.8 = (bf16[288,512]{1,0:T(8,128)(2,1)}, bf16[288,512]{1,0:T(8,128)(2,1)}, u32[]{:S(2)}, u32[]{:S(2)}) collective-permute-start(bf16[288,512]{1,0:T(8,128)(2,1)} %copy-done.9), channel_id=1, source_target_pairs={{0,12},{4,0},{8,4},{12,8},{1,13},{5,1},{9,5},{13,9},{2,14},{6,2},{... | collective-permute-start | bytes 884744 | tf_op jit(solution)/shard_map/move_weight/ppermute | solution.py:235
  85.5 10.6 %copy-start.6 = (bf16[288,512]{1,0:T(8,128)(2,1)S(1)}, bf16[288,512]{1,0:T(8,128)(2,1)}, u32[]{:S(2)}) copy-start(bf16[288,512]{1,0:T(8,128)(2,1)} %copy-done.5) | copy-start | bytes 884740
  85.5 23.0 %all-to-all-start.3 = ((bf16[8,64,1024]{2,1,0:T(8,128)(2,1)}), bf16[8,64,1024]{2,1,0:T(8,128)(2,1)S(1)}, u32[]{:S(2)}, u32[]{:S(2)}) async-start(bf16[8,64,1024]{2,1,0:T(8,128)(2,1)} %settle.1), calls=%async_computation.3 | async-start | bytes 2097152 | tf_op jit(solution)/shard_map/move_attended/all_to_all | solution.py:231
  91.4 9.0 %collective-permute-start.9 = (bf16[288,512]{1,0:T(8,128)(2,1)}, bf16[288,512]{1,0:T(8,128)(2,1)}, u32[]{:S(2)}, u32[]{:S(2)}) collective-permute-start(bf16[288,512]{1,0:T(8,128)(2,1)} %copy-done.8), channel_id=1, source_target_pairs={{0,4},{4,8},{8,12},{12,0},{1,5},{5,9},{9,13},{13,1},{2,6},{6,10},{... | collective-permute-start | bytes 884744 | tf_op jit(solution)/shard_map/move_weight/ppermute | solution.py:235
  92.5 15.6 %collective-permute-start.10 = (bf16[288,512]{1,0:T(8,128)(2,1)}, bf16[288,512]{1,0:T(8,128)(2,1)}, u32[]{:S(2)}, u32[]{:S(2)}) collective-permute-start(bf16[288,512]{1,0:T(8,128)(2,1)} %copy-done.7), channel_id=1, source_target_pairs={{0,8},{4,12},{8,0},{12,4},{1,9},{5,13},{9,1},{13,5},{2,10},{6,14},... | collective-permute-start | bytes 884744 | tf_op jit(solution)/shard_map/move_weight/ppermute | solution.py:235
  96.1 12.5 %collective-permute-start.11 = (bf16[288,512]{1,0:T(8,128)(2,1)S(1)}, bf16[288,512]{1,0:T(8,128)(2,1)}, u32[]{:S(2)}, u32[]{:S(2)}) collective-permute-start(bf16[288,512]{1,0:T(8,128)(2,1)S(1)} %copy-done.6), channel_id=1, source_target_pairs={{0,12},{4,0},{8,4},{12,8},{1,13},{5,1},{9,5},{13,9},{2,14},{6,2},{... | collective-permute-start | bytes 884744 | tf_op jit(solution)/shard_map/move_weight/ppermute | solution.py:235
  108.6 1.0 copy-start.2
  112.2 5.0 %collective-permute-start.12 = (bf16[4,2,128,512]{3,2,1,0:T(8,128)(2,1)S(1)}, bf16[4,2,128,512]{3,2,1,0:T(8,128)(2,1)S(1)}, u32[]{:S(2)}, u32[]{:S(2)}) collective-permute-start(bf16[4,2,128,512]{3,2,1,0:T(8,128)(2,1)S(1)} %project.3), channel_id=1, source_target_pairs={{0,1},{1,0},{2,3},{3,2},{4,5},{5,4},{6,7},{7,6},{8,9},{9,8},{10,11... | collective-permute-start | bytes 3145736 | tf_op jit(solution)/shard_map/project/ppermute | solution.py:239

commit v7 on v6

--- a/solution.py
+++ b/solution.py
@@ -13,7 +13,6 @@
 HD = 128
 SPAN = 128
 KEY_BLOCK = 512
-PIECES = 3
 FILL = -1e30
 LOWEST = -1e20
 LOG2_SCALE = math.log2(math.e) / math.sqrt(HD)
@@ -196,14 +195,14 @@
     outs, (held, arrived, left) = refs[:-3], refs[-3:]
     rows = held.shape[1]
     copies = []
-    for i, out in enumerate(outs):
-        k, start = i // PIECES, sum(o.shape[0] for o in outs[i // PIECES * PIECES : i])
-        page = held.at[k, slice(start, start + out.shape[0]), :]
-        part = pl.ds(pl.multiple_of(lax.rem(place[0] + k, 4) * rows + start, 16), out.shape[0])
+    for i, (k, start) in enumerate(((0, 0), (1, 0), (3, 0), (2, 0), (2, rows // 2))):
+        size = outs[i].shape[0]
+        page = held.at[k, slice(start, start + size), :]
+        part = pl.ds(pl.multiple_of(lax.rem(place[0] + k, 4) * rows + start, 16), size)
         copies.append(
             (
                 pltpu.make_async_copy(weight.at[part, :], page, arrived.at[i]),
-                pltpu.make_async_copy(page, out, left.at[i]),
+                pltpu.make_async_copy(page, outs[i], left.at[i]),
             )
         )
         copies[i][0].start()
@@ -214,14 +213,13 @@
         departure.wait()
 
 
-def project_kernel(place, attended, *refs):
-    weights, out = refs[:-1], refs[-1]
+def project_kernel(place, attended, w0, w1, w2a, w2b, w3, out):
     size = out.shape[2]
     picked = [pl.ds(pl.multiple_of((2 * r + place[1]) * size, size), size) for r in range(out.shape[1])]
     rows = jnp.concatenate([attended[p, :] for p in picked], axis=0)
-    for k in range(4):
+    for k, pieces in enumerate(((w0,), (w1,), (w2a, w2b), (w3,))):
         target = lax.rem(place[0] + 4 - k, 4)
-        weight = jnp.concatenate([w[...] for w in weights[k * PIECES : (k + 1) * PIECES]], axis=0)
+        weight = jnp.concatenate([w[...] for w in pieces], axis=0)
         term = jnp.dot(rows, weight, preferred_element_type=F32).astype(BF16)
         for r in range(out.shape[1]):
             out[target, r] = term[r * size : (r + 1) * size]
@@ -290,26 +288,23 @@
 
     columns = out_weight.shape[1]
     with jax.named_scope("move_weight"):
-        sizes = (448, 288, 288)
+        sizes = (quarter, quarter, quarter, quarter // 2, quarter // 2)
         chunks = pl.pallas_call(
             cut_kernel,
-            out_shape=[jax.ShapeDtypeStruct((size, columns), BF16) for size in sizes * 4],
+            out_shape=[jax.ShapeDtypeStruct((size, columns), BF16) for size in sizes],
             in_specs=[SMEM, ANY],
-            out_specs=[ANY] * (4 * PIECES),
+            out_specs=[ANY] * len(sizes),
             scratch_shapes=[
                 pltpu.VMEM((4, quarter, columns), BF16),
-                pltpu.SemaphoreType.DMA((4 * PIECES,)),
-                pltpu.SemaphoreType.DMA((4 * PIECES,)),
+                pltpu.SemaphoreType.DMA((len(sizes),)),
+                pltpu.SemaphoreType.DMA((len(sizes),)),
             ],
             compiler_params=grant(40),
             cost_estimate=TINY,
         )(place, lax.optimization_barrier((out_weight, packets))[0])
-
-        def pieces(j, after):
-            ready, _ = lax.optimization_barrier(([chunks[k * PIECES + j] for k in range(4)], after))
-            return [ready[0]] + [along_y(ready[k], k) for k in range(1, 4)]
-
-        weights = [pieces(j, kv[1:3]) for j in range(PIECES)]
+        moving, _ = lax.optimization_barrier((chunks[1:], kv[1:3]))
+        around = [along_y(moving[0], 1), along_y(moving[1], 3)]
+        across = [along_y(moving[2], 2), along_y(moving[3], 2)]
         mine, chunks = lax.optimization_barrier((mine, chunks))
 
     pos_ids, chunks = lax.optimization_barrier((pos_ids, chunks))
@@ -338,7 +333,7 @@
         )(all_live, mine, *kv, pos_q, pos_n)
 
     with jax.named_scope("move_partials"):
-        partial, weights[0] = lax.optimization_barrier((partial, weights[0]))
+        partial, around = lax.optimization_barrier((partial, around))
         partial = swap(partial.reshape(groups, tokens // groups, quarter + HD), ("z", "x_hi"))
     with jax.named_scope("settle"):
         attended = pl.pallas_call(
@@ -346,11 +341,11 @@
             out_shape=jax.ShapeDtypeStruct((groups, tokens // groups, quarter), BF16),
             in_specs=[VMEM],
             out_specs=VMEM,
-            compiler_params=grant(24),
+            compiler_params=grant(10),
             cost_estimate=TINY,
         )(partial)
     with jax.named_scope("move_attended"):
-        attended, weights[1] = lax.optimization_barrier((attended, weights[1]))
+        attended, across[0] = lax.optimization_barrier((attended, across[0]))
         attended = swap(attended, ("z", "x_hi")).reshape(tokens, quarter)
 
 
@@ -358,11 +353,11 @@
         return pl.pallas_call(
             project_kernel,
             out_shape=jax.ShapeDtypeStruct((4, 2, tokens // 4, columns), BF16),
-            in_specs=[SMEM] + [VMEM] * (1 + 4 * PIECES),
+            in_specs=[SMEM] + [VMEM] * 6,
             out_specs=VMEM,
-            compiler_params=grant(32),
-            cost_estimate=TINY,
-        )(jnp.stack([y, which]).astype(jnp.int32), attended, *[w[k] for k in range(4) for w in weights])
+            compiler_params=grant(14),
+            cost_estimate=TINY,
+        )(jnp.stack([y, which]).astype(jnp.int32), attended, chunks[0], around[0], *across, around[1])
 
     with jax.named_scope("project"):
         theirs = to_other(project(1 - core), "core")

time: 138 us -> 139 us (level)
  waiting for transfers between devices: 24.5 us -> 38.3 us
  starting transfers between devices: 44.5 us -> 35.7 us
  local copies, waits for them, and re-layouts: 17.5 us -> 14.2 us
    ppermute x12 -> x7, starting transfers between devices: 16.3 us -> 7.2 us  [along_y(): return lax.ppermute(x, 'y', [(i, (i + distance) % 4) for i in range(4)])]
    ppermute x12 -> x7, waiting for transfers between devices: 12.8 us -> 19.7 us  [along_y(): return lax.ppermute(x, 'y', [(i, (i + distance) % 4) for i in range(4)])]
    all_to_all x4, waiting for transfers between devices: 11.7 us -> 18.6 us  [swap(): return lax.all_to_all(x, axes, split_axis=0, concat_axis=0, tiled=False)]
    pallas_call x1, Pallas kernels: 15.7 us -> 18.5 us  [shards(): pl.pallas_call(attend_kernel, out_shape=jax.ShapeDtypeStruct((tokens, qua...]
    ppermute x1, starting transfers between devices: 2.22 us -> 4.39 us  [to_other(): return lax.ppermute(x, axis, [(0, 1), (1, 0)])]
    unnamed x26 -> x20, local copies, waits for them, and re-layouts: 10.1 us -> 8.27 us
    all_to_all x4, starting transfers between devices: 25.9 us -> 24.1 us  [swap(): return lax.all_to_all(x, axes, split_axis=0, concat_axis=0, tiled=False)]
    pallas_call x1, Pallas kernels: 3.37 us -> 1.84 us  [shards(): pl.pallas_call(cut_kernel, out_shape=[jax.ShapeDtypeStruct((size, columns...]
  transfers between devices with their start and end apart: 17 -> 12, of which waited for: 7 -> 5; matrix products, arithmetic and copies ran while one was open for 4% -> 3% of each run, Pallas kernels for 20% -> 20%
where the time goes in v7:
time: 139 us; the launch traced here: 138 us
  waiting for transfers between devices  38.3 us (28%)
  starting transfers between devices  35.7 us (26%)
  Pallas kernels  29.7 us (21%)
  blocking collectives  18.1 us (13%)
  local copies, waits for them, and re-layouts  14.2 us (10%)
    all_to_all x4, starting transfers between devices, swap(): return lax.all_to_all(x, axes, split_axis=0, concat_axis=0, tiled=False)  24.1 us
    ppermute x7, waiting for transfers between devices, along_y(): return lax.ppermute(x, 'y', [(i, (i + distance) % 4) for i in range(4)])  19.7 us
    all_to_all x4, waiting for transfers between devices, swap(): return lax.all_to_all(x, axes, split_axis=0, concat_axis=0, tiled=False)  18.6 us
    pallas_call x1, Pallas kernels, shards(): pl.pallas_call(attend_kernel, out_shape=jax.ShapeDtypeStruct((tokens, qua...  18.5 us
    all_to_all x1, blocking collectives, swap(): return lax.all_to_all(x, axes, split_axis=0, concat_axis=0, tiled=False)  18.1 us
    unnamed x20, local copies, waits for them, and re-layouts  8.27 us
    ppermute x7, starting transfers between devices, along_y(): return lax.ppermute(x, 'y', [(i, (i + distance) % 4) for i in range(4)])  7.2 us
    pallas_call x2, Pallas kernels, project(): pl.pallas_call(project_kernel, out_shape=jax.ShapeDtypeStruct((4, 2, toke...  4.9 us
  transfers between devices with their start and end apart: 12, of which 5 were waited for; matrix products, arithmetic and copies ran while one was open for 3% of the time, Pallas kernels for 20%

profile of v7, /device:TPU:1, one launch (start us, length us, event | category | flops | bytes accessed | tf_op | source)
XLA Modules:
  0.0 138.0 jit_solution(1498235297185583227)
XLA Ops:
  0.0 1.0 reshape.21
  1.0 0.7 copy.14
  1.7 5.0 %all-to-all-start = ((bf16[4,16,1024]{2,1,0:T(8,128)(2,1)}), bf16[4,16,1024]{2,1,0:T(8,128)(2,1)S(1)}, u32[]{:S(2)}, u32[]{:S(2)}) async-start(bf16[4,16,1024]{2,1,0:T(8,128)(2,1)} %copy.14), calls=%async_computation | async-start | bytes 262144 | tf_op jit(solution)/shard_map/move_queries/all_to_all | solution.py:229
  7.3 3.6 %pack.1 = (bf16[2,1056,128]{2,1,0:T(8,128)(2,1)}, bf16[2,1056,128]{2,1,0:T(8,128)(2,1)}, bf16[2,1056,128]{2,1,0:T(8,128)(2,1)}, bf16[2,1056,128]{2,1,0:T(8,128)(2,1)}) custom-call(s32[1]{0:T(128)} %bitcast.place, s32[8]{0:T(128)} %valid_len.1, s32[8]{0:T(128)} %span_ids.1, s32[1]{0:T(128)S(6)} %copy.16.offset, bf16[1024,256]{1,0:T(8,128)(2,1)} %keys_in.1, ...), custom_call_target="tpu_custom_call" | custom-call | flops 1 | bytes 1 | tf_op jit(solution)/shard_map/pack/pallas_call | solution.py:264
  10.9 0.6 all-to-all-done
  11.5 0.9 collective-permute-start
  12.5 2.4 %collective-permute-start.1 = (bf16[2,1056,128]{2,1,0:T(8,128)(2,1)}, bf16[2,1056,128]{2,1,0:T(8,128)(2,1)}, u32[]{:S(2)}, u32[]{:S(2)}) collective-permute-start(bf16[2,1056,128]{2,1,0:T(8,128)(2,1)} %get-tuple-element.39), channel_id=1, source_target_pairs={{0,8},{4,12},{8,0},{12,4},{1,9},{5,13},{9,1},{13,5},{2,10},{6,14},... | collective-permute-start | bytes 1622024 | tf_op jit(solution)/shard_map/move_kv/ppermute | solution.py:233
  14.9 1.2 collective-permute-start.2
  16.0 1.2 broadcast_in_dim.18
  17.2 7.5 %all-to-all-start.1 = ((bf16[8,64,1024]{2,1,0:T(8,128)(2,1)}), bf16[8,64,1024]{2,1,0:T(8,128)(2,1)}, u32[]{:S(2)}, u32[]{:S(2)}) async-start(bf16[8,64,1024]{2,1,0:T(8,128)(2,1)} %broadcast_in_dim.18), calls=%async_computation.1 | async-start | bytes 2097152 | tf_op jit(solution)/shard_map/move_queries/all_to_all | solution.py:229
  24.7 2.2 %copy-done.2 = bf16[4096,512]{1,0:T(8,128)(2,1)S(1)} copy-done((bf16[4096,512]{1,0:T(8,128)(2,1)S(1)}, bf16[4096,512]{1,0:T(8,128)(2,1)}, u32[]{:S(2)}) %copy-start.2) | copy-done | bytes 4194328
  26.9 1.8 %move_weight.1 = (bf16[1024,512]{1,0:T(8,128)(2,1)S(1)}, bf16[1024,512]{1,0:T(8,128)(2,1)}, bf16[1024,512]{1,0:T(8,128)(2,1)}, bf16[512,512]{1,0:T(8,128)(2,1)S(1)}, bf16[512,512]{1,0:T(8,128)(2,1)S(1)}) custom-call(s32[1]{0:T(128)} %bitcast.place, bf16[4096,512]{1,0:T(8,128)(2,1)S(1)} %copy-done.2), custom_call_target="tpu_custom_call" | custom-call | flops 1 | bytes 1 | tf_op jit(solution)/shard_map/move_weight/pallas_call | solution.py:292
  28.8 0.8 copy-done.8
  29.6 0.0 collective-permute-done.kv1
  29.6 8.2 %collective-permute-done.1.kv2 = bf16[2,1056,128]{2,1,0:T(8,128)(2,1)} collective-permute-done((bf16[2,1056,128]{2,1,0:T(8,128)(2,1)}, bf16[2,1056,128]{2,1,0:T(8,128)(2,1)}, u32[]{:S(2)}, u32[]{:S(2)}) %collective-permute-start.1) | collective-permute-done | bytes 540704 | tf_op jit(solution)/shard_map/move_kv/ppermute | solution.py:233
  37.8 0.0 collective-permute-start.3
  37.8 2.7 %collective-permute-start.4 = (bf16[1024,512]{1,0:T(8,128)(2,1)}, bf16[1024,512]{1,0:T(8,128)(2,1)S(1)}, u32[]{:S(2)}, u32[]{:S(2)}) collective-permute-start(bf16[1024,512]{1,0:T(8,128)(2,1)} %get-tuple-element.52), channel_id=1, source_target_pairs={{0,12},{4,0},{8,4},{12,8},{1,13},{5,1},{9,5},{13,9},{2,14},{6,2},{... | collective-permute-start | bytes 3145736 | tf_op jit(solution)/shard_map/move_weight/ppermute | solution.py:233
  40.5 0.7 slice_bitcast_fusion.3
  41.2 0.7 slice_bitcast_fusion.2
  41.8 0.7 slice_bitcast_fusion.1
  42.5 0.0 collective-permute-done.2.kv3
  42.5 0.7 slice_bitcast_fusion
  43.2 0.1 reshape.26.live
  43.3 0.1 copy.15.pos_q
  43.4 0.1 fusion
  43.5 0.1 concatenate.3
  43.6 1.0 copy-done.4
  44.7 1.0 copy-done.6
  45.7 18.5 %attend.1 = bf16[512,1152]{1,0:T(8,128)(2,1)} custom-call(s32[32]{0:T(128)S(1)} %reshape.26.live, bf16[512,1024]{1,0:T(8,128)(2,1)} %bitcast.8.queries, bf16[2,1056,128]{2,1,0:T(8,128)(2,1)S(1)} %copy-done.4, bf16[2,1056,128]{2,1,0:T(8,128)(2,1)S(1)} %copy-done.6, bf16[2,1056,128]{2,1,0:T(8,128)(2,1)} %collective-permute-done.1.kv2, ...), custom_call_target="tpu_custom_call" | custom-call | flops 1 | bytes 1 | tf_op jit(solution)/shard_map/attend/pallas_call | solution.py:320
  64.2 1.0 copy-done
  65.2 7.5 %all-to-all-start.2 = ((bf16[8,64,1152]{2,1,0:T(8,128)(2,1)}), bf16[8,64,1152]{2,1,0:T(8,128)(2,1)S(1)}, u32[]{:S(2)}, u32[]{:S(2)}) async-start(bf16[8,64,1152]{2,1,0:T(8,128)(2,1)} %bitcast.11), calls=%async_computation.2 | async-start | bytes 2359296 | tf_op jit(solution)/shard_map/move_partials/all_to_all | solution.py:229
  72.7 15.6 %all-to-all-done.2.parts = bf16[8,64,1152]{2,1,0:T(8,128)(2,1)S(1)} async-done(((bf16[8,64,1152]{2,1,0:T(8,128)(2,1)}), bf16[8,64,1152]{2,1,0:T(8,128)(2,1)S(1)}, u32[]{:S(2)}, u32[]{:S(2)}) %all-to-all-start.2) | async-done | bytes 1179680 | tf_op jit(solution)/shard_map/move_partials/all_to_all | solution.py:229
  88.3 0.9 settle.1
  89.2 1.0 copy-done.3
  90.2 0.0 collective-permute-done.5.w2a
  90.2 4.1 %all-to-all-start.3 = ((bf16[8,64,1024]{2,1,0:T(8,128)(2,1)}), bf16[8,64,1024]{2,1,0:T(8,128)(2,1)S(1)}, u32[]{:S(2)}, u32[]{:S(2)}) async-start(bf16[8,64,1024]{2,1,0:T(8,128)(2,1)} %copy-done.3), calls=%async_computation.3 | async-start | bytes 2097152 | tf_op jit(solution)/shard_map/move_attended/all_to_all | solution.py:229
  94.3 0.0 collective-permute-start.6
  94.3 0.1 pad_add_fusion.1.place
  94.3 11.5 %collective-permute-done.6.w2b = bf16[512,512]{1,0:T(8,128)(2,1)} collective-permute-done((bf16[512,512]{1,0:T(8,128)(2,1)}, bf16[512,512]{1,0:T(8,128)(2,1)}, u32[]{:S(2)}, u32[]{:S(2)}) %collective-permute-start.6) | collective-permute-done | bytes 524320 | tf_op jit(solution)/shard_map/move_weight/ppermute | solution.py:233
  105.8 2.3 %all-to-all-done.3 = bf16[8,64,1024]{2,1,0:T(8,128)(2,1)S(1)} async-done(((bf16[8,64,1024]{2,1,0:T(8,128)(2,1)}), bf16[8,64,1024]{2,1,0:T(8,128)(2,1)S(1)}, u32[]{:S(2)}, u32[]{:S(2)}) %all-to-all-start.3) | async-done | bytes 1048608 | tf_op jit(solution)/shard_map/move_attended/all_to_all | solution.py:229
  108.2 1.2 copy-done.1
  109.4 2.5 %project.3 = bf16[4,2,128,512]{3,2,1,0:T(8,128)(2,1)S(1)} custom-call(s32[2]{0:T(128)S(1)} %pad_add_fusion.1.place, bf16[512,1024]{1,0:T(8,128)(2,1)S(1)} %bitcast.19, bf16[1024,512]{1,0:T(8,128)(2,1)S(1)} %get-tuple-element.56.w0, bf16[1024,512]{1,0:T(8,128)(2,1)S(1)} %collective-permute-done.3.w1, bf16[512,512]{1,0:T(8,128)(2,1)} %collective-permute-done.5.w2a, ...), custom_call_target="tpu_custom_call" | custom-call | flops 1 | bytes 1 | tf_op jit(solution)/shard_map/project/pallas_call | solution.py:353
  111.8 4.4 %collective-permute-start.7 = (bf16[4,2,128,512]{3,2,1,0:T(8,128)(2,1)S(1)}, bf16[4,2,128,512]{3,2,1,0:T(8,128)(2,1)S(1)}, u32[]{:S(2)}, u32[]{:S(2)}) collective-permute-start(bf16[4,2,128,512]{3,2,1,0:T(8,128)(2,1)S(1)} %project.3), channel_id=1, source_target_pairs={{0,1},{1,0},{2,3},{3,2},{4,5},{5,4},{6,7},{7,6},{8,9},{9,8},{10,11... | collective-permute-start | bytes 3145736 | tf_op jit(solution)/shard_map/project/ppermute | solution.py:237
  116.2 0.1 pad_add_fusion.place
  116.3 2.5 %project.2 = bf16[4,2,128,512]{3,2,1,0:T(8,128)(2,1)S(1)} custom-call(s32[2]{0:T(128)S(1)} %pad_add_fusion.place, bf16[512,1024]{1,0:T(8,128)(2,1)S(1)} %bitcast.20, bf16[1024,512]{1,0:T(8,128)(2,1)S(1)} %get-tuple-element.56.w0, bf16[1024,512]{1,0:T(8,128)(2,1)S(1)} %collective-permute-done.3.w1, bf16[512,512]{1,0:T(8,128)(2,1)} %collective-permute-done.5.w2a, ...), custom_call_target="tpu_custom_call" | custom-call | flops 1 | bytes 1 | tf_op jit(solution)/shard_map/project/pallas_call | solution.py:353
  118.8 0.3 add_convert_fusion
  119.1 18.1 %all_to_all.25 = bf16[8,128,512]{2,1,0:T(8,128)(2,1)S(1)} all-to-all(bf16[8,128,512]{2,1,0:T(8,128)(2,1)S(1)} %bitcast.22), channel_id=1, replica_groups=mesh['z'=4,'x_hi'=2,'y'=4,'x_lo'=2,'core'=2] {'y','x_lo'}, dimensions={0} | all-to-all | bytes 2097152 | tf_op jit(solution)/shard_map/move_terms/all_to_all | solution.py:229
  137.2 0.8 reduce_sum.12
  (20 shorter events, 0.1 us)
Async XLA Ops:
  1.7 9.8 %all-to-all-start = ((bf16[4,16,1024]{2,1,0:T(8,128)(2,1)}), bf16[4,16,1024]{2,1,0:T(8,128)(2,1)S(1)}, u32[]{:S(2)}, u32[]{:S(2)}) async-start(bf16[4,16,1024]{2,1,0:T(8,128)(2,1)} %copy.14), calls=%async_computation | async-start | bytes 262144 | tf_op jit(solution)/shard_map/move_queries/all_to_all | solution.py:229
  11.5 18.1 %collective-permute-start = (bf16[2,1056,128]{2,1,0:T(8,128)(2,1)}, bf16[2,1056,128]{2,1,0:T(8,128)(2,1)S(1)}, u32[]{:S(2)}, u32[]{:S(2)}) collective-permute-start(bf16[2,1056,128]{2,1,0:T(8,128)(2,1)} %get-tuple-element.38), channel_id=1, source_target_pairs={{0,4},{4,8},{8,12},{12,0},{1,5},{5,9},{9,13},{13,1},{2,6},{6,10},{... | collective-permute-start | bytes 1622024 | tf_op jit(solution)/shard_map/move_kv/ppermute | solution.py:233
  12.5 25.4 %collective-permute-start.1 = (bf16[2,1056,128]{2,1,0:T(8,128)(2,1)}, bf16[2,1056,128]{2,1,0:T(8,128)(2,1)}, u32[]{:S(2)}, u32[]{:S(2)}) collective-permute-start(bf16[2,1056,128]{2,1,0:T(8,128)(2,1)} %get-tuple-element.39), channel_id=1, source_target_pairs={{0,8},{4,12},{8,0},{12,4},{1,9},{5,13},{9,1},{13,5},{2,10},{6,14},... | collective-permute-start | bytes 1622024 | tf_op jit(solution)/shard_map/move_kv/ppermute | solution.py:233
  14.9 27.6 %collective-permute-start.2 = (bf16[2,1056,128]{2,1,0:T(8,128)(2,1)}, bf16[2,1056,128]{2,1,0:T(8,128)(2,1)}, u32[]{:S(2)}, u32[]{:S(2)}) collective-permute-start(bf16[2,1056,128]{2,1,0:T(8,128)(2,1)} %get-tuple-element.40), channel_id=1, source_target_pairs={{0,12},{4,0},{8,4},{12,8},{1,13},{5,1},{9,5},{13,9},{2,14},{6,2},{... | collective-permute-start | bytes 1622024 | tf_op jit(solution)/shard_map/move_kv/ppermute | solution.py:233
  17.2 26.0 %all-to-all-start.1 = ((bf16[8,64,1024]{2,1,0:T(8,128)(2,1)}), bf16[8,64,1024]{2,1,0:T(8,128)(2,1)}, u32[]{:S(2)}, u32[]{:S(2)}) async-start(bf16[8,64,1024]{2,1,0:T(8,128)(2,1)} %broadcast_in_dim.18), calls=%async_computation.1 | async-start | bytes 2097152 | tf_op jit(solution)/shard_map/move_queries/all_to_all | solution.py:229
  24.7 2.2 %copy-start.2 = (bf16[4096,512]{1,0:T(8,128)(2,1)S(1)}, bf16[4096,512]{1,0:T(8,128)(2,1)}, u32[]{:S(2)}) copy-start(bf16[4096,512]{1,0:T(8,128)(2,1)} %weight) | copy-start | bytes 12582916
  26.9 16.3 %copy-start.9 = (s32[512]{0:T(512)S(1)}, s32[512]{0:T(512)}, u32[]{:S(2)}) copy-start(s32[512]{0:T(512)} %param.17) | copy-start | bytes 6148
  28.8 0.8 copy-start.8
  29.6 13.6 %copy-start.7 = (bf16[512,512]{1,0:T(8,128)(2,1)}, bf16[512,512]{1,0:T(8,128)(2,1)S(1)}, u32[]{:S(2)}) copy-start(bf16[512,512]{1,0:T(8,128)(2,1)S(1)} %get-tuple-element.59) | copy-start | bytes 1572868
  29.6 8.2 %copy-start.5 = (bf16[2,1056,128]{2,1,0:T(8,128)(2,1)}, bf16[2,1056,128]{2,1,0:T(8,128)(2,1)S(1)}, u32[]{:S(2)}) copy-start(bf16[2,1056,128]{2,1,0:T(8,128)(2,1)S(1)} %collective-permute-done.kv1) | copy-start | bytes 1622020
  37.8 26.3 %collective-permute-start.3 = (bf16[1024,512]{1,0:T(8,128)(2,1)}, bf16[1024,512]{1,0:T(8,128)(2,1)S(1)}, u32[]{:S(2)}, u32[]{:S(2)}) collective-permute-start(bf16[1024,512]{1,0:T(8,128)(2,1)} %get-tuple-element.51), channel_id=1, source_target_pairs={{0,4},{4,8},{8,12},{12,0},{1,5},{5,9},{9,13},{13,1},{2,6},{6,10},{... | collective-permute-start | bytes 3145736 | tf_op jit(solution)/shard_map/move_weight/ppermute | solution.py:233
  37.8 26.3 %collective-permute-start.4 = (bf16[1024,512]{1,0:T(8,128)(2,1)}, bf16[1024,512]{1,0:T(8,128)(2,1)S(1)}, u32[]{:S(2)}, u32[]{:S(2)}) collective-permute-start(bf16[1024,512]{1,0:T(8,128)(2,1)} %get-tuple-element.52), channel_id=1, source_target_pairs={{0,12},{4,0},{8,4},{12,8},{1,13},{5,1},{9,5},{13,9},{2,14},{6,2},{... | collective-permute-start | bytes 3145736 | tf_op jit(solution)/shard_map/move_weight/ppermute | solution.py:233
  43.6 1.0 copy-start.4
  44.7 1.0 copy-start.6
  64.2 1.0 copy-start
  65.2 23.1 %all-to-all-start.2 = ((bf16[8,64,1152]{2,1,0:T(8,128)(2,1)}), bf16[8,64,1152]{2,1,0:T(8,128)(2,1)S(1)}, u32[]{:S(2)}, u32[]{:S(2)}) async-start(bf16[8,64,1152]{2,1,0:T(8,128)(2,1)} %bitcast.11), calls=%async_computation.2 | async-start | bytes 2359296 | tf_op jit(solution)/shard_map/move_partials/all_to_all | solution.py:229
  72.6 17.5 %collective-permute-start.5 = (bf16[512,512]{1,0:T(8,128)(2,1)}, bf16[512,512]{1,0:T(8,128)(2,1)}, u32[]{:S(2)}, u32[]{:S(2)}) collective-permute-start(bf16[512,512]{1,0:T(8,128)(2,1)} %copy-done.8), channel_id=1, source_target_pairs={{0,8},{4,12},{8,0},{12,4},{1,9},{5,13},{9,1},{13,5},{2,10},{6,14},... | collective-permute-start | bytes 1572872 | tf_op jit(solution)/shard_map/move_weight/ppermute | solution.py:233
  89.2 1.0 copy-start.3
  90.2 18.0 %all-to-all-start.3 = ((bf16[8,64,1024]{2,1,0:T(8,128)(2,1)}), bf16[8,64,1024]{2,1,0:T(8,128)(2,1)S(1)}, u32[]{:S(2)}, u32[]{:S(2)}) async-start(bf16[8,64,1024]{2,1,0:T(8,128)(2,1)} %copy-done.3), calls=%async_computation.3 | async-start | bytes 2097152 | tf_op jit(solution)/shard_map/move_attended/all_to_all | solution.py:229
  94.3 11.6 %collective-permute-start.6 = (bf16[512,512]{1,0:T(8,128)(2,1)}, bf16[512,512]{1,0:T(8,128)(2,1)}, u32[]{:S(2)}, u32[]{:S(2)}) collective-permute-start(bf16[512,512]{1,0:T(8,128)(2,1)} %copy-done.7), channel_id=1, source_target_pairs={{0,8},{4,12},{8,0},{12,4},{1,9},{5,13},{9,1},{13,5},{2,10},{6,14},... | collective-permute-start | bytes 1572872 | tf_op jit(solution)/shard_map/move_weight/ppermute | solution.py:233
  108.2 1.2 copy-start.1
  111.8 6.9 %collective-permute-start.7 = (bf16[4,2,128,512]{3,2,1,0:T(8,128)(2,1)S(1)}, bf16[4,2,128,512]{3,2,1,0:T(8,128)(2,1)S(1)}, u32[]{:S(2)}, u32[]{:S(2)}) collective-permute-start(bf16[4,2,128,512]{3,2,1,0:T(8,128)(2,1)S(1)} %project.3), channel_id=1, source_target_pairs={{0,1},{1,0},{2,3},{3,2},{4,5},{5,4},{6,7},{7,6},{8,9},{9,8},{10,11... | collective-permute-start | bytes 3145736 | tf_op jit(solution)/shard_map/project/ppermute | solution.py:237
